TPU v7x, 32 devices: a whole 2x2x4 slice. The times are simulated.
32 devices in a mesh: segment: 4 (over y, x), node: 8 (over z, core).
Axes of the slice: x: 2, y: 2, z: 4, core: 2. Of those that a mesh axis runs over, the one named last changes fastest.
Arguments:
- activations: bfloat16 [4, 2048, 512], P('segment', 'node'), may hold values from -8 to 8
- norm_gain: float32 [4, 512], P('segment'), may hold values from 0.5 to 1.5
- project_in: bfloat16 [4, 512, 1536], P('segment'), may hold values from -0.25 to 0.25
- project_out: bfloat16 [4, 512, 512], P('segment'), may hold values from -0.5 to 0.5
- virtual_keys: bfloat16 [4, 4, 512], P('segment'), may hold values from -6 to 6
- virtual_id: int32 [2048, 1], P('node'), may hold values from 0 to 3
- local_rows: int32 [16, 2048], P(None, 'node'), may hold values from 0 to 127
- slot_block: int32 [16, 8], P('node'), may hold values from 0 to 15, as said below
- slot_count: int32 [16], P('node'), may hold values from 1 to 8, as said below
- slot_rows: int32 [16, 8, 4, 128], P('node'), may hold values from 0 to 127
Outputs:
- handed: bfloat16 [4, 2048, 512], P('segment', 'node')
Inputs may be any that keep to these rules, and one draw needn't show every extreme that they name: `virtual_id`: every virtual node has a member. `slot_block`: blocks d * 2 to (d + 1) * 2 - 1 lie on device d of node; every entry names a block of another device than the destination block's, and all entries of one device's rows that name blocks of the same device name the same block. `slot_count`: some block has 8 live slots.
All inputs are finite; a program needn't handle non-finite values.
Results may differ from a plain program's by a relative error of at most 0.0065.
Values may be sent and summed in bfloat16 or wider, within the bound.
No kernel may reach another device: no remote copies, remote signals or barrier semaphores. Data moves between devices by JAX's collectives and lax.ppermute only.
A program may use at most 64 MiB of HBM per device.

v0:
```python
import functools

import jax
import jax.numpy as jnp
from jax import lax
from jax.experimental import pallas as pl
from jax.experimental.pallas import tpu as pltpu
from jax.sharding import PartitionSpec as P

HEADS = 8
CORES = 2
EPSILON = 1e-05
CAP_LIMIT = 10.0
LOG2E = 1.4426950408889634
EXTRA = 16
F32 = jnp.float32
BF16 = jnp.bfloat16
HBM = pl.BlockSpec(memory_space=pltpu.HBM)
VMEM = pl.BlockSpec(memory_space=pltpu.VMEM)


def ring_order(chips):
    return list(range(0, 1)) + list(range(1, chips, 2)) + list(range((chips - 1) // 2 * 2, 0, -2))


def ring_place(chip, chips):
    return jnp.where(chip % 2 == 1, (chip + 1) // 2, (chips - chip // 2) % chips)


def to_next_chip(value, devices, way):
    chips = devices // CORES
    order = ring_order(chips)
    pairs = [
        (order[i] * CORES + c, order[(i + way) % chips] * CORES + c)
        for i in range(chips)
        for c in range(CORES)
    ]
    return lax.ppermute(value, "node", pairs)


def swapped(value, devices, distance):
    return lax.ppermute(value, "node", [(d, d ^ distance) for d in range(devices)])


def to_next_segment(value):
    count = lax.axis_size("segment")
    return lax.ppermute(value, "segment", [(s, (s + 1) % count) for s in range(count)])


def norm_rows(rows_in, gain_row):
    widened = rows_in.astype(F32)
    center = widened - jnp.mean(widened, axis=-1, keepdims=True)
    spread = jnp.mean(center * center, axis=-1, keepdims=True)
    return (center * lax.rsqrt(spread + EPSILON) * gain_row).astype(BF16)


def exp_capped(raw, scale):
    return jnp.exp2((CAP_LIMIT * LOG2E) * jnp.tanh(raw * (scale / CAP_LIMIT)))


def counts_of(index_rows, block_rows):
    rows = lax.broadcasted_iota(jnp.int32, (block_rows, index_rows.shape[1]), 0)
    total = jnp.zeros(rows.shape, F32)
    for j in range(index_rows.shape[0]):
        total = total + jnp.where(index_rows[j : j + 1, :] == rows, 1.0, 0.0)
    return total


def mm(a, b):
    return jnp.dot(a, b, preferred_element_type=F32)


def mm_nt(a, b):
    return lax.dot_general(a, b, (((1,), (1,)), ((), ())), preferred_element_type=F32)


def choose(mask_row, rows_ref, br):
    _, width = rows_ref.shape
    lanes = mask_row.shape[1]
    mask = jnp.broadcast_to(mask_row, (br, lanes))
    mask = jnp.concatenate([mask] * (width // lanes), axis=1)
    picked = rows_ref[:br, :].astype(F32)
    for block in range(1, rows_ref.shape[0] // br):
        other = rows_ref[block * br : (block + 1) * br, :].astype(F32)
        picked = jnp.where(mask == float(block), other, picked)
    return picked.astype(BF16)


def start_copies(pairs, sems):
    copies = [pltpu.make_async_copy(src, dst, sems.at[i]) for i, (src, dst) in enumerate(pairs)]
    for copy in copies:
        copy.start()
    return copies


def own_kernel(
    x_hbm, gain_hbm, win_hbm, vk_hbm, vid_hbm,
    normed_ref, k_ref, v_ref, gain_ref, pool_ref,
    x_ref, wk_ref, wv_ref, vk_ref, vid_ref, sems,
):
    rows, width = x_ref.shape
    virtual = vk_ref.shape[0]
    scale = (width // HEADS) ** (-0.5)
    copies = start_copies(
        [
            (x_hbm, x_ref), (gain_hbm, gain_ref),
            (win_hbm.at[:, width : 2 * width], wk_ref), (win_hbm.at[:, 2 * width :], wv_ref),
            (vk_hbm, vk_ref), (vid_hbm, vid_ref),
        ],
        sems,
    )
    copies[0].wait()
    copies[1].wait()
    normed = norm_rows(x_ref[...], gain_ref[...])
    normed_ref[...] = normed
    for copy in copies[2:]:
        copy.wait()
    k = mm(normed, wk_ref[...]).astype(BF16)
    v = mm(normed, wv_ref[...]).astype(BF16)
    k_ref[...] = k
    v_ref[...] = v

    head_of_lane = lax.broadcasted_iota(jnp.int32, (HEADS, width), 1) // (width // HEADS)
    own_head = head_of_lane == lax.broadcasted_iota(jnp.int32, (HEADS, width), 0)
    vkf = vk_ref[...].astype(F32)
    vkbd = jnp.concatenate(
        [
            jnp.where(own_head, jnp.broadcast_to(vkf[j : j + 1, :], (HEADS, width)), 0.0)
            for j in range(virtual)
        ],
        axis=0,
    ).astype(BF16)
    raw = mm_nt(vkbd, k)
    owner = lax.broadcasted_iota(jnp.int32, raw.shape, 0) // HEADS
    pool_w = jnp.where(vid_ref[...] == owner, exp_capped(raw, scale), 0.0).astype(BF16)
    pool_num = mm(pool_w, v)
    pool_den = mm(pool_w, jnp.ones((rows, width), BF16))
    parts = [
        jnp.sum(jnp.where(own_head, whole[j * HEADS : (j + 1) * HEADS], 0.0), axis=0, keepdims=True)
        for whole in (pool_num, pool_den)
        for j in range(virtual)
    ]
    pool_ref[...] = jnp.concatenate(parts, axis=0)


def attend(keys, values, counts, qbd, scale):
    p = (counts * exp_capped(mm(keys, qbd), scale)).astype(BF16)
    return mm(values, p)


def fold(o, num_ref, den_ref, b, t, add):
    wide = o.shape[0] - EXTRA
    head = wide // 2
    br = o.shape[1] // 2
    r0 = t * wide
    places = (
        (num_ref, slice(r0, r0 + head), o[:head, :br]),
        (num_ref, slice(r0 + head, r0 + wide), o[head:wide, br:]),
        (den_ref, slice(2 * t, 2 * t + 1), o[wide : wide + 1, :br]),
        (den_ref, slice(2 * t + 1, 2 * t + 2), o[wide : wide + 1, br:]),
    )
    for ref, part, value in places:
        if add:
            ref[b, part, :] += value
        else:
            ref[b, part, :] = value


def prep_kernel(
    normed_ref, k_ref, v_ref, win_hbm, lrows_hbm, srows_hbm, sblock_hbm, scount_hbm, vid_hbm, wo_hbm,
    qbd_ref, num_ref, den_ref, counts_ref, mask_ref, vcol_ref, wk_ref, wvt_ref, wo_ref,
    wq_ref, wv_ref, lrows_ref, srows_ref, vid_ref, sblock_ref, scount_ref, want_ref, sems,
):
    rows, width = normed_ref.shape
    blocks, pairs, wide, _ = qbd_ref.shape
    chips = mask_ref.shape[1]
    slots = sblock_ref.shape[1]
    br = rows // blocks
    head = width // HEADS
    scale = head ** (-0.5)
    copies = start_copies(
        [
            (sblock_hbm, sblock_ref), (scount_hbm, scount_ref),
            (win_hbm.at[:, :width], wq_ref), (lrows_hbm, lrows_ref), (srows_hbm, srows_ref),
            (vid_hbm, vid_ref), (win_hbm.at[:, width : 2 * width], wk_ref),
            (win_hbm.at[:, 2 * width :], wv_ref), (wo_hbm, wo_ref),
        ],
        sems,
    )
    counts_ref[...] = jnp.zeros(counts_ref.shape, F32)
    for copy in copies:
        copy.wait()
    me = lax.axis_index("node")
    place = ring_place(me // CORES, chips)
    core = me % CORES
    for d in range(chips * CORES):
        want_ref[d] = 0
    for b in range(blocks):
        for e in range(slots):
            entry = sblock_ref[b, e]
            want_ref[entry // blocks] = entry % blocks
    for d in range(chips * CORES):
        step = (place - ring_place(jnp.int32(d // CORES), chips) + chips) % chips
        far = jnp.where(core == d % CORES, 0, 1)
        mask_ref[far, step] = jnp.full(mask_ref.shape[2:], want_ref[d].astype(F32), F32)
    for b in range(blocks):
        for e in range(slots):
            device = sblock_ref[b, e] // blocks
            step = (place - ring_place(device // CORES, chips) + chips) % chips
            far = jnp.where(device % CORES == core, 0, 1)
            live = jnp.where(e < scount_ref[b], 1.0, 0.0).astype(F32)
            counts_ref[far, step, b] += counts_of(srows_ref[b, e], br) * live

    vcol_ref[...] = jnp.broadcast_to(vid_ref[...].astype(F32), (128, rows)).T
    wvt_ref[...] = wv_ref[...].T
    qt = mm(normed_ref[...], wq_ref[...]).astype(BF16).T
    vt = v_ref[...].T
    zero = jnp.zeros((head, br), BF16)
    ones = jnp.ones((EXTRA, br), BF16)
    for b in range(blocks):
        cols = slice(b * br, (b + 1) * br)
        counts = counts_of(lrows_ref[:, cols], br)
        counts2 = jnp.concatenate([counts, counts], axis=1)
        for t in range(pairs):
            r0 = t * wide
            mid = r0 + head
            end = r0 + wide
            bd = jnp.concatenate(
                [
                    jnp.concatenate([qt[r0:mid, cols], zero], axis=1),
                    jnp.concatenate([zero, qt[mid:end, cols]], axis=1),
                ],
                axis=0,
            )
            qbd_ref[b, t] = bd
            values = jnp.concatenate([vt[r0:end, cols], ones], axis=0)
            fold(attend(k_ref[cols, r0:end], values, counts2, bd, scale), num_ref, den_ref, b, t, False)


def project(xs, gain_ref, wk_ref, wvt_ref, k_ref, vt_ref):
    normed = norm_rows(jnp.concatenate(xs, axis=0), gain_ref[...])
    k_ref[...] = mm(normed, wk_ref[...]).astype(BF16)
    vt_ref[...] = mm_nt(wvt_ref[...], normed).astype(BF16)


def add_sources(names, b, counts_ref, qbd_ref, k_ref, vt_ref, num_ref, den_ref):
    _, pairs, wide, _ = qbd_ref.shape
    scale = (2 / wide) ** 0.5
    counts = jnp.concatenate([counts_ref[far, step, b] for far, step in names], axis=0)
    counts2 = jnp.concatenate([counts, counts], axis=1)
    ones = jnp.ones((EXTRA, counts.shape[0]), BF16)
    for t in range(pairs):
        cols = slice(t * wide, (t + 1) * wide)
        values = jnp.concatenate([vt_ref[cols, :], ones], axis=0)
        o = attend(k_ref[:, cols], values, counts2, qbd_ref[b, t], scale)
        fold(o, num_ref, den_ref, b, t, True)


def slots_kernel(
    names, mask_ref, gain_ref, wk_ref, wvt_ref, counts_ref, qbd_ref, num_in, den_in, *refs
):
    num_ref, den_ref, k_ref, vt_ref = refs[len(names) :]
    blocks, _, br = num_ref.shape
    num_ref[...] = num_in[...]
    den_ref[...] = den_in[...]
    xs = [choose(mask_ref[far, step, :1, :], ref, br) for (far, step), ref in zip(names, refs)]
    project(xs, gain_ref, wk_ref, wvt_ref, k_ref, vt_ref)
    for b in range(blocks):
        add_sources(names, b, counts_ref, qbd_ref, k_ref, vt_ref, num_ref, den_ref)


def finish_kernel(names, b, lead, *refs):
    if lead:
        (
            mask_ref, rows_ref, gain_ref, wk_ref, wvt_ref, counts_ref, qbd_ref, num_in, den_in,
            total_ref, vcol_ref, x_ref, wo_ref, out_ref, k_ref, vt_ref, num_ref, den_ref,
        ) = refs
    else:
        (
            k_ref, vt_ref, counts_ref, qbd_ref, num_in, den_in,
            total_ref, vcol_ref, x_ref, wo_ref, out_ref, num_ref, den_ref,
        ) = refs
    _, width, br = num_ref.shape
    head = width // HEADS
    num_ref[b] = num_in[b]
    den_ref[b] = den_in[b]
    if lead:
        xs = [choose(mask_ref[far, step, :1, :], rows_ref, br) for far, step in names]
        project(xs, gain_ref, wk_ref, wvt_ref, k_ref, vt_ref)
    add_sources(names, b, counts_ref, qbd_ref, k_ref, vt_ref, num_ref, den_ref)
    total = total_ref[...]
    virtual = total.shape[0] // 2
    pooled = total[:virtual] / total[virtual:]
    lanes = vcol_ref.shape[1]
    part = slice(b * br, (b + 1) * br)
    vid = vcol_ref[part, :]
    att = jnp.concatenate(
        [
            num_ref[b, h * head : (h + 1) * head, :] / den_ref[b, h : h + 1, :]
            for h in range(HEADS)
        ],
        axis=0,
    ).T
    pieces = []
    for c in range(0, width, lanes):
        own = jnp.broadcast_to(pooled[0:1, c : c + lanes], (br, lanes))
        for j in range(1, virtual):
            own = jnp.where(vid == float(j), pooled[j : j + 1, c : c + lanes], own)
        pieces.append((att[:, c : c + lanes] + own).astype(BF16))
    mixed = jnp.concatenate(pieces, axis=1)
    out_ref[...] = (x_ref[part, :].astype(F32) + mm(mixed, wo_ref[...])).astype(BF16)


def place_kernel(b, rows_ref, *refs):
    out_ref, sems = refs[-2:]
    br = rows_ref.shape[0]
    copy = pltpu.make_async_copy(rows_ref, out_ref.at[0, b * br : (b + 1) * br, :], sems.at[0])
    copy.start()
    copy.wait()


def params(mib):
    return pltpu.CompilerParams(vmem_limit_bytes=mib * 2**20)


def cost(flops):
    return pl.CostEstimate(flops=flops, bytes_accessed=1024, transcendentals=0)


def body(
    activations,
    norm_gain,
    project_in,
    project_out,
    virtual_keys,
    virtual_id,
    local_rows,
    slot_block,
    slot_count,
    slot_rows,
):
    _, rows, width = activations.shape
    br = slot_rows.shape[3]
    slots = slot_block.shape[1]
    blocks = rows // br
    devices = lax.axis_size("node")
    chips = devices // CORES
    virtual = virtual_keys.shape[1]
    pairs = HEADS // 2
    wide = width // pairs
    shape = jax.ShapeDtypeStruct
    after = lax.optimization_barrier
    x = activations[0]
    vid = virtual_id.reshape(1, rows)
    unit = 2**16

    near = {1: to_next_chip(x, devices, 1)}
    if chips > 2:
        near[chips - 1] = to_next_chip(x, devices, -1)
    far = {0: swapped(x, devices, 1)}
    normed, k, v, gain, pool = pl.pallas_call(
        own_kernel,
        out_shape=(
            shape((rows, width), BF16),
            shape((rows, width), BF16),
            shape((rows, width), BF16),
            shape((1, width), F32),
            shape((2 * virtual, width), F32),
        ),
        in_specs=[HBM] * 5,
        out_specs=[VMEM] * 5,
        scratch_shapes=[
            pltpu.VMEM((rows, width), BF16),
            pltpu.VMEM((width, width), BF16),
            pltpu.VMEM((width, width), BF16),
            pltpu.VMEM((virtual, width), BF16),
            pltpu.VMEM((1, rows), jnp.int32),
            pltpu.SemaphoreType.DMA((6,)),
        ],
        compiler_params=params(24),
        cost_estimate=cost(unit),
        name="own_rows",
    )(x, norm_gain, project_in[0], virtual_keys[0], vid)
    pool_in = swapped(pool, devices, 1)

    accumulators = (shape((blocks, width, br), F32), shape((blocks, HEADS, br), F32))
    qbd, num, den, counts, mask, vcol, wk, wvt, wo = pl.pallas_call(
        prep_kernel,
        out_shape=(
            (shape((blocks, pairs, wide, 2 * br), BF16),)
            + accumulators
            + (
                shape((CORES, chips, blocks, br, br), F32),
                shape((CORES, chips, 8, 128), F32),
                shape((rows, 128), F32),
                shape((width, width), BF16),
                shape((width, width), BF16),
                shape((width, width), BF16),
            )
        ),
        in_specs=[VMEM] * 3 + [HBM] * 7,
        out_specs=[VMEM] * 9,
        scratch_shapes=[
            pltpu.VMEM((width, width), BF16),
            pltpu.VMEM((width, width), BF16),
            pltpu.VMEM(local_rows.shape, jnp.int32),
            pltpu.VMEM(slot_rows.shape, jnp.int32),
            pltpu.VMEM((1, rows), jnp.int32),
            pltpu.SMEM((blocks, slots), jnp.int32),
            pltpu.SMEM((blocks,), jnp.int32),
            pltpu.SMEM((devices,), jnp.int32),
            pltpu.SemaphoreType.DMA((9,)),
        ],
        compiler_params=params(32),
        cost_estimate=cost(unit),
        name="prepare",
    )(
        normed, k, v, project_in[0], local_rows, slot_rows, slot_block, slot_count,
        vid, project_out[0],
    )

    def slots_call(names, num, den, name):
        return pl.pallas_call(
            functools.partial(slots_kernel, tuple(names)),
            out_shape=accumulators,
            in_specs=[VMEM] * (8 + len(names)),
            out_specs=[VMEM] * 2,
            scratch_shapes=[
                pltpu.VMEM((len(names) * br, width), BF16),
                pltpu.VMEM((width, len(names) * br), BF16),
            ],
            compiler_params=params(40),
            cost_estimate=cost(unit),
            name=name,
        )(
            mask, gain, wk, wvt, counts, qbd, num, den,
            *[(far if other else near)[step] for other, step in names],
        )

    ahead = chips // 2
    order = []
    for s in range(1, ahead + 1):
        order.append((s, 1))
        if s < chips - s:
            order.append((chips - s, -1))
    distance = 1
    for i, (step, way) in enumerate(order):
        last = i == len(order) - 1
        if distance < devices:
            pool_in, den = after((pool_in, den))
            pool = pool + pool_in
            distance *= 2
            if distance < devices:
                pool_in = swapped(pool, devices, distance)
        if i == 0 or last:
            near[step], den = after((near[step], den))
        nexts = step + way
        if nexts not in near and (nexts, way) in order:
            near[nexts] = to_next_chip(near[step], devices, way)
        far[step] = swapped(near[step], devices, 1)
        names = [(0, step)] if last else [(0, step), (1, step)]
        if i == 0:
            names = [(1, 0)] + names
        if i + 2 < len(order):
            ready = order[i + 1][0]
            near[ready], den = after((near[ready], den))
        num, den = slots_call(names, num, den, "slots_%d" % i)
    while distance < devices:
        pool = pool + pool_in
        distance *= 2
        if distance < devices:
            pool_in = swapped(pool, devices, distance)

    names = ((1, order[-1][0]),)
    out_shape = shape((br, width), BF16)
    shared = (counts, qbd, num, den, pool, vcol, x, wo)
    sums = [pltpu.VMEM((blocks, width, br), F32), pltpu.VMEM((blocks, HEADS, br), F32)]
    results = []
    for b in range(blocks):
        lead = b == 0
        kernel = functools.partial(finish_kernel, names, b, lead)
        if lead:
            result, far_k, far_vt = pl.pallas_call(
                kernel,
                out_shape=(out_shape, shape((br, width), BF16), shape((width, br), BF16)),
                in_specs=[VMEM] * 13,
                out_specs=[VMEM] * 3,
                scratch_shapes=sums,
                compiler_params=params(40),
                cost_estimate=cost(unit),
                name="finish_first",
            )(mask, far[names[0][1]], gain, wk, wvt, *shared)
        else:
            result = pl.pallas_call(
                kernel,
                out_shape=out_shape,
                in_specs=[VMEM] * 10,
                out_specs=VMEM,
                scratch_shapes=sums,
                compiler_params=params(40),
                cost_estimate=cost(unit),
                name="finish_rest",
            )(far_k, far_vt, *shared)
        results.append(result)
    results = [to_next_segment(result) for result in results]
    joined = None
    for b in range(blocks):
        earlier = [] if joined is None else [joined]
        joined = pl.pallas_call(
            functools.partial(place_kernel, b),
            out_shape=shape((1, rows, width), BF16),
            in_specs=[VMEM] + [HBM] * len(earlier),
            out_specs=HBM,
            scratch_shapes=[pltpu.SemaphoreType.DMA((1,))],
            input_output_aliases={1: 0} if earlier else {},
            compiler_params=params(24),
            cost_estimate=cost(unit),
            name="place_%d" % b,
        )(results[b], *earlier)
    return joined


def solution(mesh):
    placed = (
        P("segment", "node", None),
        P("segment", None),
        P("segment", None, None),
        P("segment", None, None),
        P("segment", None, None),
        P("node", None),
        P(None, "node"),
        P("node", None),
        P("node"),
        P("node", None, None, None),
    )
    return jax.shard_map(
        body, mesh=mesh, in_specs=placed, out_specs=P("segment", "node", None), check_vma=False
    )
```

profile of v0, /device:TPU:0, one launch (start us, length us, event | category | flops | bytes accessed | tf_op | source)
XLA Modules:
  0.0 45.5 jit_solution(15686205605407202611)
XLA Ops:
  0.0 3.0 %collective-permute-start = (bf16[256,512]{1,0:T(8,128)(2,1)}, bf16[256,512]{1,0:T(8,128)(2,1)S(1)}, u32[]{:S(2)}, u32[]{:S(2)}) collective-permute-start(bf16[256,512]{1,0:T(8,128)(2,1)} %bitcast.x_hbm.refs_11_.refs_8_), channel_id=1, source_target_pairs={{0,2},{1,3},{2,6},{3,7},{6,4},{7,5},{4,0},{5,1},{8,10},{9,11},{10,... | collective-permute-start | bytes 786440 | tf_op jit(solution)/shard_map/ppermute | solution.py:38
  3.0 1.1 %collective-permute-start.4 = (bf16[256,512]{1,0:T(8,128)(2,1)}, bf16[256,512]{1,0:T(8,128)(2,1)S(1)}, u32[]{:S(2)}, u32[]{:S(2)}) collective-permute-start(bf16[256,512]{1,0:T(8,128)(2,1)} %bitcast.x_hbm.refs_11_.refs_8_), channel_id=1, source_target_pairs={{0,4},{1,5},{2,0},{3,1},{6,2},{7,3},{4,6},{5,7},{8,12},{9,13},{10,... | collective-permute-start | bytes 786440 | tf_op jit(solution)/shard_map/ppermute | solution.py:38
  4.1 1.4 %copy-done = bf16[1,512,1536]{2,1,0:T(8,128)(2,1)S(1)} copy-done((bf16[1,512,1536]{2,1,0:T(8,128)(2,1)S(1)}, bf16[1,512,1536]{2,1,0:T(8,128)(2,1)}, u32[]{:S(2)}) %copy-start) | copy-done | bytes 1572888
  5.5 0.7 %copy-done.5 = bf16[1,4,512]{2,1,0:T(4,128)(2,1)S(1)} copy-done((bf16[1,4,512]{2,1,0:T(4,128)(2,1)S(1)}, bf16[1,4,512]{2,1,0:T(4,128)(2,1)}, u32[]{:S(2)}) %copy-start.5) | copy-done | bytes 4120
  6.2 0.7 %copy-done.6 = s32[256,1]{0,1:T(1,128)S(1)} copy-done((s32[256,1]{0,1:T(1,128)S(1)}, s32[256,1]{0,1:T(1,128)}, u32[]{:S(2)}) %copy-start.6) | copy-done | bytes 1048
  6.9 0.7 %copy-done.7 = f32[1,512]{1,0:T(1,128)S(1)} copy-done((f32[1,512]{1,0:T(1,128)S(1)}, f32[1,512]{1,0:T(1,128)}, u32[]{:S(2)}) %copy-start.7) | copy-done | bytes 2072
  7.6 2.1 %own_rows.1 = (bf16[256,512]{1,0:T(8,128)(2,1)S(1)}, bf16[256,512]{1,0:T(8,128)(2,1)S(1)}, bf16[256,512]{1,0:T(8,128)(2,1)S(1)}, f32[1,512]{1,0:T(1,128)S(1)}, f32[8,512]{1,0:T(8,128)S(1)}) custom-call(bf16[256,512]{1,0:T(8,128)(2,1)} %bitcast.x_hbm.refs_11_.refs_8_, f32[1,512]{1,0:T(1,128)S(1)} %copy-done.7, bf16[512,1536]{1,0:T(8,128)(2,1)S(1)} %bitcast.5, ...), custom_call_target="tpu_custom_call" | custom-call | flops 65536 | bytes 1024 | tf_op jit(solution)/shard_map/own_rows/pallas_call | solution.py:361
  10.3 1.0 %copy-done.2 = bf16[1,512,512]{2,1,0:T(8,128)(2,1)S(1)} copy-done((bf16[1,512,512]{2,1,0:T(8,128)(2,1)S(1)}, bf16[1,512,512]{2,1,0:T(8,128)(2,1)}, u32[]{:S(2)}) %copy-start.2) | copy-done | bytes 524312
  11.3 2.1 %prepare.1 = (bf16[2,4,128,256]{3,2,1,0:T(8,128)(2,1)S(1)}, f32[2,512,128]{2,1,0:T(8,128)S(1)}, f32[2,8,128]{2,1,0:T(8,128)S(1)}, f32[2,4,2,128,128]{4,3,2,1,0:T...) custom-call(bf16[256,512]{1,0:T(8,128)(2,1)S(1)} %get-tuple-element., ...), custom_call_target="tpu_custom_call" | custom-call | flops 65536 | bytes 1024 | tf_op jit(solution)/shard_map/prepare/pallas_call | solution.py:387
  13.6 2.6 %collective-permute-done.4.refs_0_ = bf16[256,512]{1,0:T(8,128)(2,1)S(1)} collective-permute-done((bf16[256,512]{1,0:T(8,128)(2,1)}, bf16[256,512]{1,0:T(8,128)(2,1)S(1)}, u32[]{:S(2)}, u32[]{:S(2)}) %collective-permute-start.4) | collective-permute-done | bytes 262176 | tf_op jit(solution)/shard_map/ppermute | solution.py:38
  16.2 1.7 %collective-permute-start.2 = (bf16[256,512]{1,0:T(8,128)(2,1)S(1)}, bf16[256,512]{1,0:T(8,128)(2,1)S(1)}, u32[]{:S(2)}, u32[]{:S(2)}) collective-permute-start(bf16[256,512]{1,0:T(8,128)(2,1)S(1)} %collective-permute-done.refs_1_), channel_id=1, source_target_pairs={{0,2},{1,3},{2,6},{3,7},{6,4},{7,5},{4,0},{5,1},{8,10},{9,11},{10,... | collective-permute-start | bytes 786440 | tf_op jit(solution)/shard_map/ppermute | solution.py:38
  17.9 3.0 %collective-permute-start.3 = (f32[8,512]{1,0:T(8,128)S(1)}, f32[8,512]{1,0:T(8,128)S(1)}, u32[]{:S(2)}, u32[]{:S(2)}) collective-permute-start(f32[8,512]{1,0:T(8,128)S(1)} %add.9), channel_id=1, source_target_pairs={{0,2},{1,3},{2,0},{3,1},{4,6},{5,7},{6,4},{7,5},{8,10},{9,11},{10,... | collective-permute-start | bytes 49160 | tf_op jit(solution)/shard_map/ppermute | solution.py:42
  21.0 3.1 %slots_0.1 = (f32[2,512,128]{2,1,0:T(8,128)S(1)}, f32[2,8,128]{2,1,0:T(8,128)S(1)}) custom-call(f32[2,4,8,128]{3,2,1,0:T(8,128)S(1)} %get-tuple-element.43.mask_ref.refs_0_, f32[1,512]{1,0:T(1,128)S(1)} %get-tuple-element.49.gain_ref.refs_2_, bf16[512,512]{1,0:T(8,128)(2,1)S(1)} %get-tuple-element.50.wk_ref.refs_3_, ...), custom_call_target="tpu_custom_call" | custom-call | flops 65536 | bytes 1024 | tf_op jit(solution)/shard_map/slots_0/pallas_call | solution.py:423
  24.1 2.0 %collective-permute-done.3 = f32[8,512]{1,0:T(8,128)S(1)} collective-permute-done((f32[8,512]{1,0:T(8,128)S(1)}, f32[8,512]{1,0:T(8,128)S(1)}, u32[]{:S(2)}, u32[]{:S(2)}) %collective-permute-start.3) | collective-permute-done | bytes 16416 | tf_op jit(solution)/shard_map/ppermute | solution.py:42
  26.1 1.6 %collective-permute-start.7 = (f32[8,512]{1,0:T(8,128)S(1)}, f32[8,512]{1,0:T(8,128)S(1)}, u32[]{:S(2)}, u32[]{:S(2)}) collective-permute-start(f32[8,512]{1,0:T(8,128)S(1)} %add.10), channel_id=1, source_target_pairs={{0,4},{1,5},{2,6},{3,7},{4,0},{5,1},{6,2},{7,3},{8,12},{9,13},{10,... | collective-permute-start | bytes 49160 | tf_op jit(solution)/shard_map/ppermute | solution.py:42
  27.8 2.3 %slots_1.1 = (f32[2,512,128]{2,1,0:T(8,128)S(1)}, f32[2,8,128]{2,1,0:T(8,128)S(1)}) custom-call(f32[2,4,8,128]{3,2,1,0:T(8,128)S(1)} %get-tuple-element.43.mask_ref.refs_0_, f32[1,512]{1,0:T(1,128)S(1)} %get-tuple-element.49.gain_ref.refs_2_, bf16[512,512]{1,0:T(8,128)(2,1)S(1)} %get-tuple-element.50.wk_ref.refs_3_, ...), custom_call_target="tpu_custom_call" | custom-call | flops 65536 | bytes 1024 | tf_op jit(solution)/shard_map/slots_1/pallas_call | solution.py:423
  30.1 0.7 %collective-permute-done.7 = f32[8,512]{1,0:T(8,128)S(1)} collective-permute-done((f32[8,512]{1,0:T(8,128)S(1)}, f32[8,512]{1,0:T(8,128)S(1)}, u32[]{:S(2)}, u32[]{:S(2)}) %collective-permute-start.7) | collective-permute-done | bytes 16416 | tf_op jit(solution)/shard_map/ppermute | solution.py:42
  30.8 1.6 %slots_2.1 = (f32[2,512,128]{2,1,0:T(8,128)S(1)}, f32[2,8,128]{2,1,0:T(8,128)S(1)}) custom-call(f32[2,4,8,128]{3,2,1,0:T(8,128)S(1)} %get-tuple-element.43.mask_ref.refs_0_, f32[1,512]{1,0:T(1,128)S(1)} %get-tuple-element.49.gain_ref.refs_2_, bf16[512,512]{1,0:T(8,128)(2,1)S(1)} %get-tuple-element.50.wk_ref.refs_3_, ...), custom_call_target="tpu_custom_call" | custom-call | flops 65536 | bytes 1024 | tf_op jit(solution)/shard_map/slots_2/pallas_call | solution.py:423
  32.4 2.6 %finish_first.1 = (bf16[128,512]{1,0:T(8,128)(2,1)S(1)}, bf16[128,512]{1,0:T(8,128)(2,1)S(1)}, bf16[512,128]{1,0:T(8,128)(2,1)S(1)}) custom-call(f32[2,4,8,128]{3,2,1,0:T(8,128)S(1)} %get-tuple-element.43.mask_ref.refs_0_, bf16[256,512]{1,0:T(8,128)(2,1)S(1)} %collective-permute-done.9.refs_1_, f32[1,512]{1,0:T(1,128)S(1)} %get-tuple-element.49.gain_ref.refs_2_, ...), custom_call_target="tpu_custom_call" | custom-call | flops 65536 | bytes 1024 | tf_op jit(solution)/shard_map/finish_first/pallas_call | solution.py:483
  35.0 1.6 %collective-permute-start.11 = (bf16[128,512]{1,0:T(8,128)(2,1)S(1)}, bf16[128,512]{1,0:T(8,128)(2,1)S(1)}, u32[]{:S(2)}, u32[]{:S(2)}) collective-permute-start(bf16[128,512]{1,0:T(8,128)(2,1)S(1)} %get-tuple-element.74), channel_id=1, source_target_pairs={{0,8},{8,16},{16,24},{24,0},{1,9},{9,17},{17,25},{25,1},{2,10},{10... | collective-permute-start | bytes 393224 | tf_op jit(solution)/shard_map/ppermute | solution.py:47
  36.6 1.7 %finish_rest.1 = bf16[128,512]{1,0:T(8,128)(2,1)S(1)} custom-call(bf16[128,512]{1,0:T(8,128)(2,1)S(1)} %get-tuple-element.72.refs_0_, bf16[512,128]{1,0:T(8,128)(2,1)S(1)} %get-tuple-element.73.refs_1_, f32[2,4,2,128,128]{4,3,2,1,0:T(8,128)S(1)} %get-tuple-element.52.counts_ref.refs_5_.refs_2_, ...), custom_call_target="tpu_custom_call" | custom-call | flops 65536 | bytes 1024 | tf_op jit(solution)/shard_map/finish_rest/pallas_call | solution.py:494
  38.3 1.5 %collective-permute-start.10 = (bf16[128,512]{1,0:T(8,128)(2,1)S(1)}, bf16[128,512]{1,0:T(8,128)(2,1)S(1)}, u32[]{:S(2)}, u32[]{:S(2)}) collective-permute-start(bf16[128,512]{1,0:T(8,128)(2,1)S(1)} %finish_rest.1), channel_id=1, source_target_pairs={{0,8},{8,16},{16,24},{24,0},{1,9},{9,17},{17,25},{25,1},{2,10},{10... | collective-permute-start | bytes 393224 | tf_op jit(solution)/shard_map/ppermute | solution.py:47
  39.8 2.0 %collective-permute-done.11.rows_ref = bf16[128,512]{1,0:T(8,128)(2,1)S(1)} collective-permute-done((bf16[128,512]{1,0:T(8,128)(2,1)S(1)}, bf16[128,512]{1,0:T(8,128)(2,1)S(1)}, u32[]{:S(2)}, u32[]{:S(2)}) %collective-permute-start.11) | collective-permute-done | bytes 131104 | tf_op jit(solution)/shard_map/ppermute | solution.py:47
  42.5 2.3 %collective-permute-done.10.rows_ref = bf16[128,512]{1,0:T(8,128)(2,1)S(1)} collective-permute-done((bf16[128,512]{1,0:T(8,128)(2,1)S(1)}, bf16[128,512]{1,0:T(8,128)(2,1)S(1)}, u32[]{:S(2)}, u32[]{:S(2)}) %collective-permute-start.10) | collective-permute-done | bytes 131104 | tf_op jit(solution)/shard_map/ppermute | solution.py:47
  (32 shorter events, 2.1 us)
Async XLA Ops:
  0.0 10.3 %copy-start.8 = (s32[2,8]{1,0:T(2,128)S(1)}, s32[2,8]{1,0:T(2,128)}, u32[]{:S(2)}) copy-start(s32[2,8]{1,0:T(2,128)} %sblock_hbm.1) | copy-start | bytes 196
  0.0 10.3 %copy-start.9 = (s32[2]{0:T(128)S(1)}, s32[2]{0:T(128)}, u32[]{:S(2)}) copy-start(s32[2]{0:T(128)} %scount_hbm.1) | copy-start | bytes 28
  0.0 13.5 %collective-permute-start = (bf16[256,512]{1,0:T(8,128)(2,1)}, bf16[256,512]{1,0:T(8,128)(2,1)S(1)}, u32[]{:S(2)}, u32[]{:S(2)}) collective-permute-start(bf16[256,512]{1,0:T(8,128)(2,1)} %bitcast.x_hbm.refs_11_.refs_8_), channel_id=1, source_target_pairs={{0,2},{1,3},{2,6},{3,7},{6,4},{7,5},{4,0},{5,1},{8,10},{9,11},{10,... | collective-permute-start | bytes 786440 | tf_op jit(solution)/shard_map/ppermute | solution.py:38
  3.0 13.1 %collective-permute-start.4 = (bf16[256,512]{1,0:T(8,128)(2,1)}, bf16[256,512]{1,0:T(8,128)(2,1)S(1)}, u32[]{:S(2)}, u32[]{:S(2)}) collective-permute-start(bf16[256,512]{1,0:T(8,128)(2,1)} %bitcast.x_hbm.refs_11_.refs_8_), channel_id=1, source_target_pairs={{0,4},{1,5},{2,0},{3,1},{6,2},{7,3},{4,6},{5,7},{8,12},{9,13},{10,... | collective-permute-start | bytes 786440 | tf_op jit(solution)/shard_map/ppermute | solution.py:38
  4.1 1.4 %copy-start = (bf16[1,512,1536]{2,1,0:T(8,128)(2,1)S(1)}, bf16[1,512,1536]{2,1,0:T(8,128)(2,1)}, u32[]{:S(2)}) copy-start(bf16[1,512,1536]{2,1,0:T(8,128)(2,1)} %param.12) | copy-start | bytes 4718596
  5.5 0.7 %copy-start.5 = (bf16[1,4,512]{2,1,0:T(4,128)(2,1)S(1)}, bf16[1,4,512]{2,1,0:T(4,128)(2,1)}, u32[]{:S(2)}) copy-start(bf16[1,4,512]{2,1,0:T(4,128)(2,1)} %param.14) | copy-start | bytes 12292
  6.2 0.7 %copy-start.6 = (s32[256,1]{0,1:T(1,128)S(1)}, s32[256,1]{0,1:T(1,128)}, u32[]{:S(2)}) copy-start(s32[256,1]{0,1:T(1,128)} %param.15) | copy-start | bytes 3076
  6.9 0.7 %copy-start.7 = (f32[1,512]{1,0:T(1,128)S(1)}, f32[1,512]{1,0:T(1,128)}, u32[]{:S(2)}) copy-start(f32[1,512]{1,0:T(1,128)} %gain_hbm.1) | copy-start | bytes 6148
  7.6 2.7 %copy-start.1 = (bf16[1,512,1536]{2,1,0:T(8,128)(2,1)S(1)}, bf16[1,512,1536]{2,1,0:T(8,128)(2,1)}, u32[]{:S(2)}) copy-start(bf16[1,512,1536]{2,1,0:T(8,128)(2,1)} %param.12) | copy-start | bytes 4718596
  7.6 2.7 %copy-start.3 = (s32[2,8,4,128]{3,2,1,0:T(4,128)S(1)}, s32[2,8,4,128]{3,2,1,0:T(4,128)}, u32[]{:S(2)}) copy-start(s32[2,8,4,128]{3,2,1,0:T(4,128)} %srows_hbm.1) | copy-start | bytes 98308
  7.6 2.7 %copy-start.4 = (s32[16,256]{1,0:T(8,128)S(1)}, s32[16,256]{1,0:T(8,128)}, u32[]{:S(2)}) copy-start(s32[16,256]{1,0:T(8,128)} %lrows_hbm.1) | copy-start | bytes 49156
  9.7 3.8 %collective-permute-start.1 = (f32[8,512]{1,0:T(8,128)S(1)}, f32[8,512]{1,0:T(8,128)S(1)}, u32[]{:S(2)}, u32[]{:S(2)}) collective-permute-start(f32[8,512]{1,0:T(8,128)S(1)} %get-tuple-element.44), channel_id=1, source_target_pairs={{0,1},{1,0},{2,3},{3,2},{4,5},{5,4},{6,7},{7,6},{8,9},{9,8},{10,11... | collective-permute-start | bytes 49160 | tf_op jit(solution)/shard_map/ppermute | solution.py:42
  9.8 11.2 %collective-permute-start.5 = (bf16[256,512]{1,0:T(8,128)(2,1)}, bf16[256,512]{1,0:T(8,128)(2,1)S(1)}, u32[]{:S(2)}, u32[]{:S(2)}) collective-permute-start(bf16[256,512]{1,0:T(8,128)(2,1)} %bitcast.x_hbm.refs_11_.refs_8_), channel_id=1, source_target_pairs={{0,1},{1,0},{2,3},{3,2},{4,5},{5,4},{6,7},{7,6},{8,9},{9,8},{10,11... | collective-permute-start | bytes 786440 | tf_op jit(solution)/shard_map/ppermute | solution.py:42
  10.3 1.0 %copy-start.2 = (bf16[1,512,512]{2,1,0:T(8,128)(2,1)S(1)}, bf16[1,512,512]{2,1,0:T(8,128)(2,1)}, u32[]{:S(2)}) copy-start(bf16[1,512,512]{2,1,0:T(8,128)(2,1)} %param.13) | copy-start | bytes 1572868
  13.5 7.5 %collective-permute-start.6 = (bf16[256,512]{1,0:T(8,128)(2,1)S(1)}, bf16[256,512]{1,0:T(8,128)(2,1)S(1)}, u32[]{:S(2)}, u32[]{:S(2)}) collective-permute-start(bf16[256,512]{1,0:T(8,128)(2,1)S(1)} %collective-permute-done.refs_1_), channel_id=1, source_target_pairs={{0,1},{1,0},{2,3},{3,2},{4,5},{5,4},{6,7},{7,6},{8,9},{9,8},{10,11... | collective-permute-start | bytes 786440 | tf_op jit(solution)/shard_map/ppermute | solution.py:42
  16.2 11.6 %collective-permute-start.8 = (bf16[256,512]{1,0:T(8,128)(2,1)S(1)}, bf16[256,512]{1,0:T(8,128)(2,1)S(1)}, u32[]{:S(2)}, u32[]{:S(2)}) collective-permute-start(bf16[256,512]{1,0:T(8,128)(2,1)S(1)} %collective-permute-done.4.refs_0_), channel_id=1, source_target_pairs={{0,1},{1,0},{2,3},{3,2},{4,5},{5,4},{6,7},{7,6},{8,9},{9,8},{10,11... | collective-permute-start | bytes 786440 | tf_op jit(solution)/shard_map/ppermute | solution.py:42
  16.2 14.6 %collective-permute-start.2 = (bf16[256,512]{1,0:T(8,128)(2,1)S(1)}, bf16[256,512]{1,0:T(8,128)(2,1)S(1)}, u32[]{:S(2)}, u32[]{:S(2)}) collective-permute-start(bf16[256,512]{1,0:T(8,128)(2,1)S(1)} %collective-permute-done.refs_1_), channel_id=1, source_target_pairs={{0,2},{1,3},{2,6},{3,7},{6,4},{7,5},{4,0},{5,1},{8,10},{9,11},{10,... | collective-permute-start | bytes 786440 | tf_op jit(solution)/shard_map/ppermute | solution.py:38
  17.9 8.2 %collective-permute-start.3 = (f32[8,512]{1,0:T(8,128)S(1)}, f32[8,512]{1,0:T(8,128)S(1)}, u32[]{:S(2)}, u32[]{:S(2)}) collective-permute-start(f32[8,512]{1,0:T(8,128)S(1)} %add.9), channel_id=1, source_target_pairs={{0,2},{1,3},{2,0},{3,1},{4,6},{5,7},{6,4},{7,5},{8,10},{9,11},{10,... | collective-permute-start | bytes 49160 | tf_op jit(solution)/shard_map/ppermute | solution.py:42
  26.1 4.6 %collective-permute-start.7 = (f32[8,512]{1,0:T(8,128)S(1)}, f32[8,512]{1,0:T(8,128)S(1)}, u32[]{:S(2)}, u32[]{:S(2)}) collective-permute-start(f32[8,512]{1,0:T(8,128)S(1)} %add.10), channel_id=1, source_target_pairs={{0,4},{1,5},{2,6},{3,7},{4,0},{5,1},{6,2},{7,3},{8,12},{9,13},{10,... | collective-permute-start | bytes 49160 | tf_op jit(solution)/shard_map/ppermute | solution.py:42
  30.8 1.6 %collective-permute-start.9 = (bf16[256,512]{1,0:T(8,128)(2,1)S(1)}, bf16[256,512]{1,0:T(8,128)(2,1)S(1)}, u32[]{:S(2)}, u32[]{:S(2)}) collective-permute-start(bf16[256,512]{1,0:T(8,128)(2,1)S(1)} %collective-permute-done.2.refs_0_), channel_id=1, source_target_pairs={{0,1},{1,0},{2,3},{3,2},{4,5},{5,4},{6,7},{7,6},{8,9},{9,8},{10,11... | collective-permute-start | bytes 786440 | tf_op jit(solution)/shard_map/ppermute | solution.py:42
  35.0 6.9 %collective-permute-start.11 = (bf16[128,512]{1,0:T(8,128)(2,1)S(1)}, bf16[128,512]{1,0:T(8,128)(2,1)S(1)}, u32[]{:S(2)}, u32[]{:S(2)}) collective-permute-start(bf16[128,512]{1,0:T(8,128)(2,1)S(1)} %get-tuple-element.74), channel_id=1, source_target_pairs={{0,8},{8,16},{16,24},{24,0},{1,9},{9,17},{17,25},{25,1},{2,10},{10... | collective-permute-start | bytes 393224 | tf_op jit(solution)/shard_map/ppermute | solution.py:47
  38.3 6.6 %collective-permute-start.10 = (bf16[128,512]{1,0:T(8,128)(2,1)S(1)}, bf16[128,512]{1,0:T(8,128)(2,1)S(1)}, u32[]{:S(2)}, u32[]{:S(2)}) collective-permute-start(bf16[128,512]{1,0:T(8,128)(2,1)S(1)} %finish_rest.1), channel_id=1, source_target_pairs={{0,8},{8,16},{16,24},{24,0},{1,9},{9,17},{17,25},{25,1},{2,10},{10... | collective-permute-start | bytes 393224 | tf_op jit(solution)/shard_map/ppermute | solution.py:47
where the time goes:
time: 45.8 us; the launch traced here: 45.5 us
  Pallas kernels  16.8 us (37%)
  starting transfers between devices  14.4 us (31%)
  waiting for transfers between devices  9.65 us (21%)
  local copies, waits for them, and re-layouts  4.51 us (10%)
    pallas_call x3, Pallas kernels, slots_call(): pl.pallas_call(functools.partial(slots_kernel, tuple(names)), out_shape=a...  7.07 us
    ppermute x3, starting transfers between devices, to_next_chip(): return lax.ppermute(value, 'node', pairs)  5.83 us
    ppermute x7, starting transfers between devices, swapped(): lax.ppermute(value, 'node', [(d, d ^ distance) for d in range(devices)])  5.39 us
    unnamed x20, local copies, waits for them, and re-layouts  4.51 us
    ppermute x2, waiting for transfers between devices, to_next_segment(): lax.ppermute(value, 'segment', [(s, (s + 1) % count) for s in range(count)])  4.36 us
    ppermute x2, starting transfers between devices, to_next_segment(): lax.ppermute(value, 'segment', [(s, (s + 1) % count) for s in range(count)])  3.14 us
    ppermute x7, waiting for transfers between devices, swapped(): lax.ppermute(value, 'node', [(d, d ^ distance) for d in range(devices)])  2.73 us
    ppermute x3, waiting for transfers between devices, to_next_chip(): return lax.ppermute(value, 'node', pairs)  2.56 us
  transfers between devices with their start and end apart: 12, of which 5 were waited for; matrix products, arithmetic and copies ran while one was open for 0% of the time, Pallas kernels for 30%

commit v1 on v0

v1 whole, which is shorter than its diff:
```python
import functools

import jax
import jax.numpy as jnp
from jax import lax
from jax.experimental import pallas as pl
from jax.experimental.pallas import tpu as pltpu
from jax.sharding import PartitionSpec as P

HEADS = 8
CORES = 2
EPSILON = 1e-05
CAP_LIMIT = 10.0
LOG2E = 1.4426950408889634
EXTRA = 16
PACK_MIB = 60
PREP_MIB = 32
F32 = jnp.float32
BF16 = jnp.bfloat16
HBM = pl.BlockSpec(memory_space=pltpu.HBM)
VMEM = pl.BlockSpec(memory_space=pltpu.VMEM)


def ring_order(chips):
    return list(range(0, 1)) + list(range(1, chips, 2)) + list(range((chips - 1) // 2 * 2, 0, -2))


def ring_place(chip, chips):
    return jnp.where(chip % 2 == 1, (chip + 1) // 2, (chips - chip // 2) % chips)


def to_next_chip(value, devices, way):
    chips = devices // CORES
    order = ring_order(chips)
    pairs = [
        (order[i] * CORES + c, order[(i + way) % chips] * CORES + c)
        for i in range(chips)
        for c in range(CORES)
    ]
    return lax.ppermute(value, "node", pairs)


def swapped(value, devices, distance):
    return lax.ppermute(value, "node", [(d, d ^ distance) for d in range(devices)])


def to_next_segment(value):
    count = lax.axis_size("segment")
    return lax.ppermute(value, "segment", [(s, (s + 1) % count) for s in range(count)])


def norm_rows(rows_in, gain_row):
    widened = rows_in.astype(F32)
    center = widened - jnp.mean(widened, axis=-1, keepdims=True)
    spread = jnp.mean(center * center, axis=-1, keepdims=True)
    return (center * lax.rsqrt(spread + EPSILON) * gain_row).astype(BF16)


def exp_capped(raw, scale):
    return jnp.exp2((CAP_LIMIT * LOG2E) * jnp.tanh(raw * (scale / CAP_LIMIT)))


def counts_of(index_rows, block_rows):
    rows = lax.broadcasted_iota(jnp.int32, (block_rows, index_rows.shape[1]), 0)
    total = jnp.zeros(rows.shape, F32)
    for j in range(index_rows.shape[0]):
        total = total + jnp.where(index_rows[j : j + 1, :] == rows, 1.0, 0.0)
    return total


def mm(a, b):
    return jnp.dot(a, b, preferred_element_type=F32)


def mm_nt(a, b):
    return lax.dot_general(a, b, (((1,), (1,)), ((), ())), preferred_element_type=F32)


def choose(mask_row, rows):
    lanes = mask_row.shape[1]
    count, width = rows.shape
    br = count // 2
    mask = jnp.broadcast_to(mask_row, (br, lanes))
    mask = jnp.concatenate([mask] * (width // lanes), axis=1)
    first, second = rows[:br, :].astype(F32), rows[br:, :].astype(F32)
    return jnp.where(mask > 0.5, second, first).astype(rows.dtype)


def halves(value):
    high = value.astype(BF16)
    low = (value - high.astype(F32)).astype(BF16)
    return jnp.concatenate([high, low], axis=0)


def of_own_head(shape):
    head = lax.broadcasted_iota(jnp.int32, shape, 0) % HEADS
    return head == lax.broadcasted_iota(jnp.int32, shape, 1) // (shape[1] // HEADS)


def add_pool(normed, vid_row, vkw_ref, pool_ref, weight_ref, scale, first):
    count = pool_ref.shape[0]
    raw = mm_nt(vkw_ref[...], normed)
    raw = raw[:count] + raw[count:]
    owner = lax.broadcasted_iota(jnp.int32, raw.shape, 0) // HEADS
    w = jnp.where(vid_row == owner.astype(F32), exp_capped(raw, scale), 0.0).astype(BF16)
    sums = mm(w, normed)
    totals = jnp.broadcast_to(
        jnp.sum(w.astype(F32), axis=1, keepdims=True), weight_ref.shape
    )
    pool_ref[...] = sums if first else pool_ref[...] + sums
    weight_ref[...] = totals if first else weight_ref[...] + totals


def start_copies(pairs, sems):
    copies = [pltpu.make_async_copy(src, dst, sems.at[i]) for i, (src, dst) in enumerate(pairs)]
    for copy in copies:
        copy.start()
    return copies


def pack_kernel(x_hbm, vid_hbm, load_ref, vid_ref, sems):
    rows = vid_ref.shape[1]
    copies = start_copies([(x_hbm, load_ref.at[:rows, :]), (vid_hbm, vid_ref)], sems)
    copies[1].wait()
    tile = jnp.broadcast_to(vid_ref[...].astype(F32), (EXTRA, rows))
    rest = jnp.zeros((EXTRA, load_ref.shape[1] - rows), F32)
    load_ref[rows:, :] = jnp.concatenate([tile, rest], axis=1).astype(BF16)
    copies[0].wait()


def vid_row(load_ref, rows):
    return load_ref[rows:, :rows].astype(F32)[:1, :]


def attend(keys, values, counts, qbd, scale):
    p = (counts * exp_capped(mm(keys, qbd), scale)).astype(BF16)
    return mm(values, p)


def fold(o, num_ref, den_ref, b, t, add):
    wide = o.shape[0] - EXTRA
    head = wide // 2
    br = o.shape[1] // 2
    r0 = t * wide
    places = (
        (num_ref, slice(r0, r0 + head), o[:head, :br]),
        (num_ref, slice(r0 + head, r0 + wide), o[head:wide, br:]),
        (den_ref, slice(2 * t, 2 * t + 1), o[wide : wide + 1, :br]),
        (den_ref, slice(2 * t + 1, 2 * t + 2), o[wide : wide + 1, br:]),
    )
    for ref, part, value in places:
        if add:
            ref[b, part, :] += value
        else:
            ref[b, part, :] = value


def prep_kernel(
    load_ref, gain_hbm, win_hbm, vk_hbm, lrows_hbm, srows_hbm, sblock_hbm, scount_hbm, wo_hbm,
    qbd_ref, num_ref, den_ref, counts_ref, mask_ref, vcol_ref, wk_ref, wvt_ref, wo_ref, gain_ref,
    vkw_ref, pool_ref, weight_ref,
    wq_ref, wv_ref, vk_ref, lrows_ref, srows_ref, sblock_ref, scount_ref, want_ref, sems,
):
    width = load_ref.shape[1]
    rows = load_ref.shape[0] - EXTRA
    blocks, pairs, wide, _ = qbd_ref.shape
    chips = mask_ref.shape[1]
    slots = sblock_ref.shape[1]
    virtual = vk_ref.shape[0]
    br = rows // blocks
    head = width // HEADS
    scale = head ** (-0.5)
    copies = start_copies(
        [
            (gain_hbm, gain_ref), (sblock_hbm, sblock_ref), (scount_hbm, scount_ref),
            (srows_hbm, srows_ref), (lrows_hbm, lrows_ref), (vk_hbm, vk_ref),
            (win_hbm.at[:, width : 2 * width], wk_ref), (win_hbm.at[:, :width], wq_ref),
            (win_hbm.at[:, 2 * width :], wv_ref), (wo_hbm, wo_ref),
        ],
        sems,
    )
    counts_ref[...] = jnp.zeros(counts_ref.shape, F32)
    for copy in copies:
        copy.wait()
    normed = norm_rows(load_ref[:rows, :], gain_ref[...])
    k = mm(normed, wk_ref[...]).astype(BF16)
    v = mm(normed, wv_ref[...]).astype(BF16)
    qt = mm(normed, wq_ref[...]).astype(BF16).T
    vt = v.T
    wvt_ref[...] = wv_ref[...].T

    vkf = vk_ref[...].astype(F32)
    vkbd = jnp.concatenate(
        [jnp.broadcast_to(vkf[j : j + 1, :], (HEADS, width)) for j in range(virtual)], axis=0
    )
    vkbd = jnp.where(of_own_head(vkbd.shape), vkbd, 0.0).astype(BF16)
    vkw_ref[...] = halves(mm_nt(vkbd, wk_ref[...]))
    vid = vid_row(load_ref, rows)
    add_pool(normed, vid, vkw_ref, pool_ref, weight_ref, scale, True)
    vcol_ref[...] = jnp.broadcast_to(vid, (128, rows)).T

    me = lax.axis_index("node")
    place = ring_place(me // CORES, chips)
    core = me % CORES
    for d in range(chips * CORES):
        want_ref[d] = 0
    for b in range(blocks):
        for e in range(slots):
            entry = sblock_ref[b, e]
            want_ref[entry // blocks] = entry % blocks
    for d in range(chips * CORES):
        step = (place - ring_place(jnp.int32(d // CORES), chips) + chips) % chips
        far = jnp.where(core == d % CORES, 0, 1)
        mask_ref[far, step] = jnp.full(mask_ref.shape[2:], want_ref[d].astype(F32), F32)
    for b in range(blocks):
        for e in range(slots):
            device = sblock_ref[b, e] // blocks
            step = (place - ring_place(device // CORES, chips) + chips) % chips
            far = jnp.where(device % CORES == core, 0, 1)
            live = jnp.where(e < scount_ref[b], 1.0, 0.0).astype(F32)
            counts_ref[far, step, b] += counts_of(srows_ref[b, e], br) * live

    zero = jnp.zeros((head, br), BF16)
    ones = jnp.ones((EXTRA, br), BF16)
    for b in range(blocks):
        cols = slice(b * br, (b + 1) * br)
        counts = counts_of(lrows_ref[:, cols], br)
        counts2 = jnp.concatenate([counts, counts], axis=1)
        for t in range(pairs):
            r0 = t * wide
            mid = r0 + head
            end = r0 + wide
            bd = jnp.concatenate(
                [
                    jnp.concatenate([qt[r0:mid, cols], zero], axis=1),
                    jnp.concatenate([zero, qt[mid:end, cols]], axis=1),
                ],
                axis=0,
            )
            qbd_ref[b, t] = bd
            values = jnp.concatenate([vt[r0:end, cols], ones], axis=0)
            fold(attend(k[cols, r0:end], values, counts2, bd, scale), num_ref, den_ref, b, t, False)


def take_sources(
    names, loads, mask_ref, gain_ref, wk_ref, wvt_ref, vkw_ref,
    normed_ref, k_ref, vt_ref, pool_ref, weight_ref,
):
    rows = loads[0].shape[0] - EXTRA
    width = k_ref.shape[1]
    chosen = []
    vids = []
    for i, ((far, step), load_ref) in enumerate(zip(names, loads)):
        part = norm_rows(load_ref[:rows, :], gain_ref[...])
        normed_ref[i * rows : (i + 1) * rows, :] = part
        chosen.append(choose(mask_ref[far, step, :1, :], part))
        vids.append(vid_row(load_ref, rows))
    picked = jnp.concatenate(chosen, axis=0)
    k_ref[...] = mm(picked, wk_ref[...]).astype(BF16)
    vt_ref[...] = mm_nt(wvt_ref[...], picked).astype(BF16)
    scale = (width // HEADS) ** (-0.5)
    vid = jnp.concatenate(vids, axis=1)
    add_pool(normed_ref[...], vid, vkw_ref, pool_ref, weight_ref, scale, False)


def add_sources(names, b, counts_ref, qbd_ref, k_ref, vt_ref, num_ref, den_ref):
    _, pairs, wide, _ = qbd_ref.shape
    scale = (2 / wide) ** 0.5
    counts = jnp.concatenate([counts_ref[far, step, b] for far, step in names], axis=0)
    counts2 = jnp.concatenate([counts, counts], axis=1)
    ones = jnp.ones((EXTRA, counts.shape[0]), BF16)
    for t in range(pairs):
        cols = slice(t * wide, (t + 1) * wide)
        values = jnp.concatenate([vt_ref[cols, :], ones], axis=0)
        o = attend(k_ref[:, cols], values, counts2, qbd_ref[b, t], scale)
        fold(o, num_ref, den_ref, b, t, True)


def slots_kernel(
    names, mask_ref, gain_ref, wk_ref, wvt_ref, vkw_ref, counts_ref, qbd_ref,
    num_in, den_in, pool_in, weight_in, *refs
):
    loads = refs[: len(names)]
    num_ref, den_ref, pool_ref, weight_ref, normed_ref, k_ref, vt_ref = refs[len(names) :]
    num_ref[...] = num_in[...]
    den_ref[...] = den_in[...]
    pool_ref[...] = pool_in[...]
    weight_ref[...] = weight_in[...]
    take_sources(
        names, loads, mask_ref, gain_ref, wk_ref, wvt_ref, vkw_ref,
        normed_ref, k_ref, vt_ref, pool_ref, weight_ref,
    )
    for b in range(num_ref.shape[0]):
        add_sources(names, b, counts_ref, qbd_ref, k_ref, vt_ref, num_ref, den_ref)


def finish_kernel(
    names, mask_ref, gain_ref, wk_ref, wvt_ref, vkw_ref, counts_ref, qbd_ref,
    num_in, den_in, pool_in, weight_in, last_ref, vcol_ref, load_ref, wo_ref,
    out_ref, num_ref, den_ref, pool_ref, weight_ref, normed_ref, k_ref, vt_ref,
):
    slots_kernel(
        names, mask_ref, gain_ref, wk_ref, wvt_ref, vkw_ref, counts_ref, qbd_ref,
        num_in, den_in, pool_in, weight_in, last_ref,
        num_ref, den_ref, pool_ref, weight_ref, normed_ref, k_ref, vt_ref,
    )
    blocks, width, br = num_ref.shape
    head = width // HEADS
    lanes = vcol_ref.shape[1]
    count = pool_ref.shape[0]
    weight = jnp.concatenate([weight_ref[...]] * (width // lanes), axis=1)
    both = mm_nt(halves(pool_ref[...] / weight), wvt_ref[...])
    both = jnp.where(of_own_head((count, width)), both[:count] + both[count:], 0.0)
    pooled = [
        jnp.sum(both[j : j + HEADS], axis=0, keepdims=True) for j in range(0, count, HEADS)
    ]
    for b in range(blocks):
        part = slice(b * br, (b + 1) * br)
        vid = vcol_ref[part, :]
        att = jnp.concatenate(
            [
                num_ref[b, h * head : (h + 1) * head, :] / den_ref[b, h : h + 1, :]
                for h in range(HEADS)
            ],
            axis=0,
        ).T
        pieces = []
        for c in range(0, width, lanes):
            own = jnp.broadcast_to(pooled[0][:, c : c + lanes], (br, lanes))
            for j in range(1, len(pooled)):
                own = jnp.where(vid == float(j), pooled[j][:, c : c + lanes], own)
            pieces.append((att[:, c : c + lanes] + own).astype(BF16))
        mixed = jnp.concatenate(pieces, axis=1)
        out_ref[part, :] = (load_ref[part, :].astype(F32) + mm(mixed, wo_ref[...])).astype(BF16)


def params(mib):
    return pltpu.CompilerParams(vmem_limit_bytes=mib * 2**20)


def cost(flops):
    return pl.CostEstimate(flops=flops, bytes_accessed=1024, transcendentals=0)


def body(
    activations,
    norm_gain,
    project_in,
    project_out,
    virtual_keys,
    virtual_id,
    local_rows,
    slot_block,
    slot_count,
    slot_rows,
):
    _, rows, width = activations.shape
    br = slot_rows.shape[3]
    slots = slot_block.shape[1]
    blocks = rows // br
    devices = lax.axis_size("node")
    chips = devices // CORES
    virtual = virtual_keys.shape[1]
    pairs = HEADS // 2
    wide = width // pairs
    shape = jax.ShapeDtypeStruct
    after = lax.optimization_barrier
    unit = 2**16

    load = pl.pallas_call(
        pack_kernel,
        out_shape=shape((rows + EXTRA, width), BF16),
        in_specs=[HBM] * 2,
        out_specs=VMEM,
        scratch_shapes=[pltpu.VMEM((1, rows), jnp.int32), pltpu.SemaphoreType.DMA((2,))],
        compiler_params=params(PACK_MIB),
        cost_estimate=cost(unit),
        name="pack_rows",
    )(activations[0], virtual_id.reshape(1, rows))
    near = {1: to_next_chip(load, devices, 1)}
    if chips > 2:
        near[chips - 1] = to_next_chip(load, devices, -1)
    far = {0: swapped(load, devices, 1)}

    accumulators = (
        shape((blocks, width, br), F32),
        shape((blocks, HEADS, br), F32),
        shape((virtual * HEADS, width), F32),
        shape((virtual * HEADS, 128), F32),
    )
    square = shape((width, width), BF16)
    qbd, num, den, counts, mask, vcol, wk, wvt, wo, gain, vkw, pool, weight = pl.pallas_call(
        prep_kernel,
        out_shape=(
            (shape((blocks, pairs, wide, 2 * br), BF16),)
            + accumulators[:2]
            + (
                shape((CORES, chips, blocks, br, br), F32),
                shape((CORES, chips, 8, 128), F32),
                shape((rows, 128), F32),
                square,
                square,
                square,
                shape((1, width), F32),
                shape((2 * virtual * HEADS, width), BF16),
            )
            + accumulators[2:]
        ),
        in_specs=[VMEM] + [HBM] * 8,
        out_specs=[VMEM] * 13,
        scratch_shapes=[
            pltpu.VMEM((width, width), BF16),
            pltpu.VMEM((width, width), BF16),
            pltpu.VMEM((virtual, width), BF16),
            pltpu.VMEM(local_rows.shape, jnp.int32),
            pltpu.VMEM(slot_rows.shape, jnp.int32),
            pltpu.SMEM((blocks, slots), jnp.int32),
            pltpu.SMEM((blocks,), jnp.int32),
            pltpu.SMEM((devices,), jnp.int32),
            pltpu.SemaphoreType.DMA((10,)),
        ],
        compiler_params=params(PREP_MIB),
        cost_estimate=cost(unit),
        name="prepare",
    )(
        load, norm_gain, project_in[0], virtual_keys[0], local_rows, slot_rows, slot_block,
        slot_count, project_out[0],
    )

    def work(count):
        return [
            pltpu.VMEM((count * rows, width), BF16),
            pltpu.VMEM((count * br, width), BF16),
            pltpu.VMEM((width, count * br), BF16),
        ]

    sums = (num, den, pool, weight)

    def arrive(step, sums):
        near[step], first = after((near[step], sums[1]))
        return (sums[0], first) + sums[2:]

    def slots_call(names, sums, name):
        return pl.pallas_call(
            functools.partial(slots_kernel, tuple(names)),
            out_shape=accumulators,
            in_specs=[VMEM] * (11 + len(names)),
            out_specs=[VMEM] * 4,
            scratch_shapes=work(len(names)),
            compiler_params=params(40),
            cost_estimate=cost(unit),
            name=name,
        )(
            mask, gain, wk, wvt, vkw, counts, qbd, *sums,
            *[(far if other else near)[step] for other, step in names],
        )

    ahead = chips // 2
    order = []
    for s in range(1, ahead + 1):
        order.append((s, 1))
        if s < chips - s:
            order.append((chips - s, -1))
    waiting = [(1, 0)]
    for i, (step, way) in enumerate(order):
        if step not in far:
            sums = arrive(step, sums)
            nexts = step + way
            if nexts not in near and (nexts, way) in order:
                near[nexts] = to_next_chip(near[step], devices, way)
            far[step] = swapped(near[step], devices, 1)
        waiting.append((0, step))
        if i == len(order) - 1:
            break
        waiting.append((1, step))
        if i == len(order) - 2:
            continue
        sums = slots_call(waiting, sums, "slots_%d" % i)
        waiting = []
    sums = slots_call(waiting, sums, "slots_last")
    names = ((1, order[-1][0]),)
    updated = pl.pallas_call(
        functools.partial(finish_kernel, names),
        out_shape=shape((rows, width), BF16),
        in_specs=[VMEM] * 15,
        out_specs=VMEM,
        scratch_shapes=[pltpu.VMEM(leaf.shape, leaf.dtype) for leaf in accumulators] + work(1),
        compiler_params=params(40),
        cost_estimate=cost(unit),
        name="finish",
    )(
        mask, gain, wk, wvt, vkw, counts, qbd, *sums, far[names[0][1]], vcol, load, wo
    )
    return to_next_segment(updated[None])


def solution(mesh):
    placed = (
        P("segment", "node", None),
        P("segment", None),
        P("segment", None, None),
        P("segment", None, None),
        P("segment", None, None),
        P("node", None),
        P(None, "node"),
        P("node", None),
        P("node"),
        P("node", None, None, None),
    )
    return jax.shard_map(
        body, mesh=mesh, in_specs=placed, out_specs=P("segment", "node", None), check_vma=False
    )
```

time: 45.8 us -> 49.9 us (1.090)
  waiting for transfers between devices: 9.65 us -> 18.1 us
  starting transfers between devices: 14.4 us -> 8.04 us
  local copies, waits for them, and re-layouts: 4.51 us -> 7.33 us
  Pallas kernels: 16.8 us -> 15.8 us
    ppermute x3, waiting for transfers between devices: 2.56 us -> 10.2 us  [to_next_chip(): return lax.ppermute(value, 'node', pairs)]
    ppermute x7 -> x4, starting transfers between devices: 5.39 us -> 0.58 us  [swapped(): lax.ppermute(value, 'node', [(d, d ^ distance) for d in range(devices)])]
    ppermute x2 -> x1, waiting for transfers between devices: 4.36 us -> 7.93 us  [to_next_segment(): lax.ppermute(value, 'segment', [(s, (s + 1) % count) for s in range(count)])]
    pallas_call x5 -> x2, Pallas kernels: 7.65 us -> 4.8 us  [the longest x1 3.13 us: body(): pl.pallas_call(functools.partial(finish_kernel, names), out_shape=shape((...]
    unnamed x20 -> x17, local copies, waits for them, and re-layouts: 4.51 us -> 7.33 us
    ppermute x7 -> x4, waiting for transfers between devices: 2.73 us -> 0.01 us  [swapped(): lax.ppermute(value, 'node', [(d, d ^ distance) for d in range(devices)])]
    pallas_call x1, Pallas kernels: 2.12 us -> 3.89 us  [body(): pl.pallas_call(prep_kernel, out_shape=(shape((blocks, pairs, wide, 2 * br...]
    ppermute x2 -> x1, starting transfers between devices: 3.14 us -> 1.79 us  [to_next_segment(): lax.ppermute(value, 'segment', [(s, (s + 1) % count) for s in range(count)])]
  transfers between devices with their start and end apart: 12 -> 8, of which waited for: 5 -> 3; matrix products, arithmetic and copies ran while one was open for 0% -> 0% of each run, Pallas kernels for 30% -> 22%
where the time goes in v1:
time: 49.9 us; the launch traced here: 49.4 us
  waiting for transfers between devices  18.1 us (36%)
  Pallas kernels  15.8 us (32%)
  starting transfers between devices  8.04 us (16%)
  local copies, waits for them, and re-layouts  7.33 us (15%)
    ppermute x3, waiting for transfers between devices, to_next_chip(): return lax.ppermute(value, 'node', pairs)  10.2 us
    ppermute x1, waiting for transfers between devices, to_next_segment(): lax.ppermute(value, 'segment', [(s, (s + 1) % count) for s in range(count)])  7.93 us
    unnamed x17, local copies, waits for them, and re-layouts  7.33 us
    pallas_call x2, Pallas kernels, slots_call(): pl.pallas_call(functools.partial(slots_kernel, tuple(names)), out_shape=a...  7.12 us
    ppermute x3, starting transfers between devices, to_next_chip(): return lax.ppermute(value, 'node', pairs)  5.67 us
    pallas_call x1, Pallas kernels, body(): pl.pallas_call(prep_kernel, out_shape=(shape((blocks, pairs, wide, 2 * br...  3.89 us
    pallas_call x1, Pallas kernels, body(): pl.pallas_call(functools.partial(finish_kernel, names), out_shape=shape((...  3.13 us
    ppermute x1, starting transfers between devices, to_next_segment(): lax.ppermute(value, 'segment', [(s, (s + 1) % count) for s in range(count)])  1.79 us
  transfers between devices with their start and end apart: 8, of which 3 were waited for; matrix products, arithmetic and copies ran while one was open for 0% of the time, Pallas kernels for 22%

profile of v1, /device:TPU:0, one launch (start us, length us, event | category | flops | bytes accessed | tf_op | source)
XLA Modules:
  0.0 49.4 jit_solution(1095741855173780337)
XLA Ops:
  0.0 1.7 %pack_rows.1.load_ref = bf16[272,512]{1,0:T(8,128)(2,1)} custom-call(bf16[256,512]{1,0:T(8,128)(2,1)} %bitcast.10, s32[1,256]{1,0:T(1,128)} %bitcast.11), custom_call_target="tpu_custom_call" | custom-call | flops 65536 | bytes 1024 | tf_op jit(solution)/shard_map/pack_rows/pallas_call | solution.py:370
  1.7 3.1 %collective-permute-start = (bf16[272,512]{1,0:T(8,128)(2,1)}, bf16[272,512]{1,0:T(8,128)(2,1)S(1)}, u32[]{:S(2)}, u32[]{:S(2)}) collective-permute-start(bf16[272,512]{1,0:T(8,128)(2,1)} %pack_rows.1.load_ref), channel_id=1, source_target_pairs={{0,2},{1,3},{2,6},{3,7},{6,4},{7,5},{4,0},{5,1},{8,10},{9,11},{10,... | collective-permute-start | bytes 835592 | tf_op jit(solution)/shard_map/ppermute | solution.py:40
  4.8 1.4 %copy-done = bf16[1,512,1536]{2,1,0:T(8,128)(2,1)S(1)} copy-done((bf16[1,512,1536]{2,1,0:T(8,128)(2,1)S(1)}, bf16[1,512,1536]{2,1,0:T(8,128)(2,1)}, u32[]{:S(2)}) %copy-start) | copy-done | bytes 1572888
  6.2 1.0 %copy-done.1 = bf16[1,512,512]{2,1,0:T(8,128)(2,1)S(1)} copy-done((bf16[1,512,512]{2,1,0:T(8,128)(2,1)S(1)}, bf16[1,512,512]{2,1,0:T(8,128)(2,1)}, u32[]{:S(2)}) %copy-start.1) | copy-done | bytes 524312
  7.2 0.8 %copy-done.2 = s32[2,8,4,128]{3,2,1,0:T(4,128)S(1)} copy-done((s32[2,8,4,128]{3,2,1,0:T(4,128)S(1)}, s32[2,8,4,128]{3,2,1,0:T(4,128)}, u32[]{:S(2)}) %copy-start.2) | copy-done | bytes 32792
  8.0 0.7 %copy-done.3 = s32[16,256]{1,0:T(8,128)S(1)} copy-done((s32[16,256]{1,0:T(8,128)S(1)}, s32[16,256]{1,0:T(8,128)}, u32[]{:S(2)}) %copy-start.3) | copy-done | bytes 16408
  8.7 0.7 %copy-done.4 = bf16[1,4,512]{2,1,0:T(4,128)(2,1)S(1)} copy-done((bf16[1,4,512]{2,1,0:T(4,128)(2,1)S(1)}, bf16[1,4,512]{2,1,0:T(4,128)(2,1)}, u32[]{:S(2)}) %copy-start.4) | copy-done | bytes 4120
  9.4 0.7 %copy-done.5 = f32[1,512]{1,0:T(1,128)S(1)} copy-done((f32[1,512]{1,0:T(1,128)S(1)}, f32[1,512]{1,0:T(1,128)}, u32[]{:S(2)}) %copy-start.5) | copy-done | bytes 2072
  10.1 0.7 %copy-done.6 = s32[2,8]{1,0:T(2,128)S(1)} copy-done((s32[2,8]{1,0:T(2,128)S(1)}, s32[2,8]{1,0:T(2,128)}, u32[]{:S(2)}) %copy-start.6) | copy-done | bytes 88
  10.7 0.7 %copy-done.7 = s32[2]{0:T(128)S(1)} copy-done((s32[2]{0:T(128)S(1)}, s32[2]{0:T(128)}, u32[]{:S(2)}) %copy-start.7) | copy-done | bytes 32
  11.4 3.9 %prepare.1 = (bf16[2,4,128,256]{3,2,1,0:T(8,128)(2,1)S(1)}, f32[2,512,128]{2,1,0:T(8,128)S(1)}, f32[2,8,128]{2,1,0:T(8,128)S(1)}, f32[2,4,2,128,128]{4,3,2,1,0:T...) custom-call(bf16[272,512]{1,0:T(8,128)(2,1)} %pack_rows.1.load_ref, ...), custom_call_target="tpu_custom_call" | custom-call | flops 65536 | bytes 1024 | tf_op jit(solution)/shard_map/prepare/pallas_call | solution.py:392
  15.3 0.0 collective-permute-done.refs_1_
  15.3 0.6 %collective-permute-start.2 = (bf16[272,512]{1,0:T(8,128)(2,1)S(1)}, bf16[272,512]{1,0:T(8,128)(2,1)S(1)}, u32[]{:S(2)}, u32[]{:S(2)}) collective-permute-start(bf16[272,512]{1,0:T(8,128)(2,1)S(1)} %collective-permute-done.refs_1_), channel_id=1, source_target_pairs={{0,1},{1,0},{2,3},{3,2},{4,5},{5,4},{6,7},{7,6},{8,9},{9,8},{10,11... | collective-permute-start | bytes 835592 | tf_op jit(solution)/shard_map/ppermute | solution.py:44
  15.9 1.1 %collective-permute-start.4 = (bf16[272,512]{1,0:T(8,128)(2,1)}, bf16[272,512]{1,0:T(8,128)(2,1)S(1)}, u32[]{:S(2)}, u32[]{:S(2)}) collective-permute-start(bf16[272,512]{1,0:T(8,128)(2,1)} %pack_rows.1.load_ref), channel_id=1, source_target_pairs={{0,4},{1,5},{2,0},{3,1},{6,2},{7,3},{4,6},{5,7},{8,12},{9,13},{10,... | collective-permute-start | bytes 835592 | tf_op jit(solution)/shard_map/ppermute | solution.py:40
  17.0 1.5 %collective-permute-start.3 = (bf16[272,512]{1,0:T(8,128)(2,1)S(1)}, bf16[272,512]{1,0:T(8,128)(2,1)S(1)}, u32[]{:S(2)}, u32[]{:S(2)}) collective-permute-start(bf16[272,512]{1,0:T(8,128)(2,1)S(1)} %collective-permute-done.refs_1_), channel_id=1, source_target_pairs={{0,2},{1,3},{2,6},{3,7},{6,4},{7,5},{4,0},{5,1},{8,10},{9,11},{10,... | collective-permute-start | bytes 835592 | tf_op jit(solution)/shard_map/ppermute | solution.py:40
  18.5 0.0 collective-permute-done.2.refs_2_
  18.5 3.6 %slots_0.1 = (f32[2,512,128]{2,1,0:T(8,128)S(1)}, f32[2,8,128]{2,1,0:T(8,128)S(1)}, f32[32,512]{1,0:T(8,128)S(1)}, f32[32,128]{1,0:T(8,128)S(1)}) custom-call(f32[2,4,8,128]{3,2,1,0:T(8,128)S(1)} %get-tuple-element.32.mask_ref, f32[1,512]{1,0:T(1,128)S(1)} %get-tuple-element.33.gain_ref, bf16[512,512]{1,0:T(8,128)(2,1)S(1)} %get-tuple-element.34.wk_ref, ...), custom_call_target="tpu_custom_call" | custom-call | flops 65536 | bytes 1024 | tf_op jit(solution)/shard_map/slots_0/pallas_call | solution.py:444
  22.0 5.1 %collective-permute-done.4.refs_0_ = bf16[272,512]{1,0:T(8,128)(2,1)S(1)} collective-permute-done((bf16[272,512]{1,0:T(8,128)(2,1)}, bf16[272,512]{1,0:T(8,128)(2,1)S(1)}, u32[]{:S(2)}, u32[]{:S(2)}) %collective-permute-start.4) | collective-permute-done | bytes 278560 | tf_op jit(solution)/shard_map/ppermute | solution.py:40
  27.2 5.0 %collective-permute-done.3.refs_2_ = bf16[272,512]{1,0:T(8,128)(2,1)S(1)} collective-permute-done((bf16[272,512]{1,0:T(8,128)(2,1)S(1)}, bf16[272,512]{1,0:T(8,128)(2,1)S(1)}, u32[]{:S(2)}, u32[]{:S(2)}) %collective-permute-start.3) | collective-permute-done | bytes 278560 | tf_op jit(solution)/shard_map/ppermute | solution.py:40
  32.2 3.6 %slots_last.1 = (f32[2,512,128]{2,1,0:T(8,128)S(1)}, f32[2,8,128]{2,1,0:T(8,128)S(1)}, f32[32,512]{1,0:T(8,128)S(1)}, f32[32,128]{1,0:T(8,128)S(1)}) custom-call(f32[2,4,8,128]{3,2,1,0:T(8,128)S(1)} %get-tuple-element.32.mask_ref, f32[1,512]{1,0:T(1,128)S(1)} %get-tuple-element.33.gain_ref, bf16[512,512]{1,0:T(8,128)(2,1)S(1)} %get-tuple-element.34.wk_ref, ...), custom_call_target="tpu_custom_call" | custom-call | flops 65536 | bytes 1024 | tf_op jit(solution)/shard_map/slots_last/pallas_call | solution.py:444
  35.8 3.1 %finish.1 = bf16[256,512]{1,0:T(8,128)(2,1)S(1)} custom-call(f32[2,4,8,128]{3,2,1,0:T(8,128)S(1)} %get-tuple-element.32.mask_ref, f32[1,512]{1,0:T(1,128)S(1)} %get-tuple-element.33.gain_ref, bf16[512,512]{1,0:T(8,128)(2,1)S(1)} %get-tuple-element.34.wk_ref, bf16[512,512]{1,0:T(8,128)(2,1)S(1)} %get-tuple-element.35.wvt_ref, ...), custom_call_target="tpu_custom_call" | custom-call | flops 65536 | bytes 1024 | tf_op jit(solution)/shard_map/finish/pallas_call | solution.py:482
  38.9 1.8 %collective-permute-start.7 = (bf16[1,256,512]{2,1,0:T(8,128)(2,1)S(1)}, bf16[1,256,512]{2,1,0:T(8,128)(2,1)S(1)}, u32[]{:S(2)}, u32[]{:S(2)}) collective-permute-start(bf16[1,256,512]{2,1,0:T(8,128)(2,1)S(1)} %bitcast.8), channel_id=1, source_target_pairs={{0,8},{8,16},{16,24},{24,0},{1,9},{9,17},{17,25},{25,1},{2,10},{10... | collective-permute-start | bytes 786440 | tf_op jit(solution)/shard_map/ppermute | solution.py:49
  40.7 7.9 %collective-permute-done.7 = bf16[1,256,512]{2,1,0:T(8,128)(2,1)S(1)} collective-permute-done((bf16[1,256,512]{2,1,0:T(8,128)(2,1)S(1)}, bf16[1,256,512]{2,1,0:T(8,128)(2,1)S(1)}, u32[]{:S(2)}, u32[]{:S(2)}) %collective-permute-start.7) | collective-permute-done | bytes 262176 | tf_op jit(solution)/shard_map/ppermute | solution.py:49
  48.7 0.7 %copy.12 = bf16[1,256,512]{2,1,0:T(8,128)(2,1)} copy(bf16[1,256,512]{2,1,0:T(8,128)(2,1)S(1)} %collective-permute-done.7) | data formatting | bytes 524288
  (14 shorter events, 0.0 us)
Async XLA Ops:
  1.7 13.6 %collective-permute-start = (bf16[272,512]{1,0:T(8,128)(2,1)}, bf16[272,512]{1,0:T(8,128)(2,1)S(1)}, u32[]{:S(2)}, u32[]{:S(2)}) collective-permute-start(bf16[272,512]{1,0:T(8,128)(2,1)} %pack_rows.1.load_ref), channel_id=1, source_target_pairs={{0,2},{1,3},{2,6},{3,7},{6,4},{7,5},{4,0},{5,1},{8,10},{9,11},{10,... | collective-permute-start | bytes 835592 | tf_op jit(solution)/shard_map/ppermute | solution.py:40
  4.8 13.7 %collective-permute-start.1 = (bf16[272,512]{1,0:T(8,128)(2,1)}, bf16[272,512]{1,0:T(8,128)(2,1)S(1)}, u32[]{:S(2)}, u32[]{:S(2)}) collective-permute-start(bf16[272,512]{1,0:T(8,128)(2,1)} %pack_rows.1.load_ref), channel_id=1, source_target_pairs={{0,1},{1,0},{2,3},{3,2},{4,5},{5,4},{6,7},{7,6},{8,9},{9,8},{10,11... | collective-permute-start | bytes 835592 | tf_op jit(solution)/shard_map/ppermute | solution.py:44
  4.8 1.4 %copy-start = (bf16[1,512,1536]{2,1,0:T(8,128)(2,1)S(1)}, bf16[1,512,1536]{2,1,0:T(8,128)(2,1)}, u32[]{:S(2)}) copy-start(bf16[1,512,1536]{2,1,0:T(8,128)(2,1)} %param.12) | copy-start | bytes 4718596
  6.2 1.0 %copy-start.1 = (bf16[1,512,512]{2,1,0:T(8,128)(2,1)S(1)}, bf16[1,512,512]{2,1,0:T(8,128)(2,1)}, u32[]{:S(2)}) copy-start(bf16[1,512,512]{2,1,0:T(8,128)(2,1)} %param.13) | copy-start | bytes 1572868
  7.2 0.8 %copy-start.2 = (s32[2,8,4,128]{3,2,1,0:T(4,128)S(1)}, s32[2,8,4,128]{3,2,1,0:T(4,128)}, u32[]{:S(2)}) copy-start(s32[2,8,4,128]{3,2,1,0:T(4,128)} %srows_hbm.1) | copy-start | bytes 98308
  8.0 0.7 %copy-start.3 = (s32[16,256]{1,0:T(8,128)S(1)}, s32[16,256]{1,0:T(8,128)}, u32[]{:S(2)}) copy-start(s32[16,256]{1,0:T(8,128)} %lrows_hbm.1) | copy-start | bytes 49156
  8.7 0.7 %copy-start.4 = (bf16[1,4,512]{2,1,0:T(4,128)(2,1)S(1)}, bf16[1,4,512]{2,1,0:T(4,128)(2,1)}, u32[]{:S(2)}) copy-start(bf16[1,4,512]{2,1,0:T(4,128)(2,1)} %param.14) | copy-start | bytes 12292
  9.4 0.7 %copy-start.5 = (f32[1,512]{1,0:T(1,128)S(1)}, f32[1,512]{1,0:T(1,128)}, u32[]{:S(2)}) copy-start(f32[1,512]{1,0:T(1,128)} %gain_hbm.1) | copy-start | bytes 6148
  10.1 0.7 %copy-start.6 = (s32[2,8]{1,0:T(2,128)S(1)}, s32[2,8]{1,0:T(2,128)}, u32[]{:S(2)}) copy-start(s32[2,8]{1,0:T(2,128)} %sblock_hbm.1) | copy-start | bytes 196
  10.7 0.7 %copy-start.7 = (s32[2]{0:T(128)S(1)}, s32[2]{0:T(128)}, u32[]{:S(2)}) copy-start(s32[2]{0:T(128)} %scount_hbm.1) | copy-start | bytes 28
  15.3 3.2 %collective-permute-start.2 = (bf16[272,512]{1,0:T(8,128)(2,1)S(1)}, bf16[272,512]{1,0:T(8,128)(2,1)S(1)}, u32[]{:S(2)}, u32[]{:S(2)}) collective-permute-start(bf16[272,512]{1,0:T(8,128)(2,1)S(1)} %collective-permute-done.refs_1_), channel_id=1, source_target_pairs={{0,1},{1,0},{2,3},{3,2},{4,5},{5,4},{6,7},{7,6},{8,9},{9,8},{10,11... | collective-permute-start | bytes 835592 | tf_op jit(solution)/shard_map/ppermute | solution.py:44
  15.9 11.3 %collective-permute-start.4 = (bf16[272,512]{1,0:T(8,128)(2,1)}, bf16[272,512]{1,0:T(8,128)(2,1)S(1)}, u32[]{:S(2)}, u32[]{:S(2)}) collective-permute-start(bf16[272,512]{1,0:T(8,128)(2,1)} %pack_rows.1.load_ref), channel_id=1, source_target_pairs={{0,4},{1,5},{2,0},{3,1},{6,2},{7,3},{4,6},{5,7},{8,12},{9,13},{10,... | collective-permute-start | bytes 835592 | tf_op jit(solution)/shard_map/ppermute | solution.py:40
  17.0 15.3 %collective-permute-start.3 = (bf16[272,512]{1,0:T(8,128)(2,1)S(1)}, bf16[272,512]{1,0:T(8,128)(2,1)S(1)}, u32[]{:S(2)}, u32[]{:S(2)}) collective-permute-start(bf16[272,512]{1,0:T(8,128)(2,1)S(1)} %collective-permute-done.refs_1_), channel_id=1, source_target_pairs={{0,2},{1,3},{2,6},{3,7},{6,4},{7,5},{4,0},{5,1},{8,10},{9,11},{10,... | collective-permute-start | bytes 835592 | tf_op jit(solution)/shard_map/ppermute | solution.py:40
  27.2 5.1 %collective-permute-start.5 = (bf16[272,512]{1,0:T(8,128)(2,1)S(1)}, bf16[272,512]{1,0:T(8,128)(2,1)S(1)}, u32[]{:S(2)}, u32[]{:S(2)}) collective-permute-start(bf16[272,512]{1,0:T(8,128)(2,1)S(1)} %collective-permute-done.4.refs_0_), channel_id=1, source_target_pairs={{0,1},{1,0},{2,3},{3,2},{4,5},{5,4},{6,7},{7,6},{8,9},{9,8},{10,11... | collective-permute-start | bytes 835592 | tf_op jit(solution)/shard_map/ppermute | solution.py:44
  32.2 3.6 %collective-permute-start.6 = (bf16[272,512]{1,0:T(8,128)(2,1)S(1)}, bf16[272,512]{1,0:T(8,128)(2,1)S(1)}, u32[]{:S(2)}, u32[]{:S(2)}) collective-permute-start(bf16[272,512]{1,0:T(8,128)(2,1)S(1)} %collective-permute-done.3.refs_2_), channel_id=1, source_target_pairs={{0,1},{1,0},{2,3},{3,2},{4,5},{5,4},{6,7},{7,6},{8,9},{9,8},{10,11... | collective-permute-start | bytes 835592 | tf_op jit(solution)/shard_map/ppermute | solution.py:44
  38.9 9.7 %collective-permute-start.7 = (bf16[1,256,512]{2,1,0:T(8,128)(2,1)S(1)}, bf16[1,256,512]{2,1,0:T(8,128)(2,1)S(1)}, u32[]{:S(2)}, u32[]{:S(2)}) collective-permute-start(bf16[1,256,512]{2,1,0:T(8,128)(2,1)S(1)} %bitcast.8), channel_id=1, source_target_pairs={{0,8},{8,16},{16,24},{24,0},{1,9},{9,17},{17,25},{25,1},{2,10},{10... | collective-permute-start | bytes 786440 | tf_op jit(solution)/shard_map/ppermute | solution.py:49

commit v2 on v1

--- a/solution.py
+++ b/solution.py
@@ -13,8 +13,6 @@
 CAP_LIMIT = 10.0
 LOG2E = 1.4426950408889634
 EXTRA = 16
-PACK_MIB = 60
-PREP_MIB = 32
 F32 = jnp.float32
 BF16 = jnp.bfloat16
 HBM = pl.BlockSpec(memory_space=pltpu.HBM)
@@ -116,16 +114,6 @@
     for copy in copies:
         copy.start()
     return copies
-
-
-def pack_kernel(x_hbm, vid_hbm, load_ref, vid_ref, sems):
-    rows = vid_ref.shape[1]
-    copies = start_copies([(x_hbm, load_ref.at[:rows, :]), (vid_hbm, vid_ref)], sems)
-    copies[1].wait()
-    tile = jnp.broadcast_to(vid_ref[...].astype(F32), (EXTRA, rows))
-    rest = jnp.zeros((EXTRA, load_ref.shape[1] - rows), F32)
-    load_ref[rows:, :] = jnp.concatenate([tile, rest], axis=1).astype(BF16)
-    copies[0].wait()
 
 
 def vid_row(load_ref, rows):
@@ -367,16 +355,8 @@
     after = lax.optimization_barrier
     unit = 2**16
 
-    load = pl.pallas_call(
-        pack_kernel,
-        out_shape=shape((rows + EXTRA, width), BF16),
-        in_specs=[HBM] * 2,
-        out_specs=VMEM,
-        scratch_shapes=[pltpu.VMEM((1, rows), jnp.int32), pltpu.SemaphoreType.DMA((2,))],
-        compiler_params=params(PACK_MIB),
-        cost_estimate=cost(unit),
-        name="pack_rows",
-    )(activations[0], virtual_id.reshape(1, rows))
+    ids = jnp.pad(virtual_id.reshape(1, rows).astype(BF16), ((0, EXTRA - 1), (0, width - rows)))
+    load = jnp.concatenate([activations[0], ids], axis=0)
     near = {1: to_next_chip(load, devices, 1)}
     if chips > 2:
         near[chips - 1] = to_next_chip(load, devices, -1)
@@ -419,12 +399,18 @@
             pltpu.SMEM((devices,), jnp.int32),
             pltpu.SemaphoreType.DMA((10,)),
         ],
-        compiler_params=params(PREP_MIB),
+        compiler_params=params(32),
         cost_estimate=cost(unit),
         name="prepare",
     )(
-        load, norm_gain, project_in[0], virtual_keys[0], local_rows, slot_rows, slot_block,
-        slot_count, project_out[0],
+        load,
+        *[
+            pltpu.with_memory_space_constraint(value, pltpu.HBM)
+            for value in (
+                norm_gain, project_in[0], virtual_keys[0], local_rows, slot_rows, slot_block,
+                slot_count, project_out[0],
+            )
+        ],
     )
 
     def work(count):
@@ -463,20 +449,24 @@
             order.append((chips - s, -1))
     waiting = [(1, 0)]
     for i, (step, way) in enumerate(order):
-        if step not in far:
+        if i == 0:
+            ready = [near[other] for other, _ in order[:2]]
+            *ready, first = after((*ready, sums[1]))
+            near.update({other: value for (other, _), value in zip(order, ready)})
+            sums = (sums[0], first) + sums[2:]
+        elif i > 1:
             sums = arrive(step, sums)
-            nexts = step + way
-            if nexts not in near and (nexts, way) in order:
-                near[nexts] = to_next_chip(near[step], devices, way)
-            far[step] = swapped(near[step], devices, 1)
+        nexts = step + way
+        if nexts not in near and (nexts, way) in order:
+            near[nexts] = to_next_chip(near[step], devices, way)
+        far[step] = swapped(near[step], devices, 1)
         waiting.append((0, step))
         if i == len(order) - 1:
             break
         waiting.append((1, step))
-        if i == len(order) - 2:
-            continue
-        sums = slots_call(waiting, sums, "slots_%d" % i)
-        waiting = []
+        if i > 0:
+            sums = slots_call(waiting, sums, "slots_%d" % i)
+            waiting = []
     sums = slots_call(waiting, sums, "slots_last")
     names = ((1, order[-1][0]),)
     updated = pl.pallas_call(

time: 49.9 us -> 42.7 us (0.86)
  local copies, waits for them, and re-layouts: 7.33 us -> 0.7 us
  Pallas kernels: 15.8 us -> 12.7 us
  other arithmetic: 0 us -> 1.65 us
  waiting for transfers between devices: 18.1 us -> 19.5 us
    unnamed x17 -> x1, local copies, waits for them, and re-layouts: 7.33 us -> 0.7 us
    pallas_call x1 -> x0, Pallas kernels: 1.67 us -> none  [body(): pl.pallas_call(pack_kernel, out_shape=shape((rows + EXTRA, width), BF16),...]
    ppermute x3, waiting for transfers between devices: 10.2 us -> 11.4 us  [to_next_chip(): return lax.ppermute(value, 'node', pairs)]
    pallas_call x1, Pallas kernels: 3.13 us -> 2.14 us  [body(): pl.pallas_call(functools.partial(finish_kernel, names), out_shape=shape((...]
    concatenate x0 -> x1, other arithmetic: none -> 0.97 us  [body(): load = jnp.concatenate([activations[0], ids], axis=0)]
    convert_element_type x0 -> x1, other arithmetic: none -> 0.68 us  [body(): virtual_id.reshape(1, rows).astype(BF16)]
    pallas_call x2, Pallas kernels: 7.12 us -> 6.55 us  [slots_call(): pl.pallas_call(functools.partial(slots_kernel, tuple(names)), out_shape=a...]
  transfers between devices with their start and end apart: 8 -> 8, of which waited for: 3 -> 4; matrix products, arithmetic and copies ran while one was open for 0% -> 0% of each run, Pallas kernels for 22% -> 25%
where the time goes in v2:
time: 42.7 us; the launch traced here: 42.6 us
  waiting for transfers between devices  19.5 us (46%)
  Pallas kernels  12.7 us (30%)
  starting transfers between devices  8.01 us (19%)
  other arithmetic  1.65 us (4%)
  local copies, waits for them, and re-layouts  0.7 us (2%)
    ppermute x3, waiting for transfers between devices, to_next_chip(): return lax.ppermute(value, 'node', pairs)  11.4 us
    ppermute x1, waiting for transfers between devices, to_next_segment(): lax.ppermute(value, 'segment', [(s, (s + 1) % count) for s in range(count)])  8.07 us
    pallas_call x2, Pallas kernels, slots_call(): pl.pallas_call(functools.partial(slots_kernel, tuple(names)), out_shape=a...  6.55 us
    ppermute x3, starting transfers between devices, to_next_chip(): return lax.ppermute(value, 'node', pairs)  5.89 us
    pallas_call x1, Pallas kernels, body(): pl.pallas_call(prep_kernel, out_shape=(shape((blocks, pairs, wide, 2 * br...  3.97 us
    pallas_call x1, Pallas kernels, body(): pl.pallas_call(functools.partial(finish_kernel, names), out_shape=shape((...  2.14 us
    ppermute x1, starting transfers between devices, to_next_segment(): lax.ppermute(value, 'segment', [(s, (s + 1) % count) for s in range(count)])  1.6 us
    concatenate x1, other arithmetic, body(): load = jnp.concatenate([activations[0], ids], axis=0)  0.97 us
  transfers between devices with their start and end apart: 8, of which 4 were waited for; matrix products, arithmetic and copies ran while one was open for 0% of the time, Pallas kernels for 25%

profile of v2, /device:TPU:0, one launch (start us, length us, event | category | flops | bytes accessed | tf_op | source)
XLA Modules:
  0.0 42.6 jit_solution(18322627970189118267)
XLA Ops:
  0.0 0.7 %convert_bitcast_fusion = bf16[1,256]{1,0:T(2,128)(2,1)S(1)} fusion(s32[256,1]{0,1:T(1,128)} %param.15), kind=kLoop, calls=%fused_computation.3 | loop fusion | flops 256 | bytes 1536 | tf_op jit(solution)/shard_map/convert_element_type | solution.py:358
  0.7 1.0 %fusion.1.load_ref = bf16[272,512]{1,0:T(8,128)(2,1)S(1)} fusion(bf16[1,256]{1,0:T(2,128)(2,1)S(1)} %convert_bitcast_fusion, bf16[256,512]{1,0:T(8,128)(2,1)} %bitcast.10), kind=kLoop, calls=%fused_computation.2 | loop fusion | flops 835584 | bytes 541184 | tf_op jit(solution)/shard_map/concatenate | solution.py:359
  1.7 3.1 %collective-permute-start = (bf16[272,512]{1,0:T(8,128)(2,1)S(1)}, bf16[272,512]{1,0:T(8,128)(2,1)S(1)}, u32[]{:S(2)}, u32[]{:S(2)}) collective-permute-start(bf16[272,512]{1,0:T(8,128)(2,1)S(1)} %fusion.1.load_ref), channel_id=1, source_target_pairs={{0,2},{1,3},{2,6},{3,7},{6,4},{7,5},{4,0},{5,1},{8,10},{9,11},{10,... | collective-permute-start | bytes 835592 | tf_op jit(solution)/shard_map/ppermute | solution.py:38
  4.7 1.1 %collective-permute-start.1 = (bf16[272,512]{1,0:T(8,128)(2,1)S(1)}, bf16[272,512]{1,0:T(8,128)(2,1)S(1)}, u32[]{:S(2)}, u32[]{:S(2)}) collective-permute-start(bf16[272,512]{1,0:T(8,128)(2,1)S(1)} %fusion.1.load_ref), channel_id=1, source_target_pairs={{0,4},{1,5},{2,0},{3,1},{6,2},{7,3},{4,6},{5,7},{8,12},{9,13},{10,... | collective-permute-start | bytes 835592 | tf_op jit(solution)/shard_map/ppermute | solution.py:38
  5.8 0.0 collective-permute-start.2
  5.8 4.0 %prepare.1 = (bf16[2,4,128,256]{3,2,1,0:T(8,128)(2,1)S(1)}, f32[2,512,128]{2,1,0:T(8,128)S(1)}, f32[2,8,128]{2,1,0:T(8,128)S(1)}, f32[2,4,2,128,128]{4,3,2,1,0:T...) custom-call(bf16[272,512]{1,0:T(8,128)(2,1)S(1)} %fusion.1.load_ref,, ...), custom_call_target="tpu_custom_call" | custom-call | flops 65536 | bytes 1024 | tf_op jit(solution)/shard_map/prepare/pallas_call | solution.py:372
  9.8 2.7 %collective-permute-done.refs_1_ = bf16[272,512]{1,0:T(8,128)(2,1)S(1)} collective-permute-done((bf16[272,512]{1,0:T(8,128)(2,1)S(1)}, bf16[272,512]{1,0:T(8,128)(2,1)S(1)}, u32[]{:S(2)}, u32[]{:S(2)}) %collective-permute-start) | collective-permute-done | bytes 278560 | tf_op jit(solution)/shard_map/ppermute | solution.py:38
  12.5 5.9 %collective-permute-done.1.refs_3_ = bf16[272,512]{1,0:T(8,128)(2,1)S(1)} collective-permute-done((bf16[272,512]{1,0:T(8,128)(2,1)S(1)}, bf16[272,512]{1,0:T(8,128)(2,1)S(1)}, u32[]{:S(2)}, u32[]{:S(2)}) %collective-permute-start.1) | collective-permute-done | bytes 278560 | tf_op jit(solution)/shard_map/ppermute | solution.py:38
  18.4 0.0 collective-permute-start.3
  18.4 0.5 %collective-permute-start.4 = (bf16[272,512]{1,0:T(8,128)(2,1)S(1)}, bf16[272,512]{1,0:T(8,128)(2,1)S(1)}, u32[]{:S(2)}, u32[]{:S(2)}) collective-permute-start(bf16[272,512]{1,0:T(8,128)(2,1)S(1)} %collective-permute-done.1.refs_3_), channel_id=1, source_target_pairs={{0,1},{1,0},{2,3},{3,2},{4,5},{5,4},{6,7},{7,6},{8,9},{9,8},{10,11... | collective-permute-start | bytes 835592 | tf_op jit(solution)/shard_map/ppermute | solution.py:42
  18.9 1.7 %collective-permute-start.5 = (bf16[272,512]{1,0:T(8,128)(2,1)S(1)}, bf16[272,512]{1,0:T(8,128)(2,1)S(1)}, u32[]{:S(2)}, u32[]{:S(2)}) collective-permute-start(bf16[272,512]{1,0:T(8,128)(2,1)S(1)} %collective-permute-done.refs_1_), channel_id=1, source_target_pairs={{0,2},{1,3},{2,6},{3,7},{6,4},{7,5},{4,0},{5,1},{8,10},{9,11},{10,... | collective-permute-start | bytes 835592 | tf_op jit(solution)/shard_map/ppermute | solution.py:38
  20.6 0.0 collective-permute-done.2.refs_0_
  20.6 0.0 collective-permute-done.3.refs_2_
  20.6 0.0 collective-permute-done.4.refs_4_
  20.6 4.9 %slots_1.1 = (f32[2,512,128]{2,1,0:T(8,128)S(1)}, f32[2,8,128]{2,1,0:T(8,128)S(1)}, f32[32,512]{1,0:T(8,128)S(1)}, f32[32,128]{1,0:T(8,128)S(1)}) custom-call(f32[2,4,8,128]{3,2,1,0:T(8,128)S(1)} %get-tuple-element.31.mask_ref, f32[1,512]{1,0:T(1,128)S(1)} %get-tuple-element.32.gain_ref, bf16[512,512]{1,0:T(8,128)(2,1)S(1)} %get-tuple-element.33.wk_ref, ...), custom_call_target="tpu_custom_call" | custom-call | flops 65536 | bytes 1024 | tf_op jit(solution)/shard_map/slots_1/pallas_call | solution.py:430
  25.5 2.8 %collective-permute-done.5.refs_0_ = bf16[272,512]{1,0:T(8,128)(2,1)S(1)} collective-permute-done((bf16[272,512]{1,0:T(8,128)(2,1)S(1)}, bf16[272,512]{1,0:T(8,128)(2,1)S(1)}, u32[]{:S(2)}, u32[]{:S(2)}) %collective-permute-start.5) | collective-permute-done | bytes 278560 | tf_op jit(solution)/shard_map/ppermute | solution.py:38
  28.4 0.0 collective-permute-start.6
  28.4 1.7 %slots_last.1 = (f32[2,512,128]{2,1,0:T(8,128)S(1)}, f32[2,8,128]{2,1,0:T(8,128)S(1)}, f32[32,512]{1,0:T(8,128)S(1)}, f32[32,128]{1,0:T(8,128)S(1)}) custom-call(f32[2,4,8,128]{3,2,1,0:T(8,128)S(1)} %get-tuple-element.31.mask_ref, f32[1,512]{1,0:T(1,128)S(1)} %get-tuple-element.32.gain_ref, bf16[512,512]{1,0:T(8,128)(2,1)S(1)} %get-tuple-element.33.wk_ref, ...), custom_call_target="tpu_custom_call" | custom-call | flops 65536 | bytes 1024 | tf_op jit(solution)/shard_map/slots_last/pallas_call | solution.py:430
  30.0 0.0 collective-permute-done.6.last_ref
  30.0 2.1 %finish.1 = bf16[256,512]{1,0:T(8,128)(2,1)S(1)} custom-call(f32[2,4,8,128]{3,2,1,0:T(8,128)S(1)} %get-tuple-element.31.mask_ref, f32[1,512]{1,0:T(1,128)S(1)} %get-tuple-element.32.gain_ref, bf16[512,512]{1,0:T(8,128)(2,1)S(1)} %get-tuple-element.33.wk_ref, bf16[512,512]{1,0:T(8,128)(2,1)S(1)} %get-tuple-element.34.wvt_ref, ...), custom_call_target="tpu_custom_call" | custom-call | flops 65536 | bytes 1024 | tf_op jit(solution)/shard_map/finish/pallas_call | solution.py:472
  32.2 1.6 %collective-permute-start.7 = (bf16[1,256,512]{2,1,0:T(8,128)(2,1)S(1)}, bf16[1,256,512]{2,1,0:T(8,128)(2,1)S(1)}, u32[]{:S(2)}, u32[]{:S(2)}) collective-permute-start(bf16[1,256,512]{2,1,0:T(8,128)(2,1)S(1)} %bitcast.7), channel_id=1, source_target_pairs={{0,8},{8,16},{16,24},{24,0},{1,9},{9,17},{17,25},{25,1},{2,10},{10... | collective-permute-start | bytes 786440 | tf_op jit(solution)/shard_map/ppermute | solution.py:47
  33.8 8.1 %collective-permute-done.7 = bf16[1,256,512]{2,1,0:T(8,128)(2,1)S(1)} collective-permute-done((bf16[1,256,512]{2,1,0:T(8,128)(2,1)S(1)}, bf16[1,256,512]{2,1,0:T(8,128)(2,1)S(1)}, u32[]{:S(2)}, u32[]{:S(2)}) %collective-permute-start.7) | collective-permute-done | bytes 262176 | tf_op jit(solution)/shard_map/ppermute | solution.py:47
  41.9 0.7 %copy.12 = bf16[1,256,512]{2,1,0:T(8,128)(2,1)} copy(bf16[1,256,512]{2,1,0:T(8,128)(2,1)S(1)} %collective-permute-done.7) | data formatting | bytes 524288
Async XLA Ops:
  1.7 10.8 %collective-permute-start = (bf16[272,512]{1,0:T(8,128)(2,1)S(1)}, bf16[272,512]{1,0:T(8,128)(2,1)S(1)}, u32[]{:S(2)}, u32[]{:S(2)}) collective-permute-start(bf16[272,512]{1,0:T(8,128)(2,1)S(1)} %fusion.1.load_ref), channel_id=1, source_target_pairs={{0,2},{1,3},{2,6},{3,7},{6,4},{7,5},{4,0},{5,1},{8,10},{9,11},{10,... | collective-permute-start | bytes 835592 | tf_op jit(solution)/shard_map/ppermute | solution.py:38
  4.7 13.6 %collective-permute-start.1 = (bf16[272,512]{1,0:T(8,128)(2,1)S(1)}, bf16[272,512]{1,0:T(8,128)(2,1)S(1)}, u32[]{:S(2)}, u32[]{:S(2)}) collective-permute-start(bf16[272,512]{1,0:T(8,128)(2,1)S(1)} %fusion.1.load_ref), channel_id=1, source_target_pairs={{0,4},{1,5},{2,0},{3,1},{6,2},{7,3},{4,6},{5,7},{8,12},{9,13},{10,... | collective-permute-start | bytes 835592 | tf_op jit(solution)/shard_map/ppermute | solution.py:38
  5.8 14.8 %collective-permute-start.2 = (bf16[272,512]{1,0:T(8,128)(2,1)S(1)}, bf16[272,512]{1,0:T(8,128)(2,1)S(1)}, u32[]{:S(2)}, u32[]{:S(2)}) collective-permute-start(bf16[272,512]{1,0:T(8,128)(2,1)S(1)} %fusion.1.load_ref), channel_id=1, source_target_pairs={{0,1},{1,0},{2,3},{3,2},{4,5},{5,4},{6,7},{7,6},{8,9},{9,8},{10,11... | collective-permute-start | bytes 835592 | tf_op jit(solution)/shard_map/ppermute | solution.py:42
  18.4 2.3 %collective-permute-start.3 = (bf16[272,512]{1,0:T(8,128)(2,1)S(1)}, bf16[272,512]{1,0:T(8,128)(2,1)S(1)}, u32[]{:S(2)}, u32[]{:S(2)}) collective-permute-start(bf16[272,512]{1,0:T(8,128)(2,1)S(1)} %collective-permute-done.refs_1_), channel_id=1, source_target_pairs={{0,1},{1,0},{2,3},{3,2},{4,5},{5,4},{6,7},{7,6},{8,9},{9,8},{10,11... | collective-permute-start | bytes 835592 | tf_op jit(solution)/shard_map/ppermute | solution.py:42
  18.4 2.2 %collective-permute-start.4 = (bf16[272,512]{1,0:T(8,128)(2,1)S(1)}, bf16[272,512]{1,0:T(8,128)(2,1)S(1)}, u32[]{:S(2)}, u32[]{:S(2)}) collective-permute-start(bf16[272,512]{1,0:T(8,128)(2,1)S(1)} %collective-permute-done.1.refs_3_), channel_id=1, source_target_pairs={{0,1},{1,0},{2,3},{3,2},{4,5},{5,4},{6,7},{7,6},{8,9},{9,8},{10,11... | collective-permute-start | bytes 835592 | tf_op jit(solution)/shard_map/ppermute | solution.py:42
  18.9 9.5 %collective-permute-start.5 = (bf16[272,512]{1,0:T(8,128)(2,1)S(1)}, bf16[272,512]{1,0:T(8,128)(2,1)S(1)}, u32[]{:S(2)}, u32[]{:S(2)}) collective-permute-start(bf16[272,512]{1,0:T(8,128)(2,1)S(1)} %collective-permute-done.refs_1_), channel_id=1, source_target_pairs={{0,2},{1,3},{2,6},{3,7},{6,4},{7,5},{4,0},{5,1},{8,10},{9,11},{10,... | collective-permute-start | bytes 835592 | tf_op jit(solution)/shard_map/ppermute | solution.py:38
  28.4 1.7 %collective-permute-start.6 = (bf16[272,512]{1,0:T(8,128)(2,1)S(1)}, bf16[272,512]{1,0:T(8,128)(2,1)S(1)}, u32[]{:S(2)}, u32[]{:S(2)}) collective-permute-start(bf16[272,512]{1,0:T(8,128)(2,1)S(1)} %collective-permute-done.5.refs_0_), channel_id=1, source_target_pairs={{0,1},{1,0},{2,3},{3,2},{4,5},{5,4},{6,7},{7,6},{8,9},{9,8},{10,11... | collective-permute-start | bytes 835592 | tf_op jit(solution)/shard_map/ppermute | solution.py:42
  32.2 9.7 %collective-permute-start.7 = (bf16[1,256,512]{2,1,0:T(8,128)(2,1)S(1)}, bf16[1,256,512]{2,1,0:T(8,128)(2,1)S(1)}, u32[]{:S(2)}, u32[]{:S(2)}) collective-permute-start(bf16[1,256,512]{2,1,0:T(8,128)(2,1)S(1)} %bitcast.7), channel_id=1, source_target_pairs={{0,8},{8,16},{16,24},{24,0},{1,9},{9,17},{17,25},{25,1},{2,10},{10... | collective-permute-start | bytes 786440 | tf_op jit(solution)/shard_map/ppermute | solution.py:47

commit v3 on v2

--- a/solution.py
+++ b/solution.py
@@ -42,6 +42,10 @@
     return lax.ppermute(value, "node", [(d, d ^ distance) for d in range(devices)])
 
 
+def swapped_parts(value, devices, cut):
+    return [swapped(value[:cut], devices, 1), swapped(value[cut:], devices, 1)]
+
+
 def to_next_segment(value):
     count = lax.axis_size("segment")
     return lax.ppermute(value, "segment", [(s, (s + 1) % count) for s in range(count)])
@@ -117,7 +121,21 @@
 
 
 def vid_row(load_ref, rows):
-    return load_ref[rows:, :rows].astype(F32)[:1, :]
+    last = load_ref.shape[0]
+    return load_ref[last - EXTRA :, :rows].astype(F32)[:1, :]
+
+
+def load_rows(refs):
+    last = refs[-1].shape[0] - EXTRA
+    return jnp.concatenate([ref[...] for ref in refs[:-1]] + [refs[-1][:last, :]], axis=0)
+
+
+def grouped(refs, sizes):
+    groups = []
+    for size in sizes:
+        groups.append(refs[:size])
+        refs = refs[size:]
+    return groups
 
 
 def attend(keys, values, counts, qbd, scale):
@@ -234,15 +252,15 @@
     names, loads, mask_ref, gain_ref, wk_ref, wvt_ref, vkw_ref,
     normed_ref, k_ref, vt_ref, pool_ref, weight_ref,
 ):
-    rows = loads[0].shape[0] - EXTRA
     width = k_ref.shape[1]
     chosen = []
     vids = []
-    for i, ((far, step), load_ref) in enumerate(zip(names, loads)):
-        part = norm_rows(load_ref[:rows, :], gain_ref[...])
+    for i, ((far, step), pieces) in enumerate(zip(names, loads)):
+        part = norm_rows(load_rows(pieces), gain_ref[...])
+        rows = part.shape[0]
         normed_ref[i * rows : (i + 1) * rows, :] = part
         chosen.append(choose(mask_ref[far, step, :1, :], part))
-        vids.append(vid_row(load_ref, rows))
+        vids.append(vid_row(pieces[-1], rows))
     picked = jnp.concatenate(chosen, axis=0)
     k_ref[...] = mm(picked, wk_ref[...]).astype(BF16)
     vt_ref[...] = mm_nt(wvt_ref[...], picked).astype(BF16)
@@ -265,11 +283,11 @@
 
 
 def slots_kernel(
-    names, mask_ref, gain_ref, wk_ref, wvt_ref, vkw_ref, counts_ref, qbd_ref,
+    names, sizes, mask_ref, gain_ref, wk_ref, wvt_ref, vkw_ref, counts_ref, qbd_ref,
     num_in, den_in, pool_in, weight_in, *refs
 ):
-    loads = refs[: len(names)]
-    num_ref, den_ref, pool_ref, weight_ref, normed_ref, k_ref, vt_ref = refs[len(names) :]
+    loads = grouped(refs, sizes)
+    num_ref, den_ref, pool_ref, weight_ref, normed_ref, k_ref, vt_ref = refs[sum(sizes) :]
     num_ref[...] = num_in[...]
     den_ref[...] = den_in[...]
     pool_ref[...] = pool_in[...]
@@ -288,7 +306,7 @@
     out_ref, num_ref, den_ref, pool_ref, weight_ref, normed_ref, k_ref, vt_ref,
 ):
     slots_kernel(
-        names, mask_ref, gain_ref, wk_ref, wvt_ref, vkw_ref, counts_ref, qbd_ref,
+        names, (1,), mask_ref, gain_ref, wk_ref, wvt_ref, vkw_ref, counts_ref, qbd_ref,
         num_in, den_in, pool_in, weight_in, last_ref,
         num_ref, den_ref, pool_ref, weight_ref, normed_ref, k_ref, vt_ref,
     )
@@ -355,12 +373,13 @@
     after = lax.optimization_barrier
     unit = 2**16
 
-    ids = jnp.pad(virtual_id.reshape(1, rows).astype(BF16), ((0, EXTRA - 1), (0, width - rows)))
+    ids = after(virtual_id.reshape(1, rows))
+    ids = jnp.pad(ids.astype(BF16), ((0, EXTRA - 1), (0, width - rows)))
     load = jnp.concatenate([activations[0], ids], axis=0)
     near = {1: to_next_chip(load, devices, 1)}
     if chips > 2:
         near[chips - 1] = to_next_chip(load, devices, -1)
-    far = {0: swapped(load, devices, 1)}
+    far = {0: swapped_parts(load, devices, br)}
 
     accumulators = (
         shape((blocks, width, br), F32),
@@ -427,10 +446,13 @@
         return (sums[0], first) + sums[2:]
 
     def slots_call(names, sums, name):
+        loads = [(far if other else near)[step] for other, step in names]
+        loads = [load if isinstance(load, list) else [load] for load in loads]
+        sizes = tuple(len(load) for load in loads)
         return pl.pallas_call(
-            functools.partial(slots_kernel, tuple(names)),
+            functools.partial(slots_kernel, tuple(names), sizes),
             out_shape=accumulators,
-            in_specs=[VMEM] * (11 + len(names)),
+            in_specs=[VMEM] * (11 + sum(sizes)),
             out_specs=[VMEM] * 4,
             scratch_shapes=work(len(names)),
             compiler_params=params(40),
@@ -438,7 +460,7 @@
             name=name,
         )(
             mask, gain, wk, wvt, vkw, counts, qbd, *sums,
-            *[(far if other else near)[step] for other, step in names],
+            *[piece for load in loads for piece in load],
         )
 
     ahead = chips // 2
@@ -449,22 +471,19 @@
             order.append((chips - s, -1))
     waiting = [(1, 0)]
     for i, (step, way) in enumerate(order):
-        if i == 0:
-            ready = [near[other] for other, _ in order[:2]]
-            *ready, first = after((*ready, sums[1]))
-            near.update({other: value for (other, _), value in zip(order, ready)})
-            sums = (sums[0], first) + sums[2:]
-        elif i > 1:
-            sums = arrive(step, sums)
+        sums = arrive(step, sums)
         nexts = step + way
         if nexts not in near and (nexts, way) in order:
             near[nexts] = to_next_chip(near[step], devices, way)
-        far[step] = swapped(near[step], devices, 1)
+        if i == len(order) - 1:
+            far[step] = swapped(near[step], devices, 1)
+        else:
+            far[step] = swapped_parts(near[step], devices, br)
         waiting.append((0, step))
         if i == len(order) - 1:
             break
         waiting.append((1, step))
-        if i > 0:
+        if i < len(order) - 1:
             sums = slots_call(waiting, sums, "slots_%d" % i)
             waiting = []
     sums = slots_call(waiting, sums, "slots_last")

time: 42.7 us -> 42.7 us (level); the launches traced: 42.6 us -> 42.1 us
  waiting for transfers between devices: 19.5 us -> 9.92 us
  starting transfers between devices: 8.01 us -> 14.8 us
  Pallas kernels: 12.7 us -> 14 us
  local copies, waits for them, and re-layouts: 0.7 us -> 1.67 us
    ppermute x3, waiting for transfers between devices: 11.4 us -> 1.15 us  [to_next_chip(): return lax.ppermute(value, 'node', pairs)]
    ppermute x3, starting transfers between devices: 5.89 us -> 10.9 us  [to_next_chip(): return lax.ppermute(value, 'node', pairs)]
    ppermute x4 -> x7, starting transfers between devices: 0.52 us -> 2.31 us  [swapped(): lax.ppermute(value, 'node', [(d, d ^ distance) for d in range(devices)])]
    pallas_call x2 -> x3, Pallas kernels: 6.55 us -> 7.88 us  [slots_call(): pl.pallas_call(functools.partial(slots_kernel, tuple(names), sizes), out_...]
    ppermute x4 -> x7, waiting for transfers between devices: 0.01 us -> 1 us  [swapped(): lax.ppermute(value, 'node', [(d, d ^ distance) for d in range(devices)])]
    slice x0 -> x6, local copies, waits for them, and re-layouts: none -> 0.97 us  [swapped_parts(): return [swapped(value[:cut], devices, 1), swapped(value[cut:], devices, 1)]]
  transfers between devices with their start and end apart: 8 -> 11, of which waited for: 4 -> 3; matrix products, arithmetic and copies ran while one was open for 0% -> 2% of each run, Pallas kernels for 25% -> 28%
where the time goes in v3:
time: 42.7 us; the launch traced here: 42.1 us
  starting transfers between devices  14.8 us (35%)
  Pallas kernels  14 us (33%)
  waiting for transfers between devices  9.92 us (23%)
  local copies, waits for them, and re-layouts  1.67 us (4%)
  other arithmetic  1.65 us (4%)
    ppermute x3, starting transfers between devices, to_next_chip(): return lax.ppermute(value, 'node', pairs)  10.9 us
    pallas_call x3, Pallas kernels, slots_call(): pl.pallas_call(functools.partial(slots_kernel, tuple(names), sizes), out_...  7.88 us
    ppermute x1, waiting for transfers between devices, to_next_segment(): lax.ppermute(value, 'segment', [(s, (s + 1) % count) for s in range(count)])  7.77 us
    pallas_call x1, Pallas kernels, body(): pl.pallas_call(prep_kernel, out_shape=(shape((blocks, pairs, wide, 2 * br...  3.97 us
    ppermute x7, starting transfers between devices, swapped(): lax.ppermute(value, 'node', [(d, d ^ distance) for d in range(devices)])  2.31 us
    pallas_call x1, Pallas kernels, body(): pl.pallas_call(functools.partial(finish_kernel, names), out_shape=shape((...  2.14 us
    ppermute x1, starting transfers between devices, to_next_segment(): lax.ppermute(value, 'segment', [(s, (s + 1) % count) for s in range(count)])  1.54 us
    ppermute x3, waiting for transfers between devices, to_next_chip(): return lax.ppermute(value, 'node', pairs)  1.15 us
  transfers between devices with their start and end apart: 11, of which 3 were waited for; matrix products, arithmetic and copies ran while one was open for 2% of the time, Pallas kernels for 28%

profile of v3, /device:TPU:0, one launch (start us, length us, event | category | flops | bytes accessed | tf_op | source)
XLA Modules:
  0.0 42.1 jit_solution(8192880188052445947)
XLA Ops:
  0.0 0.7 %convert_element_type.5 = bf16[1,256]{1,0:T(2,128)(2,1)S(1)} convert(s32[1,256]{1,0:T(1,128)} %bitcast.13) | non-fusion elementwise | flops 256 | bytes 1536 | tf_op jit(solution)/shard_map/convert_element_type | solution.py:377
  0.7 1.0 %fusion.1.load_ref = bf16[272,512]{1,0:T(8,128)(2,1)S(1)} fusion(bf16[1,256]{1,0:T(2,128)(2,1)S(1)} %convert_element_type.5, bf16[256,512]{1,0:T(8,128)(2,1)} %bitcast.10), kind=kLoop, calls=%fused_computation.2 | loop fusion | flops 835584 | bytes 541184 | tf_op jit(solution)/shard_map/concatenate | solution.py:378
  1.7 3.1 %collective-permute-start = (bf16[272,512]{1,0:T(8,128)(2,1)S(1)}, bf16[272,512]{1,0:T(8,128)(2,1)S(1)}, u32[]{:S(2)}, u32[]{:S(2)}) collective-permute-start(bf16[272,512]{1,0:T(8,128)(2,1)S(1)} %fusion.1.load_ref), channel_id=1, source_target_pairs={{0,2},{1,3},{2,6},{3,7},{6,4},{7,5},{4,0},{5,1},{8,10},{9,11},{10,... | collective-permute-start | bytes 835592 | tf_op jit(solution)/shard_map/ppermute | solution.py:38
  4.7 1.1 %collective-permute-start.5 = (bf16[272,512]{1,0:T(8,128)(2,1)S(1)}, bf16[272,512]{1,0:T(8,128)(2,1)S(1)}, u32[]{:S(2)}, u32[]{:S(2)}) collective-permute-start(bf16[272,512]{1,0:T(8,128)(2,1)S(1)} %fusion.1.load_ref), channel_id=1, source_target_pairs={{0,4},{1,5},{2,0},{3,1},{6,2},{7,3},{4,6},{5,7},{8,12},{9,13},{10,... | collective-permute-start | bytes 835592 | tf_op jit(solution)/shard_map/ppermute | solution.py:38
  5.8 0.9 %slice_bitcast_fusion = bf16[128,512]{1,0:T(8,128)(2,1)S(1)} fusion(bf16[1,256,512]{2,1,0:T(8,128)(2,1)} %param.10), kind=kLoop, calls=%fused_computation.3 | loop fusion | bytes 262144 | tf_op jit(solution)/shard_map/slice | solution.py:46
  6.7 0.1 collective-permute-start.1
  6.8 0.6 %collective-permute-start.2 = (bf16[144,512]{1,0:T(8,128)(2,1)S(1)}, bf16[144,512]{1,0:T(8,128)(2,1)S(1)}, u32[]{:S(2)}, u32[]{:S(2)}) collective-permute-start(bf16[144,512]{1,0:T(8,128)(2,1)S(1)} %slice.28), channel_id=1, source_target_pairs={{0,1},{1,0},{2,3},{3,2},{4,5},{5,4},{6,7},{7,6},{8,9},{9,8},{10,11... | collective-permute-start | bytes 442376 | tf_op jit(solution)/shard_map/ppermute | solution.py:42
  7.4 4.0 %prepare.1 = (bf16[2,4,128,256]{3,2,1,0:T(8,128)(2,1)S(1)}, f32[2,512,128]{2,1,0:T(8,128)S(1)}, f32[2,8,128]{2,1,0:T(8,128)S(1)}, f32[2,4,2,128,128]{4,3,2,1,0:T...) custom-call(bf16[272,512]{1,0:T(8,128)(2,1)S(1)} %fusion.1.load_ref,, ...), custom_call_target="tpu_custom_call" | custom-call | flops 65536 | bytes 1024 | tf_op jit(solution)/shard_map/prepare/pallas_call | solution.py:391
  11.4 1.1 %collective-permute-done.refs_2_ = bf16[272,512]{1,0:T(8,128)(2,1)S(1)} collective-permute-done((bf16[272,512]{1,0:T(8,128)(2,1)S(1)}, bf16[272,512]{1,0:T(8,128)(2,1)S(1)}, u32[]{:S(2)}, u32[]{:S(2)}) %collective-permute-start) | collective-permute-done | bytes 278560 | tf_op jit(solution)/shard_map/ppermute | solution.py:38
  12.5 0.1 collective-permute-start.4
  12.6 0.6 %collective-permute-start.3 = (bf16[128,512]{1,0:T(8,128)(2,1)S(1)}, bf16[128,512]{1,0:T(8,128)(2,1)S(1)}, u32[]{:S(2)}, u32[]{:S(2)}) collective-permute-start(bf16[128,512]{1,0:T(8,128)(2,1)S(1)} %slice.24), channel_id=1, source_target_pairs={{0,1},{1,0},{2,3},{3,2},{4,5},{5,4},{6,7},{7,6},{8,9},{9,8},{10,11... | collective-permute-start | bytes 393224 | tf_op jit(solution)/shard_map/ppermute | solution.py:42
  13.2 6.7 %collective-permute-start.8 = (bf16[272,512]{1,0:T(8,128)(2,1)S(1)}, bf16[272,512]{1,0:T(8,128)(2,1)S(1)}, u32[]{:S(2)}, u32[]{:S(2)}) collective-permute-start(bf16[272,512]{1,0:T(8,128)(2,1)S(1)} %collective-permute-done.refs_2_), channel_id=1, source_target_pairs={{0,2},{1,3},{2,6},{3,7},{6,4},{7,5},{4,0},{5,1},{8,10},{9,11},{10,... | collective-permute-start | bytes 835592 | tf_op jit(solution)/shard_map/ppermute | solution.py:38
  19.9 0.0 collective-permute-done.2.refs_1_
  19.9 3.6 %slots_0.1 = (f32[2,512,128]{2,1,0:T(8,128)S(1)}, f32[2,8,128]{2,1,0:T(8,128)S(1)}, f32[32,512]{1,0:T(8,128)S(1)}, f32[32,128]{1,0:T(8,128)S(1)}) custom-call(f32[2,4,8,128]{3,2,1,0:T(8,128)S(1)} %get-tuple-element.36.mask_ref, f32[1,512]{1,0:T(1,128)S(1)} %get-tuple-element.37.gain_ref, bf16[512,512]{1,0:T(8,128)(2,1)S(1)} %get-tuple-element.38.wk_ref, ...), custom_call_target="tpu_custom_call" | custom-call | flops 65536 | bytes 1024 | tf_op jit(solution)/shard_map/slots_0/pallas_call | solution.py:452
  23.5 0.1 collective-permute-start.7
  23.6 0.6 %collective-permute-start.6 = (bf16[128,512]{1,0:T(8,128)(2,1)S(1)}, bf16[128,512]{1,0:T(8,128)(2,1)S(1)}, u32[]{:S(2)}, u32[]{:S(2)}) collective-permute-start(bf16[128,512]{1,0:T(8,128)(2,1)S(1)} %slice.26), channel_id=1, source_target_pairs={{0,1},{1,0},{2,3},{3,2},{4,5},{5,4},{6,7},{7,6},{8,9},{9,8},{10,11... | collective-permute-start | bytes 393224 | tf_op jit(solution)/shard_map/ppermute | solution.py:42
  24.2 1.0 %collective-permute-done.6.refs_1_ = bf16[128,512]{1,0:T(8,128)(2,1)S(1)} collective-permute-done((bf16[128,512]{1,0:T(8,128)(2,1)S(1)}, bf16[128,512]{1,0:T(8,128)(2,1)S(1)}, u32[]{:S(2)}, u32[]{:S(2)}) %collective-permute-start.6) | collective-permute-done | bytes 131104 | tf_op jit(solution)/shard_map/ppermute | solution.py:42
  25.2 2.7 %slots_1.1 = (f32[2,512,128]{2,1,0:T(8,128)S(1)}, f32[2,8,128]{2,1,0:T(8,128)S(1)}, f32[32,512]{1,0:T(8,128)S(1)}, f32[32,128]{1,0:T(8,128)S(1)}) custom-call(f32[2,4,8,128]{3,2,1,0:T(8,128)S(1)} %get-tuple-element.36.mask_ref, f32[1,512]{1,0:T(1,128)S(1)} %get-tuple-element.37.gain_ref, bf16[512,512]{1,0:T(8,128)(2,1)S(1)} %get-tuple-element.38.wk_ref, ...), custom_call_target="tpu_custom_call" | custom-call | flops 65536 | bytes 1024 | tf_op jit(solution)/shard_map/slots_1/pallas_call | solution.py:452
  27.9 0.4 %collective-permute-start.9 = (bf16[272,512]{1,0:T(8,128)(2,1)S(1)}, bf16[272,512]{1,0:T(8,128)(2,1)S(1)}, u32[]{:S(2)}, u32[]{:S(2)}) collective-permute-start(bf16[272,512]{1,0:T(8,128)(2,1)S(1)} %collective-permute-done.8.refs_0_), channel_id=1, source_target_pairs={{0,1},{1,0},{2,3},{3,2},{4,5},{5,4},{6,7},{7,6},{8,9},{9,8},{10,11... | collective-permute-start | bytes 835592 | tf_op jit(solution)/shard_map/ppermute | solution.py:42
  28.3 1.6 %slots_last.1 = (f32[2,512,128]{2,1,0:T(8,128)S(1)}, f32[2,8,128]{2,1,0:T(8,128)S(1)}, f32[32,512]{1,0:T(8,128)S(1)}, f32[32,128]{1,0:T(8,128)S(1)}) custom-call(f32[2,4,8,128]{3,2,1,0:T(8,128)S(1)} %get-tuple-element.36.mask_ref, f32[1,512]{1,0:T(1,128)S(1)} %get-tuple-element.37.gain_ref, bf16[512,512]{1,0:T(8,128)(2,1)S(1)} %get-tuple-element.38.wk_ref, ...), custom_call_target="tpu_custom_call" | custom-call | flops 65536 | bytes 1024 | tf_op jit(solution)/shard_map/slots_last/pallas_call | solution.py:452
  30.0 2.1 %finish.1 = bf16[256,512]{1,0:T(8,128)(2,1)S(1)} custom-call(f32[2,4,8,128]{3,2,1,0:T(8,128)S(1)} %get-tuple-element.36.mask_ref, f32[1,512]{1,0:T(1,128)S(1)} %get-tuple-element.37.gain_ref, bf16[512,512]{1,0:T(8,128)(2,1)S(1)} %get-tuple-element.38.wk_ref, bf16[512,512]{1,0:T(8,128)(2,1)S(1)} %get-tuple-element.39.wvt_ref, ...), custom_call_target="tpu_custom_call" | custom-call | flops 65536 | bytes 1024 | tf_op jit(solution)/shard_map/finish/pallas_call | solution.py:491
  32.1 1.5 %collective-permute-start.10 = (bf16[1,256,512]{2,1,0:T(8,128)(2,1)S(1)}, bf16[1,256,512]{2,1,0:T(8,128)(2,1)S(1)}, u32[]{:S(2)}, u32[]{:S(2)}) collective-permute-start(bf16[1,256,512]{2,1,0:T(8,128)(2,1)S(1)} %bitcast.8), channel_id=1, source_target_pairs={{0,8},{8,16},{16,24},{24,0},{1,9},{9,17},{17,25},{25,1},{2,10},{10... | collective-permute-start | bytes 786440 | tf_op jit(solution)/shard_map/ppermute | solution.py:51
  33.7 7.8 %collective-permute-done.10 = bf16[1,256,512]{2,1,0:T(8,128)(2,1)S(1)} collective-permute-done((bf16[1,256,512]{2,1,0:T(8,128)(2,1)S(1)}, bf16[1,256,512]{2,1,0:T(8,128)(2,1)S(1)}, u32[]{:S(2)}, u32[]{:S(2)}) %collective-permute-start.10) | collective-permute-done | bytes 262176 | tf_op jit(solution)/shard_map/ppermute | solution.py:51
  41.4 0.7 %copy.12 = bf16[1,256,512]{2,1,0:T(8,128)(2,1)} copy(bf16[1,256,512]{2,1,0:T(8,128)(2,1)S(1)} %collective-permute-done.10) | data formatting | bytes 524288
  (12 shorter events, 0.1 us)
Async XLA Ops:
  1.7 10.8 %collective-permute-start = (bf16[272,512]{1,0:T(8,128)(2,1)S(1)}, bf16[272,512]{1,0:T(8,128)(2,1)S(1)}, u32[]{:S(2)}, u32[]{:S(2)}) collective-permute-start(bf16[272,512]{1,0:T(8,128)(2,1)S(1)} %fusion.1.load_ref), channel_id=1, source_target_pairs={{0,2},{1,3},{2,6},{3,7},{6,4},{7,5},{4,0},{5,1},{8,10},{9,11},{10,... | collective-permute-start | bytes 835592 | tf_op jit(solution)/shard_map/ppermute | solution.py:38
  4.7 18.8 %collective-permute-start.5 = (bf16[272,512]{1,0:T(8,128)(2,1)S(1)}, bf16[272,512]{1,0:T(8,128)(2,1)S(1)}, u32[]{:S(2)}, u32[]{:S(2)}) collective-permute-start(bf16[272,512]{1,0:T(8,128)(2,1)S(1)} %fusion.1.load_ref), channel_id=1, source_target_pairs={{0,4},{1,5},{2,0},{3,1},{6,2},{7,3},{4,6},{5,7},{8,12},{9,13},{10,... | collective-permute-start | bytes 835592 | tf_op jit(solution)/shard_map/ppermute | solution.py:38
  6.7 6.5 %collective-permute-start.1 = (bf16[128,512]{1,0:T(8,128)(2,1)S(1)}, bf16[128,512]{1,0:T(8,128)(2,1)S(1)}, u32[]{:S(2)}, u32[]{:S(2)}) collective-permute-start(bf16[128,512]{1,0:T(8,128)(2,1)S(1)} %slice_bitcast_fusion), channel_id=1, source_target_pairs={{0,1},{1,0},{2,3},{3,2},{4,5},{5,4},{6,7},{7,6},{8,9},{9,8},{10,11... | collective-permute-start | bytes 393224 | tf_op jit(solution)/shard_map/ppermute | solution.py:42
  6.8 13.1 %collective-permute-start.2 = (bf16[144,512]{1,0:T(8,128)(2,1)S(1)}, bf16[144,512]{1,0:T(8,128)(2,1)S(1)}, u32[]{:S(2)}, u32[]{:S(2)}) collective-permute-start(bf16[144,512]{1,0:T(8,128)(2,1)S(1)} %slice.28), channel_id=1, source_target_pairs={{0,1},{1,0},{2,3},{3,2},{4,5},{5,4},{6,7},{7,6},{8,9},{9,8},{10,11... | collective-permute-start | bytes 442376 | tf_op jit(solution)/shard_map/ppermute | solution.py:42
  12.5 7.4 %collective-permute-start.4 = (bf16[144,512]{1,0:T(8,128)(2,1)S(1)}, bf16[144,512]{1,0:T(8,128)(2,1)S(1)}, u32[]{:S(2)}, u32[]{:S(2)}) collective-permute-start(bf16[144,512]{1,0:T(8,128)(2,1)S(1)} %slice.25), channel_id=1, source_target_pairs={{0,1},{1,0},{2,3},{3,2},{4,5},{5,4},{6,7},{7,6},{8,9},{9,8},{10,11... | collective-permute-start | bytes 442376 | tf_op jit(solution)/shard_map/ppermute | solution.py:42
  12.6 7.3 %collective-permute-start.3 = (bf16[128,512]{1,0:T(8,128)(2,1)S(1)}, bf16[128,512]{1,0:T(8,128)(2,1)S(1)}, u32[]{:S(2)}, u32[]{:S(2)}) collective-permute-start(bf16[128,512]{1,0:T(8,128)(2,1)S(1)} %slice.24), channel_id=1, source_target_pairs={{0,1},{1,0},{2,3},{3,2},{4,5},{5,4},{6,7},{7,6},{8,9},{9,8},{10,11... | collective-permute-start | bytes 393224 | tf_op jit(solution)/shard_map/ppermute | solution.py:42
  13.2 14.7 %collective-permute-start.8 = (bf16[272,512]{1,0:T(8,128)(2,1)S(1)}, bf16[272,512]{1,0:T(8,128)(2,1)S(1)}, u32[]{:S(2)}, u32[]{:S(2)}) collective-permute-start(bf16[272,512]{1,0:T(8,128)(2,1)S(1)} %collective-permute-done.refs_2_), channel_id=1, source_target_pairs={{0,2},{1,3},{2,6},{3,7},{6,4},{7,5},{4,0},{5,1},{8,10},{9,11},{10,... | collective-permute-start | bytes 835592 | tf_op jit(solution)/shard_map/ppermute | solution.py:38
  23.5 1.6 %collective-permute-start.7 = (bf16[144,512]{1,0:T(8,128)(2,1)S(1)}, bf16[144,512]{1,0:T(8,128)(2,1)S(1)}, u32[]{:S(2)}, u32[]{:S(2)}) collective-permute-start(bf16[144,512]{1,0:T(8,128)(2,1)S(1)} %slice.27), channel_id=1, source_target_pairs={{0,1},{1,0},{2,3},{3,2},{4,5},{5,4},{6,7},{7,6},{8,9},{9,8},{10,11... | collective-permute-start | bytes 442376 | tf_op jit(solution)/shard_map/ppermute | solution.py:42
  23.6 1.5 %collective-permute-start.6 = (bf16[128,512]{1,0:T(8,128)(2,1)S(1)}, bf16[128,512]{1,0:T(8,128)(2,1)S(1)}, u32[]{:S(2)}, u32[]{:S(2)}) collective-permute-start(bf16[128,512]{1,0:T(8,128)(2,1)S(1)} %slice.26), channel_id=1, source_target_pairs={{0,1},{1,0},{2,3},{3,2},{4,5},{5,4},{6,7},{7,6},{8,9},{9,8},{10,11... | collective-permute-start | bytes 393224 | tf_op jit(solution)/shard_map/ppermute | solution.py:42
  27.9 2.1 %collective-permute-start.9 = (bf16[272,512]{1,0:T(8,128)(2,1)S(1)}, bf16[272,512]{1,0:T(8,128)(2,1)S(1)}, u32[]{:S(2)}, u32[]{:S(2)}) collective-permute-start(bf16[272,512]{1,0:T(8,128)(2,1)S(1)} %collective-permute-done.8.refs_0_), channel_id=1, source_target_pairs={{0,1},{1,0},{2,3},{3,2},{4,5},{5,4},{6,7},{7,6},{8,9},{9,8},{10,11... | collective-permute-start | bytes 835592 | tf_op jit(solution)/shard_map/ppermute | solution.py:42
  32.1 9.3 %collective-permute-start.10 = (bf16[1,256,512]{2,1,0:T(8,128)(2,1)S(1)}, bf16[1,256,512]{2,1,0:T(8,128)(2,1)S(1)}, u32[]{:S(2)}, u32[]{:S(2)}) collective-permute-start(bf16[1,256,512]{2,1,0:T(8,128)(2,1)S(1)} %bitcast.8), channel_id=1, source_target_pairs={{0,8},{8,16},{16,24},{24,0},{1,9},{9,17},{17,25},{25,1},{2,10},{10... | collective-permute-start | bytes 786440 | tf_op jit(solution)/shard_map/ppermute | solution.py:51

commit v4 on v3

--- a/solution.py
+++ b/solution.py
@@ -42,8 +42,10 @@
     return lax.ppermute(value, "node", [(d, d ^ distance) for d in range(devices)])
 
 
-def swapped_parts(value, devices, cut):
-    return [swapped(value[:cut], devices, 1), swapped(value[cut:], devices, 1)]
+def swapped_parts(value, devices, parts):
+    tiles = value.shape[0] // 16
+    cuts = [0] + [16 * (-(-tiles * (i + 1) // parts)) for i in range(parts)]
+    return [swapped(value[a:b], devices, 1) for a, b in zip(cuts, cuts[1:])]
 
 
 def to_next_segment(value):
@@ -118,6 +120,16 @@
     for copy in copies:
         copy.start()
     return copies
+
+
+def pack_kernel(x_hbm, vid_hbm, load_ref, vid_ref, sems):
+    rows = vid_ref.shape[1]
+    copies = start_copies([(x_hbm, load_ref.at[:rows, :]), (vid_hbm, vid_ref)], sems)
+    copies[1].wait()
+    tile = jnp.broadcast_to(vid_ref[...].astype(F32), (EXTRA, rows))
+    rest = jnp.zeros((EXTRA, load_ref.shape[1] - rows), F32)
+    load_ref[rows:, :] = jnp.concatenate([tile, rest], axis=1).astype(BF16)
+    copies[0].wait()
 
 
 def vid_row(load_ref, rows):
@@ -373,13 +385,23 @@
     after = lax.optimization_barrier
     unit = 2**16
 
-    ids = after(virtual_id.reshape(1, rows))
-    ids = jnp.pad(ids.astype(BF16), ((0, EXTRA - 1), (0, width - rows)))
-    load = jnp.concatenate([activations[0], ids], axis=0)
+    load = pl.pallas_call(
+        pack_kernel,
+        out_shape=shape((rows + EXTRA, width), BF16),
+        in_specs=[HBM] * 2,
+        out_specs=VMEM,
+        scratch_shapes=[pltpu.VMEM((1, rows), jnp.int32), pltpu.SemaphoreType.DMA((2,))],
+        compiler_params=params(24),
+        cost_estimate=cost(unit),
+        name="pack_rows",
+    )(
+        pltpu.with_memory_space_constraint(activations[0], pltpu.HBM),
+        pltpu.with_memory_space_constraint(virtual_id.reshape(1, rows), pltpu.HBM),
+    )
     near = {1: to_next_chip(load, devices, 1)}
     if chips > 2:
         near[chips - 1] = to_next_chip(load, devices, -1)
-    far = {0: swapped_parts(load, devices, br)}
+    far = {0: swapped(load, devices, 1)}
 
     accumulators = (
         shape((blocks, width, br), F32),
@@ -471,22 +493,21 @@
             order.append((chips - s, -1))
     waiting = [(1, 0)]
     for i, (step, way) in enumerate(order):
+        last = i == len(order) - 1
         sums = arrive(step, sums)
+        if not last:
+            far[step] = swapped_parts(near[step], devices, 3 if i == 0 else 2)
+        else:
+            far[step] = swapped(near[step], devices, 1)
+        waiting.append((0, step))
+        if not last:
+            waiting.append((1, step))
+        sums = slots_call(waiting, sums, "slots_%d" % i)
+        waiting = []
         nexts = step + way
         if nexts not in near and (nexts, way) in order:
+            sums = arrive(step, sums)
             near[nexts] = to_next_chip(near[step], devices, way)
-        if i == len(order) - 1:
-            far[step] = swapped(near[step], devices, 1)
-        else:
-            far[step] = swapped_parts(near[step], devices, br)
-        waiting.append((0, step))
-        if i == len(order) - 1:
-            break
-        waiting.append((1, step))
-        if i < len(order) - 1:
-            sums = slots_call(waiting, sums, "slots_%d" % i)
-            waiting = []
-    sums = slots_call(waiting, sums, "slots_last")
     names = ((1, order[-1][0]),)
     updated = pl.pallas_call(
         functools.partial(finish_kernel, names),

time: 42.7 us -> 45.8 us (1.073)
  the two profiles are of different devices: /device:TPU:0 before, /device:TPU:28 now
where the time goes in v4:
time: 45.8 us; the launch traced here: 45.6 us
  waiting for transfers between devices  24 us (52%)
  Pallas kernels  14.9 us (33%)
  starting transfers between devices  5.9 us (13%)
  local copies, waits for them, and re-layouts  0.74 us (2%)
    ppermute x3, waiting for transfers between devices, to_next_chip(): return lax.ppermute(value, 'node', pairs)  13.7 us
    ppermute x1, waiting for transfers between devices, to_next_segment(): lax.ppermute(value, 'segment', [(s, (s + 1) % count) for s in range(count)])  8.12 us
    pallas_call x3, Pallas kernels, slots_call(): pl.pallas_call(functools.partial(slots_kernel, tuple(names), sizes), out_...  7.86 us
    pallas_call x1, Pallas kernels, body(): pl.pallas_call(prep_kernel, out_shape=(shape((blocks, pairs, wide, 2 * br...  3.97 us
    ppermute x3, starting transfers between devices, to_next_chip(): return lax.ppermute(value, 'node', pairs)  3.04 us
    ppermute x7, waiting for transfers between devices, swapped(): lax.ppermute(value, 'node', [(d, d ^ distance) for d in range(devices)])  2.18 us
    pallas_call x1, Pallas kernels, body(): pl.pallas_call(functools.partial(finish_kernel, names), out_shape=shape((...  2.14 us
    ppermute x1, starting transfers between devices, to_next_segment(): lax.ppermute(value, 'segment', [(s, (s + 1) % count) for s in range(count)])  1.55 us
  transfers between devices with their start and end apart: 11, of which 5 were waited for; matrix products, arithmetic and copies ran while one was open for 0% of the time, Pallas kernels for 26%

profile of v4, /device:TPU:28, one launch (start us, length us, event | category | flops | bytes accessed | tf_op | source)
XLA Modules:
  0.0 45.6 jit_solution(8840915961456770112)
XLA Ops:
  0.0 1.0 %pack_rows.1.load_ref = bf16[272,512]{1,0:T(8,128)(2,1)S(1)} custom-call(bf16[256,512]{1,0:T(8,128)(2,1)} %bitcast.9, s32[1,256]{1,0:T(1,128)} %bitcast.11), custom_call_target="tpu_custom_call" | custom-call | flops 65536 | bytes 1024 | tf_op jit(solution)/shard_map/pack_rows/pallas_call | solution.py:388
  1.0 0.5 %collective-permute-start = (bf16[272,512]{1,0:T(8,128)(2,1)S(1)}, bf16[272,512]{1,0:T(8,128)(2,1)S(1)}, u32[]{:S(2)}, u32[]{:S(2)}) collective-permute-start(bf16[272,512]{1,0:T(8,128)(2,1)S(1)} %pack_rows.1.load_ref), channel_id=1, source_target_pairs={{0,2},{1,3},{2,6},{3,7},{6,4},{7,5},{4,0},{5,1},{8,10},{9,11},{10,... | collective-permute-start | bytes 835592 | tf_op jit(solution)/shard_map/ppermute | solution.py:38
  1.5 2.5 %collective-permute-start.5 = (bf16[272,512]{1,0:T(8,128)(2,1)S(1)}, bf16[272,512]{1,0:T(8,128)(2,1)S(1)}, u32[]{:S(2)}, u32[]{:S(2)}) collective-permute-start(bf16[272,512]{1,0:T(8,128)(2,1)S(1)} %pack_rows.1.load_ref), channel_id=1, source_target_pairs={{0,4},{1,5},{2,0},{3,1},{6,2},{7,3},{4,6},{5,7},{8,12},{9,13},{10,... | collective-permute-start | bytes 835592 | tf_op jit(solution)/shard_map/ppermute | solution.py:38
  4.0 4.0 %prepare.1 = (bf16[2,4,128,256]{3,2,1,0:T(8,128)(2,1)S(1)}, f32[2,512,128]{2,1,0:T(8,128)S(1)}, f32[2,8,128]{2,1,0:T(8,128)S(1)}, f32[2,4,2,128,128]{4,3,2,1,0:T...) custom-call(bf16[272,512]{1,0:T(8,128)(2,1)S(1)} %pack_rows.1.load_r, ...), custom_call_target="tpu_custom_call" | custom-call | flops 65536 | bytes 1024 | tf_op jit(solution)/shard_map/prepare/pallas_call | solution.py:413
  7.9 8.4 %collective-permute-done.refs_1_ = bf16[272,512]{1,0:T(8,128)(2,1)S(1)} collective-permute-done((bf16[272,512]{1,0:T(8,128)(2,1)S(1)}, bf16[272,512]{1,0:T(8,128)(2,1)S(1)}, u32[]{:S(2)}, u32[]{:S(2)}) %collective-permute-start) | collective-permute-done | bytes 278560 | tf_op jit(solution)/shard_map/ppermute | solution.py:38
  16.4 0.1 collective-permute-start.2
  16.4 0.5 %collective-permute-start.3 = (bf16[96,512]{1,0:T(8,128)(2,1)S(1)}, bf16[96,512]{1,0:T(8,128)(2,1)S(1)}, u32[]{:S(2)}, u32[]{:S(2)}) collective-permute-start(bf16[96,512]{1,0:T(8,128)(2,1)S(1)} %get-tuple-element.71), channel_id=1, source_target_pairs={{0,1},{1,0},{2,3},{3,2},{4,5},{5,4},{6,7},{7,6},{8,9},{9,8},{10,11... | collective-permute-start | bytes 294920 | tf_op jit(solution)/shard_map/ppermute | solution.py:42
  16.9 0.1 collective-permute-start.4
  17.0 0.0 collective-permute-done.1.refs_0_
  17.0 1.2 %collective-permute-done.4.refs_4_ = bf16[80,512]{1,0:T(8,128)(2,1)S(1)} collective-permute-done((bf16[80,512]{1,0:T(8,128)(2,1)S(1)}, bf16[80,512]{1,0:T(8,128)(2,1)S(1)}, u32[]{:S(2)}, u32[]{:S(2)}) %collective-permute-start.4) | collective-permute-done | bytes 81952 | tf_op jit(solution)/shard_map/ppermute | solution.py:42
  18.2 0.0 collective-permute-done.2.refs_2_
  18.2 3.6 %slots_0.1 = (f32[2,512,128]{2,1,0:T(8,128)S(1)}, f32[2,8,128]{2,1,0:T(8,128)S(1)}, f32[32,512]{1,0:T(8,128)S(1)}, f32[32,128]{1,0:T(8,128)S(1)}) custom-call(f32[2,4,8,128]{3,2,1,0:T(8,128)S(1)} %get-tuple-element.38.mask_ref, f32[1,512]{1,0:T(1,128)S(1)} %get-tuple-element.39.gain_ref, bf16[512,512]{1,0:T(8,128)(2,1)S(1)} %get-tuple-element.40.wk_ref, ...), custom_call_target="tpu_custom_call" | custom-call | flops 65536 | bytes 1024 | tf_op jit(solution)/shard_map/slots_0/pallas_call | solution.py:474
  21.8 0.1 collective-permute-start.8
  21.8 0.0 collective-permute-done.5.refs_0_
  21.9 0.2 collective-permute-start.6
  22.1 0.4 collective-permute-start.7
  22.5 1.0 %collective-permute-done.7.refs_2_ = bf16[128,512]{1,0:T(8,128)(2,1)S(1)} collective-permute-done((bf16[128,512]{1,0:T(8,128)(2,1)S(1)}, bf16[128,512]{1,0:T(8,128)(2,1)S(1)}, u32[]{:S(2)}, u32[]{:S(2)}) %collective-permute-start.7) | collective-permute-done | bytes 131104 | tf_op jit(solution)/shard_map/ppermute | solution.py:42
  23.5 2.7 %slots_1.1 = (f32[2,512,128]{2,1,0:T(8,128)S(1)}, f32[2,8,128]{2,1,0:T(8,128)S(1)}, f32[32,512]{1,0:T(8,128)S(1)}, f32[32,128]{1,0:T(8,128)S(1)}) custom-call(f32[2,4,8,128]{3,2,1,0:T(8,128)S(1)} %get-tuple-element.38.mask_ref, f32[1,512]{1,0:T(1,128)S(1)} %get-tuple-element.39.gain_ref, bf16[512,512]{1,0:T(8,128)(2,1)S(1)} %get-tuple-element.40.wk_ref, ...), custom_call_target="tpu_custom_call" | custom-call | flops 65536 | bytes 1024 | tf_op jit(solution)/shard_map/slots_1/pallas_call | solution.py:474
  26.2 5.2 %collective-permute-done.8.refs_0_ = bf16[272,512]{1,0:T(8,128)(2,1)S(1)} collective-permute-done((bf16[272,512]{1,0:T(8,128)(2,1)S(1)}, bf16[272,512]{1,0:T(8,128)(2,1)S(1)}, u32[]{:S(2)}, u32[]{:S(2)}) %collective-permute-start.8) | collective-permute-done | bytes 278560 | tf_op jit(solution)/shard_map/ppermute | solution.py:38
  31.5 1.6 %slots_2.1 = (f32[2,512,128]{2,1,0:T(8,128)S(1)}, f32[2,8,128]{2,1,0:T(8,128)S(1)}, f32[32,512]{1,0:T(8,128)S(1)}, f32[32,128]{1,0:T(8,128)S(1)}) custom-call(f32[2,4,8,128]{3,2,1,0:T(8,128)S(1)} %get-tuple-element.38.mask_ref, f32[1,512]{1,0:T(1,128)S(1)} %get-tuple-element.39.gain_ref, bf16[512,512]{1,0:T(8,128)(2,1)S(1)} %get-tuple-element.40.wk_ref, ...), custom_call_target="tpu_custom_call" | custom-call | flops 65536 | bytes 1024 | tf_op jit(solution)/shard_map/slots_2/pallas_call | solution.py:474
  33.1 2.1 %finish.1 = bf16[256,512]{1,0:T(8,128)(2,1)S(1)} custom-call(f32[2,4,8,128]{3,2,1,0:T(8,128)S(1)} %get-tuple-element.38.mask_ref, f32[1,512]{1,0:T(1,128)S(1)} %get-tuple-element.39.gain_ref, bf16[512,512]{1,0:T(8,128)(2,1)S(1)} %get-tuple-element.40.wk_ref, bf16[512,512]{1,0:T(8,128)(2,1)S(1)} %get-tuple-element.41.wvt_ref, ...), custom_call_target="tpu_custom_call" | custom-call | flops 65536 | bytes 1024 | tf_op jit(solution)/shard_map/finish/pallas_call | solution.py:512
  35.3 1.6 %collective-permute-start.10 = (bf16[1,256,512]{2,1,0:T(8,128)(2,1)S(1)}, bf16[1,256,512]{2,1,0:T(8,128)(2,1)S(1)}, u32[]{:S(2)}, u32[]{:S(2)}) collective-permute-start(bf16[1,256,512]{2,1,0:T(8,128)(2,1)S(1)} %bitcast.6), channel_id=1, source_target_pairs={{0,8},{8,16},{16,24},{24,0},{1,9},{9,17},{17,25},{25,1},{2,10},{10... | collective-permute-start | bytes 786440 | tf_op jit(solution)/shard_map/ppermute | solution.py:53
  36.8 8.1 %collective-permute-done.10 = bf16[1,256,512]{2,1,0:T(8,128)(2,1)S(1)} collective-permute-done((bf16[1,256,512]{2,1,0:T(8,128)(2,1)S(1)}, bf16[1,256,512]{2,1,0:T(8,128)(2,1)S(1)}, u32[]{:S(2)}, u32[]{:S(2)}) %collective-permute-start.10) | collective-permute-done | bytes 262176 | tf_op jit(solution)/shard_map/ppermute | solution.py:53
  44.9 0.7 %copy.12 = bf16[1,256,512]{2,1,0:T(8,128)(2,1)} copy(bf16[1,256,512]{2,1,0:T(8,128)(2,1)S(1)} %collective-permute-done.10) | data formatting | bytes 524288
  (9 shorter events, 0.1 us)
Async XLA Ops:
  1.0 15.4 %collective-permute-start = (bf16[272,512]{1,0:T(8,128)(2,1)S(1)}, bf16[272,512]{1,0:T(8,128)(2,1)S(1)}, u32[]{:S(2)}, u32[]{:S(2)}) collective-permute-start(bf16[272,512]{1,0:T(8,128)(2,1)S(1)} %pack_rows.1.load_ref), channel_id=1, source_target_pairs={{0,2},{1,3},{2,6},{3,7},{6,4},{7,5},{4,0},{5,1},{8,10},{9,11},{10,... | collective-permute-start | bytes 835592 | tf_op jit(solution)/shard_map/ppermute | solution.py:38
  1.5 15.6 %collective-permute-start.1 = (bf16[272,512]{1,0:T(8,128)(2,1)S(1)}, bf16[272,512]{1,0:T(8,128)(2,1)S(1)}, u32[]{:S(2)}, u32[]{:S(2)}) collective-permute-start(bf16[272,512]{1,0:T(8,128)(2,1)S(1)} %pack_rows.1.load_ref), channel_id=1, source_target_pairs={{0,1},{1,0},{2,3},{3,2},{4,5},{5,4},{6,7},{7,6},{8,9},{9,8},{10,11... | collective-permute-start | bytes 835592 | tf_op jit(solution)/shard_map/ppermute | solution.py:42
  1.5 20.4 %collective-permute-start.5 = (bf16[272,512]{1,0:T(8,128)(2,1)S(1)}, bf16[272,512]{1,0:T(8,128)(2,1)S(1)}, u32[]{:S(2)}, u32[]{:S(2)}) collective-permute-start(bf16[272,512]{1,0:T(8,128)(2,1)S(1)} %pack_rows.1.load_ref), channel_id=1, source_target_pairs={{0,4},{1,5},{2,0},{3,1},{6,2},{7,3},{4,6},{5,7},{8,12},{9,13},{10,... | collective-permute-start | bytes 835592 | tf_op jit(solution)/shard_map/ppermute | solution.py:38
  16.4 1.9 %collective-permute-start.2 = (bf16[96,512]{1,0:T(8,128)(2,1)S(1)}, bf16[96,512]{1,0:T(8,128)(2,1)S(1)}, u32[]{:S(2)}, u32[]{:S(2)}) collective-permute-start(bf16[96,512]{1,0:T(8,128)(2,1)S(1)} %get-tuple-element.72), channel_id=1, source_target_pairs={{0,1},{1,0},{2,3},{3,2},{4,5},{5,4},{6,7},{7,6},{8,9},{9,8},{10,11... | collective-permute-start | bytes 294920 | tf_op jit(solution)/shard_map/ppermute | solution.py:42
  16.4 1.8 %collective-permute-start.3 = (bf16[96,512]{1,0:T(8,128)(2,1)S(1)}, bf16[96,512]{1,0:T(8,128)(2,1)S(1)}, u32[]{:S(2)}, u32[]{:S(2)}) collective-permute-start(bf16[96,512]{1,0:T(8,128)(2,1)S(1)} %get-tuple-element.71), channel_id=1, source_target_pairs={{0,1},{1,0},{2,3},{3,2},{4,5},{5,4},{6,7},{7,6},{8,9},{9,8},{10,11... | collective-permute-start | bytes 294920 | tf_op jit(solution)/shard_map/ppermute | solution.py:42
  16.9 1.3 %collective-permute-start.4 = (bf16[80,512]{1,0:T(8,128)(2,1)S(1)}, bf16[80,512]{1,0:T(8,128)(2,1)S(1)}, u32[]{:S(2)}, u32[]{:S(2)}) collective-permute-start(bf16[80,512]{1,0:T(8,128)(2,1)S(1)} %slice.17), channel_id=1, source_target_pairs={{0,1},{1,0},{2,3},{3,2},{4,5},{5,4},{6,7},{7,6},{8,9},{9,8},{10,11... | collective-permute-start | bytes 245768 | tf_op jit(solution)/shard_map/ppermute | solution.py:42
  21.8 9.7 %collective-permute-start.8 = (bf16[272,512]{1,0:T(8,128)(2,1)S(1)}, bf16[272,512]{1,0:T(8,128)(2,1)S(1)}, u32[]{:S(2)}, u32[]{:S(2)}) collective-permute-start(bf16[272,512]{1,0:T(8,128)(2,1)S(1)} %collective-permute-done.refs_1_), channel_id=1, source_target_pairs={{0,2},{1,3},{2,6},{3,7},{6,4},{7,5},{4,0},{5,1},{8,10},{9,11},{10,... | collective-permute-start | bytes 835592 | tf_op jit(solution)/shard_map/ppermute | solution.py:38
  21.9 1.7 %collective-permute-start.6 = (bf16[144,512]{1,0:T(8,128)(2,1)S(1)}, bf16[144,512]{1,0:T(8,128)(2,1)S(1)}, u32[]{:S(2)}, u32[]{:S(2)}) collective-permute-start(bf16[144,512]{1,0:T(8,128)(2,1)S(1)} %slice.18), channel_id=1, source_target_pairs={{0,1},{1,0},{2,3},{3,2},{4,5},{5,4},{6,7},{7,6},{8,9},{9,8},{10,11... | collective-permute-start | bytes 442376 | tf_op jit(solution)/shard_map/ppermute | solution.py:42
  22.1 1.4 %collective-permute-start.7 = (bf16[128,512]{1,0:T(8,128)(2,1)S(1)}, bf16[128,512]{1,0:T(8,128)(2,1)S(1)}, u32[]{:S(2)}, u32[]{:S(2)}) collective-permute-start(bf16[128,512]{1,0:T(8,128)(2,1)S(1)} %slice.19), channel_id=1, source_target_pairs={{0,1},{1,0},{2,3},{3,2},{4,5},{5,4},{6,7},{7,6},{8,9},{9,8},{10,11... | collective-permute-start | bytes 393224 | tf_op jit(solution)/shard_map/ppermute | solution.py:42
  31.5 1.7 %collective-permute-start.9 = (bf16[272,512]{1,0:T(8,128)(2,1)S(1)}, bf16[272,512]{1,0:T(8,128)(2,1)S(1)}, u32[]{:S(2)}, u32[]{:S(2)}) collective-permute-start(bf16[272,512]{1,0:T(8,128)(2,1)S(1)} %collective-permute-done.8.refs_0_), channel_id=1, source_target_pairs={{0,1},{1,0},{2,3},{3,2},{4,5},{5,4},{6,7},{7,6},{8,9},{9,8},{10,11... | collective-permute-start | bytes 835592 | tf_op jit(solution)/shard_map/ppermute | solution.py:42
  35.3 9.7 %collective-permute-start.10 = (bf16[1,256,512]{2,1,0:T(8,128)(2,1)S(1)}, bf16[1,256,512]{2,1,0:T(8,128)(2,1)S(1)}, u32[]{:S(2)}, u32[]{:S(2)}) collective-permute-start(bf16[1,256,512]{2,1,0:T(8,128)(2,1)S(1)} %bitcast.6), channel_id=1, source_target_pairs={{0,8},{8,16},{16,24},{24,0},{1,9},{9,17},{17,25},{25,1},{2,10},{10... | collective-permute-start | bytes 786440 | tf_op jit(solution)/shard_map/ppermute | solution.py:53

commit v5 on v4

--- a/solution.py
+++ b/solution.py
@@ -13,6 +13,7 @@
 CAP_LIMIT = 10.0
 LOG2E = 1.4426950408889634
 EXTRA = 16
+PARTS = 2
 F32 = jnp.float32
 BF16 = jnp.bfloat16
 HBM = pl.BlockSpec(memory_space=pltpu.HBM)
@@ -399,8 +400,6 @@
         pltpu.with_memory_space_constraint(virtual_id.reshape(1, rows), pltpu.HBM),
     )
     near = {1: to_next_chip(load, devices, 1)}
-    if chips > 2:
-        near[chips - 1] = to_next_chip(load, devices, -1)
     far = {0: swapped(load, devices, 1)}
 
     accumulators = (
@@ -461,6 +460,9 @@
             pltpu.VMEM((width, count * br), BF16),
         ]
 
+    if chips > 2:
+        back, den = after((load, den))
+        near[chips - 1] = to_next_chip(back, devices, -1)
     sums = (num, den, pool, weight)
 
     def arrive(step, sums):
@@ -496,18 +498,17 @@
         last = i == len(order) - 1
         sums = arrive(step, sums)
         if not last:
-            far[step] = swapped_parts(near[step], devices, 3 if i == 0 else 2)
+            far[step] = swapped_parts(near[step], devices, PARTS)
         else:
             far[step] = swapped(near[step], devices, 1)
+        nexts = step + way
+        if nexts not in near and (nexts, way) in order:
+            near[nexts] = to_next_chip(near[step], devices, way)
         waiting.append((0, step))
         if not last:
             waiting.append((1, step))
         sums = slots_call(waiting, sums, "slots_%d" % i)
         waiting = []
-        nexts = step + way
-        if nexts not in near and (nexts, way) in order:
-            sums = arrive(step, sums)
-            near[nexts] = to_next_chip(near[step], devices, way)
     names = ((1, order[-1][0]),)
     updated = pl.pallas_call(
         functools.partial(finish_kernel, names),

time: 45.8 us -> 41.9 us (0.915)
  the two profiles are of different devices: /device:TPU:28 before, /device:TPU:0 now
where the time goes in v5:
time: 41.9 us; the launch traced here: 41.4 us
  Pallas kernels  14.9 us (36%)
  starting transfers between devices  14.3 us (34%)
  waiting for transfers between devices  11.3 us (27%)
  local copies, waits for them, and re-layouts  0.75 us (2%)
    ppermute x3, starting transfers between devices, to_next_chip(): return lax.ppermute(value, 'node', pairs)  11 us
    pallas_call x3, Pallas kernels, slots_call(): pl.pallas_call(functools.partial(slots_kernel, tuple(names), sizes), out_...  7.87 us
    ppermute x1, waiting for transfers between devices, to_next_segment(): lax.ppermute(value, 'segment', [(s, (s + 1) % count) for s in range(count)])  7.76 us
    pallas_call x1, Pallas kernels, body(): pl.pallas_call(prep_kernel, out_shape=(shape((blocks, pairs, wide, 2 * br...  3.97 us
    ppermute x3, waiting for transfers between devices, to_next_chip(): return lax.ppermute(value, 'node', pairs)  2.53 us
    pallas_call x1, Pallas kernels, body(): pl.pallas_call(functools.partial(finish_kernel, names), out_shape=shape((...  2.14 us
    ppermute x6, starting transfers between devices, swapped(): lax.ppermute(value, 'node', [(d, d ^ distance) for d in range(devices)])  1.69 us
    ppermute x1, starting transfers between devices, to_next_segment(): lax.ppermute(value, 'segment', [(s, (s + 1) % count) for s in range(count)])  1.54 us
  transfers between devices with their start and end apart: 10, of which 3 were waited for; matrix products, arithmetic and copies ran while one was open for 0% of the time, Pallas kernels for 29%

profile of v5, /device:TPU:0, one launch (start us, length us, event | category | flops | bytes accessed | tf_op | source)
XLA Modules:
  0.0 41.4 jit_solution(12407241067591201037)
XLA Ops:
  0.0 1.0 %pack_rows.1.load_ref = bf16[272,512]{1,0:T(8,128)(2,1)S(1)} custom-call(bf16[256,512]{1,0:T(8,128)(2,1)} %bitcast.9, s32[1,256]{1,0:T(1,128)} %bitcast.11), custom_call_target="tpu_custom_call" | custom-call | flops 65536 | bytes 1024 | tf_op jit(solution)/shard_map/pack_rows/pallas_call | solution.py:389
  1.0 3.1 %collective-permute-start = (bf16[272,512]{1,0:T(8,128)(2,1)S(1)}, bf16[272,512]{1,0:T(8,128)(2,1)S(1)}, u32[]{:S(2)}, u32[]{:S(2)}) collective-permute-start(bf16[272,512]{1,0:T(8,128)(2,1)S(1)} %pack_rows.1.load_ref), channel_id=1, source_target_pairs={{0,2},{1,3},{2,6},{3,7},{6,4},{7,5},{4,0},{5,1},{8,10},{9,11},{10,... | collective-permute-start | bytes 835592 | tf_op jit(solution)/shard_map/ppermute | solution.py:39
  4.1 0.0 collective-permute-start.1
  4.1 4.0 %prepare.1 = (bf16[2,4,128,256]{3,2,1,0:T(8,128)(2,1)S(1)}, f32[2,512,128]{2,1,0:T(8,128)S(1)}, f32[2,8,128]{2,1,0:T(8,128)S(1)}, f32[2,4,2,128,128]{4,3,2,1,0:T...) custom-call(bf16[272,512]{1,0:T(8,128)(2,1)S(1)} %pack_rows.1.load_r, ...), custom_call_target="tpu_custom_call" | custom-call | flops 65536 | bytes 1024 | tf_op jit(solution)/shard_map/prepare/pallas_call | solution.py:412
  8.0 1.2 %collective-permute-start.4 = (bf16[272,512]{1,0:T(8,128)(2,1)S(1)}, bf16[272,512]{1,0:T(8,128)(2,1)S(1)}, u32[]{:S(2)}, u32[]{:S(2)}) collective-permute-start(bf16[272,512]{1,0:T(8,128)(2,1)S(1)} %pack_rows.1.load_ref), channel_id=1, source_target_pairs={{0,4},{1,5},{2,0},{3,1},{6,2},{7,3},{4,6},{5,7},{8,12},{9,13},{10,... | collective-permute-start | bytes 835592 | tf_op jit(solution)/shard_map/ppermute | solution.py:39
  9.2 2.5 %collective-permute-done.refs_1_ = bf16[272,512]{1,0:T(8,128)(2,1)S(1)} collective-permute-done((bf16[272,512]{1,0:T(8,128)(2,1)S(1)}, bf16[272,512]{1,0:T(8,128)(2,1)S(1)}, u32[]{:S(2)}, u32[]{:S(2)}) %collective-permute-start) | collective-permute-done | bytes 278560 | tf_op jit(solution)/shard_map/ppermute | solution.py:39
  11.7 0.1 collective-permute-start.2
  11.8 0.6 %collective-permute-start.3 = (bf16[128,512]{1,0:T(8,128)(2,1)S(1)}, bf16[128,512]{1,0:T(8,128)(2,1)S(1)}, u32[]{:S(2)}, u32[]{:S(2)}) collective-permute-start(bf16[128,512]{1,0:T(8,128)(2,1)S(1)} %slice.13), channel_id=1, source_target_pairs={{0,1},{1,0},{2,3},{3,2},{4,5},{5,4},{6,7},{7,6},{8,9},{9,8},{10,11... | collective-permute-start | bytes 393224 | tf_op jit(solution)/shard_map/ppermute | solution.py:43
  12.4 6.8 %collective-permute-start.7 = (bf16[272,512]{1,0:T(8,128)(2,1)S(1)}, bf16[272,512]{1,0:T(8,128)(2,1)S(1)}, u32[]{:S(2)}, u32[]{:S(2)}) collective-permute-start(bf16[272,512]{1,0:T(8,128)(2,1)S(1)} %collective-permute-done.refs_1_), channel_id=1, source_target_pairs={{0,2},{1,3},{2,6},{3,7},{6,4},{7,5},{4,0},{5,1},{8,10},{9,11},{10,... | collective-permute-start | bytes 835592 | tf_op jit(solution)/shard_map/ppermute | solution.py:39
  19.2 0.0 collective-permute-done.3.refs_3_
  19.2 0.0 collective-permute-done.2.refs_2_
  19.2 3.6 %slots_0.1 = (f32[2,512,128]{2,1,0:T(8,128)S(1)}, f32[2,8,128]{2,1,0:T(8,128)S(1)}, f32[32,512]{1,0:T(8,128)S(1)}, f32[32,128]{1,0:T(8,128)S(1)}) custom-call(f32[2,4,8,128]{3,2,1,0:T(8,128)S(1)} %get-tuple-element.38.mask_ref, f32[1,512]{1,0:T(1,128)S(1)} %get-tuple-element.39.gain_ref, bf16[512,512]{1,0:T(8,128)(2,1)S(1)} %get-tuple-element.40.wk_ref, ...), custom_call_target="tpu_custom_call" | custom-call | flops 65536 | bytes 1024 | tf_op jit(solution)/shard_map/slots_0/pallas_call | solution.py:476
  22.8 0.0 collective-permute-done.4.refs_0_
  22.8 0.1 collective-permute-start.5
  22.9 0.6 %collective-permute-start.6 = (bf16[128,512]{1,0:T(8,128)(2,1)S(1)}, bf16[128,512]{1,0:T(8,128)(2,1)S(1)}, u32[]{:S(2)}, u32[]{:S(2)}) collective-permute-start(bf16[128,512]{1,0:T(8,128)(2,1)S(1)} %slice.15), channel_id=1, source_target_pairs={{0,1},{1,0},{2,3},{3,2},{4,5},{5,4},{6,7},{7,6},{8,9},{9,8},{10,11... | collective-permute-start | bytes 393224 | tf_op jit(solution)/shard_map/ppermute | solution.py:43
  23.5 1.0 %collective-permute-done.6.refs_2_ = bf16[128,512]{1,0:T(8,128)(2,1)S(1)} collective-permute-done((bf16[128,512]{1,0:T(8,128)(2,1)S(1)}, bf16[128,512]{1,0:T(8,128)(2,1)S(1)}, u32[]{:S(2)}, u32[]{:S(2)}) %collective-permute-start.6) | collective-permute-done | bytes 131104 | tf_op jit(solution)/shard_map/ppermute | solution.py:43
  24.4 0.0 collective-permute-done.5.refs_1_
  24.4 2.7 %slots_1.1 = (f32[2,512,128]{2,1,0:T(8,128)S(1)}, f32[2,8,128]{2,1,0:T(8,128)S(1)}, f32[32,512]{1,0:T(8,128)S(1)}, f32[32,128]{1,0:T(8,128)S(1)}) custom-call(f32[2,4,8,128]{3,2,1,0:T(8,128)S(1)} %get-tuple-element.38.mask_ref, f32[1,512]{1,0:T(1,128)S(1)} %get-tuple-element.39.gain_ref, bf16[512,512]{1,0:T(8,128)(2,1)S(1)} %get-tuple-element.40.wk_ref, ...), custom_call_target="tpu_custom_call" | custom-call | flops 65536 | bytes 1024 | tf_op jit(solution)/shard_map/slots_1/pallas_call | solution.py:476
  27.1 0.4 %collective-permute-start.8 = (bf16[272,512]{1,0:T(8,128)(2,1)S(1)}, bf16[272,512]{1,0:T(8,128)(2,1)S(1)}, u32[]{:S(2)}, u32[]{:S(2)}) collective-permute-start(bf16[272,512]{1,0:T(8,128)(2,1)S(1)} %collective-permute-done.7.refs_0_), channel_id=1, source_target_pairs={{0,1},{1,0},{2,3},{3,2},{4,5},{5,4},{6,7},{7,6},{8,9},{9,8},{10,11... | collective-permute-start | bytes 835592 | tf_op jit(solution)/shard_map/ppermute | solution.py:43
  27.6 1.6 %slots_2.1 = (f32[2,512,128]{2,1,0:T(8,128)S(1)}, f32[2,8,128]{2,1,0:T(8,128)S(1)}, f32[32,512]{1,0:T(8,128)S(1)}, f32[32,128]{1,0:T(8,128)S(1)}) custom-call(f32[2,4,8,128]{3,2,1,0:T(8,128)S(1)} %get-tuple-element.38.mask_ref, f32[1,512]{1,0:T(1,128)S(1)} %get-tuple-element.39.gain_ref, bf16[512,512]{1,0:T(8,128)(2,1)S(1)} %get-tuple-element.40.wk_ref, ...), custom_call_target="tpu_custom_call" | custom-call | flops 65536 | bytes 1024 | tf_op jit(solution)/shard_map/slots_2/pallas_call | solution.py:476
  29.2 2.1 %finish.1 = bf16[256,512]{1,0:T(8,128)(2,1)S(1)} custom-call(f32[2,4,8,128]{3,2,1,0:T(8,128)S(1)} %get-tuple-element.38.mask_ref, f32[1,512]{1,0:T(1,128)S(1)} %get-tuple-element.39.gain_ref, bf16[512,512]{1,0:T(8,128)(2,1)S(1)} %get-tuple-element.40.wk_ref, bf16[512,512]{1,0:T(8,128)(2,1)S(1)} %get-tuple-element.41.wvt_ref, ...), custom_call_target="tpu_custom_call" | custom-call | flops 65536 | bytes 1024 | tf_op jit(solution)/shard_map/finish/pallas_call | solution.py:513
  31.4 1.5 %collective-permute-start.9 = (bf16[1,256,512]{2,1,0:T(8,128)(2,1)S(1)}, bf16[1,256,512]{2,1,0:T(8,128)(2,1)S(1)}, u32[]{:S(2)}, u32[]{:S(2)}) collective-permute-start(bf16[1,256,512]{2,1,0:T(8,128)(2,1)S(1)} %bitcast.6), channel_id=1, source_target_pairs={{0,8},{8,16},{16,24},{24,0},{1,9},{9,17},{17,25},{25,1},{2,10},{10... | collective-permute-start | bytes 786440 | tf_op jit(solution)/shard_map/ppermute | solution.py:54
  32.9 7.8 %collective-permute-done.9 = bf16[1,256,512]{2,1,0:T(8,128)(2,1)S(1)} collective-permute-done((bf16[1,256,512]{2,1,0:T(8,128)(2,1)S(1)}, bf16[1,256,512]{2,1,0:T(8,128)(2,1)S(1)}, u32[]{:S(2)}, u32[]{:S(2)}) %collective-permute-start.9) | collective-permute-done | bytes 262176 | tf_op jit(solution)/shard_map/ppermute | solution.py:54
  40.7 0.7 %copy.12 = bf16[1,256,512]{2,1,0:T(8,128)(2,1)} copy(bf16[1,256,512]{2,1,0:T(8,128)(2,1)S(1)} %collective-permute-done.9) | data formatting | bytes 524288
  (7 shorter events, 0.1 us)
Async XLA Ops:
  1.0 10.7 %collective-permute-start = (bf16[272,512]{1,0:T(8,128)(2,1)S(1)}, bf16[272,512]{1,0:T(8,128)(2,1)S(1)}, u32[]{:S(2)}, u32[]{:S(2)}) collective-permute-start(bf16[272,512]{1,0:T(8,128)(2,1)S(1)} %pack_rows.1.load_ref), channel_id=1, source_target_pairs={{0,2},{1,3},{2,6},{3,7},{6,4},{7,5},{4,0},{5,1},{8,10},{9,11},{10,... | collective-permute-start | bytes 835592 | tf_op jit(solution)/shard_map/ppermute | solution.py:39
  4.1 15.1 %collective-permute-start.1 = (bf16[272,512]{1,0:T(8,128)(2,1)S(1)}, bf16[272,512]{1,0:T(8,128)(2,1)S(1)}, u32[]{:S(2)}, u32[]{:S(2)}) collective-permute-start(bf16[272,512]{1,0:T(8,128)(2,1)S(1)} %pack_rows.1.load_ref), channel_id=1, source_target_pairs={{0,1},{1,0},{2,3},{3,2},{4,5},{5,4},{6,7},{7,6},{8,9},{9,8},{10,11... | collective-permute-start | bytes 835592 | tf_op jit(solution)/shard_map/ppermute | solution.py:43
  8.0 14.7 %collective-permute-start.4 = (bf16[272,512]{1,0:T(8,128)(2,1)S(1)}, bf16[272,512]{1,0:T(8,128)(2,1)S(1)}, u32[]{:S(2)}, u32[]{:S(2)}) collective-permute-start(bf16[272,512]{1,0:T(8,128)(2,1)S(1)} %pack_rows.1.load_ref), channel_id=1, source_target_pairs={{0,4},{1,5},{2,0},{3,1},{6,2},{7,3},{4,6},{5,7},{8,12},{9,13},{10,... | collective-permute-start | bytes 835592 | tf_op jit(solution)/shard_map/ppermute | solution.py:39
  11.7 7.5 %collective-permute-start.2 = (bf16[144,512]{1,0:T(8,128)(2,1)S(1)}, bf16[144,512]{1,0:T(8,128)(2,1)S(1)}, u32[]{:S(2)}, u32[]{:S(2)}) collective-permute-start(bf16[144,512]{1,0:T(8,128)(2,1)S(1)} %slice.12), channel_id=1, source_target_pairs={{0,1},{1,0},{2,3},{3,2},{4,5},{5,4},{6,7},{7,6},{8,9},{9,8},{10,11... | collective-permute-start | bytes 442376 | tf_op jit(solution)/shard_map/ppermute | solution.py:43
  11.8 7.4 %collective-permute-start.3 = (bf16[128,512]{1,0:T(8,128)(2,1)S(1)}, bf16[128,512]{1,0:T(8,128)(2,1)S(1)}, u32[]{:S(2)}, u32[]{:S(2)}) collective-permute-start(bf16[128,512]{1,0:T(8,128)(2,1)S(1)} %slice.13), channel_id=1, source_target_pairs={{0,1},{1,0},{2,3},{3,2},{4,5},{5,4},{6,7},{7,6},{8,9},{9,8},{10,11... | collective-permute-start | bytes 393224 | tf_op jit(solution)/shard_map/ppermute | solution.py:43
  12.4 14.7 %collective-permute-start.7 = (bf16[272,512]{1,0:T(8,128)(2,1)S(1)}, bf16[272,512]{1,0:T(8,128)(2,1)S(1)}, u32[]{:S(2)}, u32[]{:S(2)}) collective-permute-start(bf16[272,512]{1,0:T(8,128)(2,1)S(1)} %collective-permute-done.refs_1_), channel_id=1, source_target_pairs={{0,2},{1,3},{2,6},{3,7},{6,4},{7,5},{4,0},{5,1},{8,10},{9,11},{10,... | collective-permute-start | bytes 835592 | tf_op jit(solution)/shard_map/ppermute | solution.py:39
  22.8 1.6 %collective-permute-start.5 = (bf16[144,512]{1,0:T(8,128)(2,1)S(1)}, bf16[144,512]{1,0:T(8,128)(2,1)S(1)}, u32[]{:S(2)}, u32[]{:S(2)}) collective-permute-start(bf16[144,512]{1,0:T(8,128)(2,1)S(1)} %slice.14), channel_id=1, source_target_pairs={{0,1},{1,0},{2,3},{3,2},{4,5},{5,4},{6,7},{7,6},{8,9},{9,8},{10,11... | collective-permute-start | bytes 442376 | tf_op jit(solution)/shard_map/ppermute | solution.py:43
  22.9 1.5 %collective-permute-start.6 = (bf16[128,512]{1,0:T(8,128)(2,1)S(1)}, bf16[128,512]{1,0:T(8,128)(2,1)S(1)}, u32[]{:S(2)}, u32[]{:S(2)}) collective-permute-start(bf16[128,512]{1,0:T(8,128)(2,1)S(1)} %slice.15), channel_id=1, source_target_pairs={{0,1},{1,0},{2,3},{3,2},{4,5},{5,4},{6,7},{7,6},{8,9},{9,8},{10,11... | collective-permute-start | bytes 393224 | tf_op jit(solution)/shard_map/ppermute | solution.py:43
  27.1 2.1 %collective-permute-start.8 = (bf16[272,512]{1,0:T(8,128)(2,1)S(1)}, bf16[272,512]{1,0:T(8,128)(2,1)S(1)}, u32[]{:S(2)}, u32[]{:S(2)}) collective-permute-start(bf16[272,512]{1,0:T(8,128)(2,1)S(1)} %collective-permute-done.7.refs_0_), channel_id=1, source_target_pairs={{0,1},{1,0},{2,3},{3,2},{4,5},{5,4},{6,7},{7,6},{8,9},{9,8},{10,11... | collective-permute-start | bytes 835592 | tf_op jit(solution)/shard_map/ppermute | solution.py:43
  31.4 9.3 %collective-permute-start.9 = (bf16[1,256,512]{2,1,0:T(8,128)(2,1)S(1)}, bf16[1,256,512]{2,1,0:T(8,128)(2,1)S(1)}, u32[]{:S(2)}, u32[]{:S(2)}) collective-permute-start(bf16[1,256,512]{2,1,0:T(8,128)(2,1)S(1)} %bitcast.6), channel_id=1, source_target_pairs={{0,8},{8,16},{16,24},{24,0},{1,9},{9,17},{17,25},{25,1},{2,10},{10... | collective-permute-start | bytes 786440 | tf_op jit(solution)/shard_map/ppermute | solution.py:54

commit v6 on v5

--- a/solution.py
+++ b/solution.py
@@ -493,22 +493,30 @@
         order.append((s, 1))
         if s < chips - s:
             order.append((chips - s, -1))
-    waiting = [(1, 0)]
-    for i, (step, way) in enumerate(order):
-        last = i == len(order) - 1
-        sums = arrive(step, sums)
-        if not last:
-            far[step] = swapped_parts(near[step], devices, PARTS)
-        else:
-            far[step] = swapped(near[step], devices, 1)
+    sums = slots_call([(1, 0)], sums, "slots_own")
+
+    def hop_on(step, way):
         nexts = step + way
         if nexts not in near and (nexts, way) in order:
             near[nexts] = to_next_chip(near[step], devices, way)
-        waiting.append((0, step))
-        if not last:
-            waiting.append((1, step))
-        sums = slots_call(waiting, sums, "slots_%d" % i)
-        waiting = []
+
+    firsts = order[:-1][:2]
+    for step, way in firsts:
+        sums = arrive(step, sums)
+        hop_on(step, way)
+    for step, _ in firsts:
+        far[step] = swapped_parts(near[step], devices, PARTS)
+    if firsts:
+        sums = slots_call([(0, step) for step, _ in firsts], sums, "slots_near")
+        sums = slots_call([(1, step) for step, _ in firsts], sums, "slots_far")
+    for i, (step, way) in enumerate(order[len(firsts) :]):
+        sums = arrive(step, sums)
+        hop_on(step, way)
+        far[step] = swapped(near[step], devices, 1)
+        names = [(0, step), (1, step)]
+        if step == order[-1][0]:
+            names = names[:1]
+        sums = slots_call(names, sums, "slots_%d" % i)
     names = ((1, order[-1][0]),)
     updated = pl.pallas_call(
         functools.partial(finish_kernel, names),

time: 41.9 us -> 40.7 us (0.971)
  waiting for transfers between devices: 11.3 us -> 9.7 us
  Pallas kernels: 14.9 us -> 15.7 us
  starting transfers between devices: 14.3 us -> 13.8 us
    ppermute x6, waiting for transfers between devices: 1 us -> 0.02 us  [swapped(): lax.ppermute(value, 'node', [(d, d ^ distance) for d in range(devices)])]
    ppermute x3, waiting for transfers between devices: 2.53 us -> 1.62 us  [to_next_chip(): return lax.ppermute(value, 'node', pairs)]
    pallas_call x3 -> x4, Pallas kernels: 7.87 us -> 8.66 us  [slots_call(): pl.pallas_call(functools.partial(slots_kernel, tuple(names), sizes), out_...]
    ppermute x3, starting transfers between devices: 11 us -> 10.5 us  [to_next_chip(): return lax.ppermute(value, 'node', pairs)]
  transfers between devices with their start and end apart: 10 -> 10, of which waited for: 3 -> 2; matrix products, arithmetic and copies ran while one was open for 0% -> 0% of each run, Pallas kernels for 29% -> 31%
where the time goes in v6:
time: 40.7 us; the launch traced here: 40.1 us
  Pallas kernels  15.7 us (39%)
  starting transfers between devices  13.8 us (34%)
  waiting for transfers between devices  9.7 us (24%)
  local copies, waits for them, and re-layouts  0.74 us (2%)
    ppermute x3, starting transfers between devices, to_next_chip(): return lax.ppermute(value, 'node', pairs)  10.5 us
    pallas_call x4, Pallas kernels, slots_call(): pl.pallas_call(functools.partial(slots_kernel, tuple(names), sizes), out_...  8.66 us
    ppermute x1, waiting for transfers between devices, to_next_segment(): lax.ppermute(value, 'segment', [(s, (s + 1) % count) for s in range(count)])  8.06 us
    pallas_call x1, Pallas kernels, body(): pl.pallas_call(prep_kernel, out_shape=(shape((blocks, pairs, wide, 2 * br...  3.97 us
    pallas_call x1, Pallas kernels, body(): pl.pallas_call(functools.partial(finish_kernel, names), out_shape=shape((...  2.14 us
    ppermute x6, starting transfers between devices, swapped(): lax.ppermute(value, 'node', [(d, d ^ distance) for d in range(devices)])  1.82 us
    ppermute x3, waiting for transfers between devices, to_next_chip(): return lax.ppermute(value, 'node', pairs)  1.62 us
    ppermute x1, starting transfers between devices, to_next_segment(): lax.ppermute(value, 'segment', [(s, (s + 1) % count) for s in range(count)])  1.53 us
  transfers between devices with their start and end apart: 10, of which 2 were waited for; matrix products, arithmetic and copies ran while one was open for 0% of the time, Pallas kernels for 31%

profile of v6, /device:TPU:0, one launch (start us, length us, event | category | flops | bytes accessed | tf_op | source)
XLA Modules:
  0.0 40.1 jit_solution(1702630765420996929)
XLA Ops:
  0.0 1.0 %pack_rows.1.load_ref = bf16[272,512]{1,0:T(8,128)(2,1)S(1)} custom-call(bf16[256,512]{1,0:T(8,128)(2,1)} %bitcast.9, s32[1,256]{1,0:T(1,128)} %bitcast.11), custom_call_target="tpu_custom_call" | custom-call | flops 65536 | bytes 1024 | tf_op jit(solution)/shard_map/pack_rows/pallas_call | solution.py:389
  1.0 0.5 %collective-permute-start = (bf16[272,512]{1,0:T(8,128)(2,1)S(1)}, bf16[272,512]{1,0:T(8,128)(2,1)S(1)}, u32[]{:S(2)}, u32[]{:S(2)}) collective-permute-start(bf16[272,512]{1,0:T(8,128)(2,1)S(1)} %pack_rows.1.load_ref), channel_id=1, source_target_pairs={{0,1},{1,0},{2,3},{3,2},{4,5},{5,4},{6,7},{7,6},{8,9},{9,8},{10,11... | collective-permute-start | bytes 835592 | tf_op jit(solution)/shard_map/ppermute | solution.py:43
  1.5 2.6 %collective-permute-start.2 = (bf16[272,512]{1,0:T(8,128)(2,1)S(1)}, bf16[272,512]{1,0:T(8,128)(2,1)S(1)}, u32[]{:S(2)}, u32[]{:S(2)}) collective-permute-start(bf16[272,512]{1,0:T(8,128)(2,1)S(1)} %pack_rows.1.load_ref), channel_id=1, source_target_pairs={{0,2},{1,3},{2,6},{3,7},{6,4},{7,5},{4,0},{5,1},{8,10},{9,11},{10,... | collective-permute-start | bytes 835592 | tf_op jit(solution)/shard_map/ppermute | solution.py:39
  4.1 4.0 %prepare.1 = (bf16[2,4,128,256]{3,2,1,0:T(8,128)(2,1)S(1)}, f32[2,512,128]{2,1,0:T(8,128)S(1)}, f32[2,8,128]{2,1,0:T(8,128)S(1)}, f32[2,4,2,128,128]{4,3,2,1,0:T...) custom-call(bf16[272,512]{1,0:T(8,128)(2,1)S(1)} %pack_rows.1.load_r, ...), custom_call_target="tpu_custom_call" | custom-call | flops 65536 | bytes 1024 | tf_op jit(solution)/shard_map/prepare/pallas_call | solution.py:412
  8.1 1.1 %collective-permute-start.1 = (bf16[272,512]{1,0:T(8,128)(2,1)S(1)}, bf16[272,512]{1,0:T(8,128)(2,1)S(1)}, u32[]{:S(2)}, u32[]{:S(2)}) collective-permute-start(bf16[272,512]{1,0:T(8,128)(2,1)S(1)} %pack_rows.1.load_ref), channel_id=1, source_target_pairs={{0,4},{1,5},{2,0},{3,1},{6,2},{7,3},{4,6},{5,7},{8,12},{9,13},{10,... | collective-permute-start | bytes 835592 | tf_op jit(solution)/shard_map/ppermute | solution.py:39
  9.2 0.0 collective-permute-done.refs_0_
  9.2 1.6 %slots_own.1 = (f32[2,512,128]{2,1,0:T(8,128)S(1)}, f32[2,8,128]{2,1,0:T(8,128)S(1)}, f32[32,512]{1,0:T(8,128)S(1)}, f32[32,128]{1,0:T(8,128)S(1)}) custom-call(f32[2,4,8,128]{3,2,1,0:T(8,128)S(1)} %get-tuple-element.42.mask_ref, f32[1,512]{1,0:T(1,128)S(1)} %get-tuple-element.43.gain_ref, bf16[512,512]{1,0:T(8,128)(2,1)S(1)} %get-tuple-element.44.wk_ref, ...), custom_call_target="tpu_custom_call" | custom-call | flops 65536 | bytes 1024 | tf_op jit(solution)/shard_map/slots_own/pallas_call | solution.py:476
  10.9 1.6 %collective-permute-done.2.refs_0_ = bf16[272,512]{1,0:T(8,128)(2,1)S(1)} collective-permute-done((bf16[272,512]{1,0:T(8,128)(2,1)S(1)}, bf16[272,512]{1,0:T(8,128)(2,1)S(1)}, u32[]{:S(2)}, u32[]{:S(2)}) %collective-permute-start.2) | collective-permute-done | bytes 278560 | tf_op jit(solution)/shard_map/ppermute | solution.py:39
  12.5 6.7 %collective-permute-start.7 = (bf16[272,512]{1,0:T(8,128)(2,1)S(1)}, bf16[272,512]{1,0:T(8,128)(2,1)S(1)}, u32[]{:S(2)}, u32[]{:S(2)}) collective-permute-start(bf16[272,512]{1,0:T(8,128)(2,1)S(1)} %collective-permute-done.2.refs_0_), channel_id=1, source_target_pairs={{0,2},{1,3},{2,6},{3,7},{6,4},{7,5},{4,0},{5,1},{8,10},{9,11},{10,... | collective-permute-start | bytes 835592 | tf_op jit(solution)/shard_map/ppermute | solution.py:39
  19.2 0.0 collective-permute-done.1.refs_1_
  19.3 0.1 collective-permute-start.5
  19.3 0.5 %collective-permute-start.3 = (bf16[144,512]{1,0:T(8,128)(2,1)S(1)}, bf16[144,512]{1,0:T(8,128)(2,1)S(1)}, u32[]{:S(2)}, u32[]{:S(2)}) collective-permute-start(bf16[144,512]{1,0:T(8,128)(2,1)S(1)} %slice.12), channel_id=1, source_target_pairs={{0,1},{1,0},{2,3},{3,2},{4,5},{5,4},{6,7},{7,6},{8,9},{9,8},{10,11... | collective-permute-start | bytes 442376 | tf_op jit(solution)/shard_map/ppermute | solution.py:43
  19.9 0.1 collective-permute-start.6
  20.0 0.4 %collective-permute-start.4 = (bf16[128,512]{1,0:T(8,128)(2,1)S(1)}, bf16[128,512]{1,0:T(8,128)(2,1)S(1)}, u32[]{:S(2)}, u32[]{:S(2)}) collective-permute-start(bf16[128,512]{1,0:T(8,128)(2,1)S(1)} %slice.13), channel_id=1, source_target_pairs={{0,1},{1,0},{2,3},{3,2},{4,5},{5,4},{6,7},{7,6},{8,9},{9,8},{10,11... | collective-permute-start | bytes 393224 | tf_op jit(solution)/shard_map/ppermute | solution.py:43
  20.4 2.7 %slots_near.1 = (f32[2,512,128]{2,1,0:T(8,128)S(1)}, f32[2,8,128]{2,1,0:T(8,128)S(1)}, f32[32,512]{1,0:T(8,128)S(1)}, f32[32,128]{1,0:T(8,128)S(1)}) custom-call(f32[2,4,8,128]{3,2,1,0:T(8,128)S(1)} %get-tuple-element.42.mask_ref, f32[1,512]{1,0:T(1,128)S(1)} %get-tuple-element.43.gain_ref, bf16[512,512]{1,0:T(8,128)(2,1)S(1)} %get-tuple-element.44.wk_ref, ...), custom_call_target="tpu_custom_call" | custom-call | flops 65536 | bytes 1024 | tf_op jit(solution)/shard_map/slots_near/pallas_call | solution.py:476
  23.2 0.0 collective-permute-done.5.refs_2_
  23.2 2.7 %slots_far.1 = (f32[2,512,128]{2,1,0:T(8,128)S(1)}, f32[2,8,128]{2,1,0:T(8,128)S(1)}, f32[32,512]{1,0:T(8,128)S(1)}, f32[32,128]{1,0:T(8,128)S(1)}) custom-call(f32[2,4,8,128]{3,2,1,0:T(8,128)S(1)} %get-tuple-element.42.mask_ref, f32[1,512]{1,0:T(1,128)S(1)} %get-tuple-element.43.gain_ref, bf16[512,512]{1,0:T(8,128)(2,1)S(1)} %get-tuple-element.44.wk_ref, ...), custom_call_target="tpu_custom_call" | custom-call | flops 65536 | bytes 1024 | tf_op jit(solution)/shard_map/slots_far/pallas_call | solution.py:476
  25.9 0.2 collective-permute-start.8
  26.0 1.7 %slots_0.1 = (f32[2,512,128]{2,1,0:T(8,128)S(1)}, f32[2,8,128]{2,1,0:T(8,128)S(1)}, f32[32,512]{1,0:T(8,128)S(1)}, f32[32,128]{1,0:T(8,128)S(1)}) custom-call(f32[2,4,8,128]{3,2,1,0:T(8,128)S(1)} %get-tuple-element.42.mask_ref, f32[1,512]{1,0:T(1,128)S(1)} %get-tuple-element.43.gain_ref, bf16[512,512]{1,0:T(8,128)(2,1)S(1)} %get-tuple-element.44.wk_ref, ...), custom_call_target="tpu_custom_call" | custom-call | flops 65536 | bytes 1024 | tf_op jit(solution)/shard_map/slots_0/pallas_call | solution.py:476
  27.7 0.0 collective-permute-done.8.last_ref
  27.7 2.1 %finish.1 = bf16[256,512]{1,0:T(8,128)(2,1)S(1)} custom-call(f32[2,4,8,128]{3,2,1,0:T(8,128)S(1)} %get-tuple-element.42.mask_ref, f32[1,512]{1,0:T(1,128)S(1)} %get-tuple-element.43.gain_ref, bf16[512,512]{1,0:T(8,128)(2,1)S(1)} %get-tuple-element.44.wk_ref, bf16[512,512]{1,0:T(8,128)(2,1)S(1)} %get-tuple-element.45.wvt_ref, ...), custom_call_target="tpu_custom_call" | custom-call | flops 65536 | bytes 1024 | tf_op jit(solution)/shard_map/finish/pallas_call | solution.py:521
  29.8 1.5 %collective-permute-start.9 = (bf16[1,256,512]{2,1,0:T(8,128)(2,1)S(1)}, bf16[1,256,512]{2,1,0:T(8,128)(2,1)S(1)}, u32[]{:S(2)}, u32[]{:S(2)}) collective-permute-start(bf16[1,256,512]{2,1,0:T(8,128)(2,1)S(1)} %bitcast.6), channel_id=1, source_target_pairs={{0,8},{8,16},{16,24},{24,0},{1,9},{9,17},{17,25},{25,1},{2,10},{10... | collective-permute-start | bytes 786440 | tf_op jit(solution)/shard_map/ppermute | solution.py:54
  31.4 8.1 %collective-permute-done.9 = bf16[1,256,512]{2,1,0:T(8,128)(2,1)S(1)} collective-permute-done((bf16[1,256,512]{2,1,0:T(8,128)(2,1)S(1)}, bf16[1,256,512]{2,1,0:T(8,128)(2,1)S(1)}, u32[]{:S(2)}, u32[]{:S(2)}) %collective-permute-start.9) | collective-permute-done | bytes 262176 | tf_op jit(solution)/shard_map/ppermute | solution.py:54
  39.4 0.7 %copy.12 = bf16[1,256,512]{2,1,0:T(8,128)(2,1)} copy(bf16[1,256,512]{2,1,0:T(8,128)(2,1)S(1)} %collective-permute-done.9) | data formatting | bytes 524288
  (8 shorter events, 0.1 us)
Async XLA Ops:
  1.0 8.2 %collective-permute-start = (bf16[272,512]{1,0:T(8,128)(2,1)S(1)}, bf16[272,512]{1,0:T(8,128)(2,1)S(1)}, u32[]{:S(2)}, u32[]{:S(2)}) collective-permute-start(bf16[272,512]{1,0:T(8,128)(2,1)S(1)} %pack_rows.1.load_ref), channel_id=1, source_target_pairs={{0,1},{1,0},{2,3},{3,2},{4,5},{5,4},{6,7},{7,6},{8,9},{9,8},{10,11... | collective-permute-start | bytes 835592 | tf_op jit(solution)/shard_map/ppermute | solution.py:43
  1.5 11.0 %collective-permute-start.2 = (bf16[272,512]{1,0:T(8,128)(2,1)S(1)}, bf16[272,512]{1,0:T(8,128)(2,1)S(1)}, u32[]{:S(2)}, u32[]{:S(2)}) collective-permute-start(bf16[272,512]{1,0:T(8,128)(2,1)S(1)} %pack_rows.1.load_ref), channel_id=1, source_target_pairs={{0,2},{1,3},{2,6},{3,7},{6,4},{7,5},{4,0},{5,1},{8,10},{9,11},{10,... | collective-permute-start | bytes 835592 | tf_op jit(solution)/shard_map/ppermute | solution.py:39
  8.1 11.1 %collective-permute-start.1 = (bf16[272,512]{1,0:T(8,128)(2,1)S(1)}, bf16[272,512]{1,0:T(8,128)(2,1)S(1)}, u32[]{:S(2)}, u32[]{:S(2)}) collective-permute-start(bf16[272,512]{1,0:T(8,128)(2,1)S(1)} %pack_rows.1.load_ref), channel_id=1, source_target_pairs={{0,4},{1,5},{2,0},{3,1},{6,2},{7,3},{4,6},{5,7},{8,12},{9,13},{10,... | collective-permute-start | bytes 835592 | tf_op jit(solution)/shard_map/ppermute | solution.py:39
  12.5 13.4 %collective-permute-start.7 = (bf16[272,512]{1,0:T(8,128)(2,1)S(1)}, bf16[272,512]{1,0:T(8,128)(2,1)S(1)}, u32[]{:S(2)}, u32[]{:S(2)}) collective-permute-start(bf16[272,512]{1,0:T(8,128)(2,1)S(1)} %collective-permute-done.2.refs_0_), channel_id=1, source_target_pairs={{0,2},{1,3},{2,6},{3,7},{6,4},{7,5},{4,0},{5,1},{8,10},{9,11},{10,... | collective-permute-start | bytes 835592 | tf_op jit(solution)/shard_map/ppermute | solution.py:39
  19.3 3.9 %collective-permute-start.5 = (bf16[144,512]{1,0:T(8,128)(2,1)S(1)}, bf16[144,512]{1,0:T(8,128)(2,1)S(1)}, u32[]{:S(2)}, u32[]{:S(2)}) collective-permute-start(bf16[144,512]{1,0:T(8,128)(2,1)S(1)} %slice.14), channel_id=1, source_target_pairs={{0,1},{1,0},{2,3},{3,2},{4,5},{5,4},{6,7},{7,6},{8,9},{9,8},{10,11... | collective-permute-start | bytes 442376 | tf_op jit(solution)/shard_map/ppermute | solution.py:43
  19.3 3.8 %collective-permute-start.3 = (bf16[144,512]{1,0:T(8,128)(2,1)S(1)}, bf16[144,512]{1,0:T(8,128)(2,1)S(1)}, u32[]{:S(2)}, u32[]{:S(2)}) collective-permute-start(bf16[144,512]{1,0:T(8,128)(2,1)S(1)} %slice.12), channel_id=1, source_target_pairs={{0,1},{1,0},{2,3},{3,2},{4,5},{5,4},{6,7},{7,6},{8,9},{9,8},{10,11... | collective-permute-start | bytes 442376 | tf_op jit(solution)/shard_map/ppermute | solution.py:43
  19.9 3.3 %collective-permute-start.6 = (bf16[128,512]{1,0:T(8,128)(2,1)S(1)}, bf16[128,512]{1,0:T(8,128)(2,1)S(1)}, u32[]{:S(2)}, u32[]{:S(2)}) collective-permute-start(bf16[128,512]{1,0:T(8,128)(2,1)S(1)} %slice.15), channel_id=1, source_target_pairs={{0,1},{1,0},{2,3},{3,2},{4,5},{5,4},{6,7},{7,6},{8,9},{9,8},{10,11... | collective-permute-start | bytes 393224 | tf_op jit(solution)/shard_map/ppermute | solution.py:43
  20.0 3.1 %collective-permute-start.4 = (bf16[128,512]{1,0:T(8,128)(2,1)S(1)}, bf16[128,512]{1,0:T(8,128)(2,1)S(1)}, u32[]{:S(2)}, u32[]{:S(2)}) collective-permute-start(bf16[128,512]{1,0:T(8,128)(2,1)S(1)} %slice.13), channel_id=1, source_target_pairs={{0,1},{1,0},{2,3},{3,2},{4,5},{5,4},{6,7},{7,6},{8,9},{9,8},{10,11... | collective-permute-start | bytes 393224 | tf_op jit(solution)/shard_map/ppermute | solution.py:43
  25.9 1.8 %collective-permute-start.8 = (bf16[272,512]{1,0:T(8,128)(2,1)S(1)}, bf16[272,512]{1,0:T(8,128)(2,1)S(1)}, u32[]{:S(2)}, u32[]{:S(2)}) collective-permute-start(bf16[272,512]{1,0:T(8,128)(2,1)S(1)} %collective-permute-done.7.refs_0_), channel_id=1, source_target_pairs={{0,1},{1,0},{2,3},{3,2},{4,5},{5,4},{6,7},{7,6},{8,9},{9,8},{10,11... | collective-permute-start | bytes 835592 | tf_op jit(solution)/shard_map/ppermute | solution.py:43
  29.8 9.6 %collective-permute-start.9 = (bf16[1,256,512]{2,1,0:T(8,128)(2,1)S(1)}, bf16[1,256,512]{2,1,0:T(8,128)(2,1)S(1)}, u32[]{:S(2)}, u32[]{:S(2)}) collective-permute-start(bf16[1,256,512]{2,1,0:T(8,128)(2,1)S(1)} %bitcast.6), channel_id=1, source_target_pairs={{0,8},{8,16},{16,24},{24,0},{1,9},{9,17},{17,25},{25,1},{2,10},{10... | collective-permute-start | bytes 786440 | tf_op jit(solution)/shard_map/ppermute | solution.py:54

commit v7 on v5

--- a/solution.py
+++ b/solution.py
@@ -399,8 +399,8 @@
         pltpu.with_memory_space_constraint(activations[0], pltpu.HBM),
         pltpu.with_memory_space_constraint(virtual_id.reshape(1, rows), pltpu.HBM),
     )
-    near = {1: to_next_chip(load, devices, 1)}
-    far = {0: swapped(load, devices, 1)}
+    near = {1: [to_next_chip(load, devices, 1)]}
+    far = {0: [swapped(load, devices, 1)]}
 
     accumulators = (
         shape((blocks, width, br), F32),
@@ -460,18 +460,19 @@
             pltpu.VMEM((width, count * br), BF16),
         ]
 
+    sums = (num, den, pool, weight)
+
+    def tie(values, sums):
+        *values, first = after((*values, sums[1]))
+        return values, (sums[0], first) + sums[2:]
+
+    cut = 16 * ((rows + EXTRA) // 32)
     if chips > 2:
-        back, den = after((load, den))
-        near[chips - 1] = to_next_chip(back, devices, -1)
-    sums = (num, den, pool, weight)
-
-    def arrive(step, sums):
-        near[step], first = after((near[step], sums[1]))
-        return (sums[0], first) + sums[2:]
+        (early,), sums = tie([load[:cut]], sums)
+        early = to_next_chip(early, devices, -1)
 
     def slots_call(names, sums, name):
         loads = [(far if other else near)[step] for other, step in names]
-        loads = [load if isinstance(load, list) else [load] for load in loads]
         sizes = tuple(len(load) for load in loads)
         return pl.pallas_call(
             functools.partial(slots_kernel, tuple(names), sizes),
@@ -493,22 +494,27 @@
         order.append((s, 1))
         if s < chips - s:
             order.append((chips - s, -1))
-    waiting = [(1, 0)]
+    sums = slots_call([(1, 0)], sums, "slots_own")
+
     for i, (step, way) in enumerate(order):
         last = i == len(order) - 1
-        sums = arrive(step, sums)
-        if not last:
-            far[step] = swapped_parts(near[step], devices, PARTS)
+        tied = list(near[step])
+        if i == 0 and chips > 2:
+            (late, early, *tied), sums = tie([load[cut:], early] + tied, sums)
+            near[chips - 1] = [early, to_next_chip(late, devices, -1)]
         else:
-            far[step] = swapped(near[step], devices, 1)
-        nexts = step + way
-        if nexts not in near and (nexts, way) in order:
-            near[nexts] = to_next_chip(near[step], devices, way)
-        waiting.append((0, step))
-        if not last:
-            waiting.append((1, step))
-        sums = slots_call(waiting, sums, "slots_%d" % i)
-        waiting = []
+            tied, sums = tie(tied, sums)
+        near[step] = tied
+        if step + way not in near and (step + way, way) in order:
+            near[step + way] = [to_next_chip(piece, devices, way) for piece in tied]
+        if last:
+            far[step] = [swapped(piece, devices, 1) for piece in tied]
+        elif len(tied) == 1:
+            far[step] = swapped_parts(tied[0], devices, PARTS)
+        else:
+            far[step] = [swapped(piece, devices, 1) for piece in tied]
+        names = [(0, step)] if last else [(0, step), (1, step)]
+        sums = slots_call(names, sums, "slots_%d" % i)
     names = ((1, order[-1][0]),)
     updated = pl.pallas_call(
         functools.partial(finish_kernel, names),
@@ -520,7 +526,7 @@
         cost_estimate=cost(unit),
         name="finish",
     )(
-        mask, gain, wk, wvt, vkw, counts, qbd, *sums, far[names[0][1]], vcol, load, wo
+        mask, gain, wk, wvt, vkw, counts, qbd, *sums, *far[names[0][1]], vcol, load, wo
     )
     return to_next_segment(updated[None])
 

time: 41.9 us -> 44.8 us (1.069)
  waiting for transfers between devices: 11.3 us -> 18.5 us
  starting transfers between devices: 14.3 us -> 9.01 us
  Pallas kernels: 14.9 us -> 15.7 us
    ppermute x3 -> x4, waiting for transfers between devices: 2.53 us -> 8.76 us  [to_next_chip(): return lax.ppermute(value, 'node', pairs)]
    ppermute x3 -> x4, starting transfers between devices: 11 us -> 6.02 us  [to_next_chip(): return lax.ppermute(value, 'node', pairs)]
    pallas_call x3 -> x4, Pallas kernels: 7.87 us -> 8.64 us  [slots_call(): pl.pallas_call(functools.partial(slots_kernel, tuple(names), sizes), out_...]
    ppermute x6, waiting for transfers between devices: 1 us -> 1.67 us  [swapped(): lax.ppermute(value, 'node', [(d, d ^ distance) for d in range(devices)])]
  transfers between devices with their start and end apart: 10 -> 11, of which waited for: 3 -> 6; matrix products, arithmetic and copies ran while one was open for 0% -> 0% of each run, Pallas kernels for 29% -> 29%
where the time goes in v7:
time: 44.8 us; the launch traced here: 44.1 us
  waiting for transfers between devices  18.5 us (41%)
  Pallas kernels  15.7 us (35%)
  starting transfers between devices  9.01 us (20%)
  local copies, waits for them, and re-layouts  0.74 us (2%)
    ppermute x4, waiting for transfers between devices, to_next_chip(): return lax.ppermute(value, 'node', pairs)  8.76 us
    pallas_call x4, Pallas kernels, slots_call(): pl.pallas_call(functools.partial(slots_kernel, tuple(names), sizes), out_...  8.64 us
    ppermute x1, waiting for transfers between devices, to_next_segment(): lax.ppermute(value, 'segment', [(s, (s + 1) % count) for s in range(count)])  8.07 us
    ppermute x4, starting transfers between devices, to_next_chip(): return lax.ppermute(value, 'node', pairs)  6.02 us
    pallas_call x1, Pallas kernels, body(): pl.pallas_call(prep_kernel, out_shape=(shape((blocks, pairs, wide, 2 * br...  3.97 us
    pallas_call x1, Pallas kernels, body(): pl.pallas_call(functools.partial(finish_kernel, names), out_shape=shape((...  2.14 us
    ppermute x6, waiting for transfers between devices, swapped(): lax.ppermute(value, 'node', [(d, d ^ distance) for d in range(devices)])  1.67 us
    ppermute x1, starting transfers between devices, to_next_segment(): lax.ppermute(value, 'segment', [(s, (s + 1) % count) for s in range(count)])  1.55 us
  transfers between devices with their start and end apart: 11, of which 6 were waited for; matrix products, arithmetic and copies ran while one was open for 0% of the time, Pallas kernels for 29%

profile of v7, /device:TPU:0, one launch (start us, length us, event | category | flops | bytes accessed | tf_op | source)
XLA Modules:
  0.0 44.1 jit_solution(9384474595453675588)
XLA Ops:
  0.0 1.0 %pack_rows.1.load_ref = bf16[272,512]{1,0:T(8,128)(2,1)S(1)} custom-call(bf16[256,512]{1,0:T(8,128)(2,1)} %bitcast.9, s32[1,256]{1,0:T(1,128)} %bitcast.11), custom_call_target="tpu_custom_call" | custom-call | flops 65536 | bytes 1024 | tf_op jit(solution)/shard_map/pack_rows/pallas_call | solution.py:389
  1.0 0.5 %collective-permute-start = (bf16[272,512]{1,0:T(8,128)(2,1)S(1)}, bf16[272,512]{1,0:T(8,128)(2,1)S(1)}, u32[]{:S(2)}, u32[]{:S(2)}) collective-permute-start(bf16[272,512]{1,0:T(8,128)(2,1)S(1)} %pack_rows.1.load_ref), channel_id=1, source_target_pairs={{0,1},{1,0},{2,3},{3,2},{4,5},{5,4},{6,7},{7,6},{8,9},{9,8},{10,11... | collective-permute-start | bytes 835592 | tf_op jit(solution)/shard_map/ppermute | solution.py:43
  1.5 2.6 %collective-permute-start.2 = (bf16[272,512]{1,0:T(8,128)(2,1)S(1)}, bf16[272,512]{1,0:T(8,128)(2,1)S(1)}, u32[]{:S(2)}, u32[]{:S(2)}) collective-permute-start(bf16[272,512]{1,0:T(8,128)(2,1)S(1)} %pack_rows.1.load_ref), channel_id=1, source_target_pairs={{0,2},{1,3},{2,6},{3,7},{6,4},{7,5},{4,0},{5,1},{8,10},{9,11},{10,... | collective-permute-start | bytes 835592 | tf_op jit(solution)/shard_map/ppermute | solution.py:39
  4.1 4.0 %prepare.1 = (bf16[2,4,128,256]{3,2,1,0:T(8,128)(2,1)S(1)}, f32[2,512,128]{2,1,0:T(8,128)S(1)}, f32[2,8,128]{2,1,0:T(8,128)S(1)}, f32[2,4,2,128,128]{4,3,2,1,0:T...) custom-call(bf16[272,512]{1,0:T(8,128)(2,1)S(1)} %pack_rows.1.load_r, ...), custom_call_target="tpu_custom_call" | custom-call | flops 65536 | bytes 1024 | tf_op jit(solution)/shard_map/prepare/pallas_call | solution.py:412
  8.1 1.1 %collective-permute-start.1 = (bf16[128,512]{1,0:T(8,128)(2,1)S(1)}, bf16[128,512]{1,0:T(8,128)(2,1)S(1)}, u32[]{:S(2)}, u32[]{:S(2)}) collective-permute-start(bf16[128,512]{1,0:T(8,128)(2,1)S(1)} %slice.16), channel_id=1, source_target_pairs={{0,4},{1,5},{2,0},{3,1},{6,2},{7,3},{4,6},{5,7},{8,12},{9,13},{10,... | collective-permute-start | bytes 393224 | tf_op jit(solution)/shard_map/ppermute | solution.py:39
  9.2 1.6 %slots_own.1 = (f32[2,512,128]{2,1,0:T(8,128)S(1)}, f32[2,8,128]{2,1,0:T(8,128)S(1)}, f32[32,512]{1,0:T(8,128)S(1)}, f32[32,128]{1,0:T(8,128)S(1)}) custom-call(f32[2,4,8,128]{3,2,1,0:T(8,128)S(1)} %get-tuple-element.45.mask_ref, f32[1,512]{1,0:T(1,128)S(1)} %get-tuple-element.46.gain_ref, bf16[512,512]{1,0:T(8,128)(2,1)S(1)} %get-tuple-element.47.wk_ref, ...), custom_call_target="tpu_custom_call" | custom-call | flops 65536 | bytes 1024 | tf_op jit(solution)/shard_map/slots_own/pallas_call | solution.py:477
  10.9 4.3 %collective-permute-done.1.refs_0_ = bf16[128,512]{1,0:T(8,128)(2,1)S(1)} collective-permute-done((bf16[128,512]{1,0:T(8,128)(2,1)S(1)}, bf16[128,512]{1,0:T(8,128)(2,1)S(1)}, u32[]{:S(2)}, u32[]{:S(2)}) %collective-permute-start.1) | collective-permute-done | bytes 131104 | tf_op jit(solution)/shard_map/ppermute | solution.py:39
  15.2 0.1 collective-permute-start.3
  15.4 1.7 %collective-permute-start.5 = (bf16[144,512]{1,0:T(8,128)(2,1)S(1)}, bf16[144,512]{1,0:T(8,128)(2,1)S(1)}, u32[]{:S(2)}, u32[]{:S(2)}) collective-permute-start(bf16[144,512]{1,0:T(8,128)(2,1)S(1)} %slice.17), channel_id=1, source_target_pairs={{0,4},{1,5},{2,0},{3,1},{6,2},{7,3},{4,6},{5,7},{8,12},{9,13},{10,... | collective-permute-start | bytes 442376 | tf_op jit(solution)/shard_map/ppermute | solution.py:39
  17.1 0.2 collective-permute-start.4
  17.3 0.6 %collective-permute-start.8 = (bf16[272,512]{1,0:T(8,128)(2,1)S(1)}, bf16[272,512]{1,0:T(8,128)(2,1)S(1)}, u32[]{:S(2)}, u32[]{:S(2)}) collective-permute-start(bf16[272,512]{1,0:T(8,128)(2,1)S(1)} %collective-permute-done.2.refs_0_), channel_id=1, source_target_pairs={{0,2},{1,3},{2,6},{3,7},{6,4},{7,5},{4,0},{5,1},{8,10},{9,11},{10,... | collective-permute-start | bytes 835592 | tf_op jit(solution)/shard_map/ppermute | solution.py:39
  17.9 0.6 %collective-permute-done.4.refs_2_ = bf16[128,512]{1,0:T(8,128)(2,1)S(1)} collective-permute-done((bf16[128,512]{1,0:T(8,128)(2,1)S(1)}, bf16[128,512]{1,0:T(8,128)(2,1)S(1)}, u32[]{:S(2)}, u32[]{:S(2)}) %collective-permute-start.4) | collective-permute-done | bytes 131104 | tf_op jit(solution)/shard_map/ppermute | solution.py:43
  18.5 2.7 %slots_0.1 = (f32[2,512,128]{2,1,0:T(8,128)S(1)}, f32[2,8,128]{2,1,0:T(8,128)S(1)}, f32[32,512]{1,0:T(8,128)S(1)}, f32[32,128]{1,0:T(8,128)S(1)}) custom-call(f32[2,4,8,128]{3,2,1,0:T(8,128)S(1)} %get-tuple-element.45.mask_ref, f32[1,512]{1,0:T(1,128)S(1)} %get-tuple-element.46.gain_ref, bf16[512,512]{1,0:T(8,128)(2,1)S(1)} %get-tuple-element.47.wk_ref, ...), custom_call_target="tpu_custom_call" | custom-call | flops 65536 | bytes 1024 | tf_op jit(solution)/shard_map/slots_0/pallas_call | solution.py:477
  21.2 0.7 %collective-permute-done.5.refs_1_ = bf16[144,512]{1,0:T(8,128)(2,1)S(1)} collective-permute-done((bf16[144,512]{1,0:T(8,128)(2,1)S(1)}, bf16[144,512]{1,0:T(8,128)(2,1)S(1)}, u32[]{:S(2)}, u32[]{:S(2)}) %collective-permute-start.5) | collective-permute-done | bytes 147488 | tf_op jit(solution)/shard_map/ppermute | solution.py:39
  21.9 0.5 %collective-permute-start.6 = (bf16[128,512]{1,0:T(8,128)(2,1)S(1)}, bf16[128,512]{1,0:T(8,128)(2,1)S(1)}, u32[]{:S(2)}, u32[]{:S(2)}) collective-permute-start(bf16[128,512]{1,0:T(8,128)(2,1)S(1)} %collective-permute-done.1.refs_0_), channel_id=1, source_target_pairs={{0,1},{1,0},{2,3},{3,2},{4,5},{5,4},{6,7},{7,6},{8,9},{9,8},{10,11... | collective-permute-start | bytes 393224 | tf_op jit(solution)/shard_map/ppermute | solution.py:43
  22.4 1.0 %collective-permute-done.6.refs_2_ = bf16[128,512]{1,0:T(8,128)(2,1)S(1)} collective-permute-done((bf16[128,512]{1,0:T(8,128)(2,1)S(1)}, bf16[128,512]{1,0:T(8,128)(2,1)S(1)}, u32[]{:S(2)}, u32[]{:S(2)}) %collective-permute-start.6) | collective-permute-done | bytes 131104 | tf_op jit(solution)/shard_map/ppermute | solution.py:43
  23.5 2.7 %slots_1.1 = (f32[2,512,128]{2,1,0:T(8,128)S(1)}, f32[2,8,128]{2,1,0:T(8,128)S(1)}, f32[32,512]{1,0:T(8,128)S(1)}, f32[32,128]{1,0:T(8,128)S(1)}) custom-call(f32[2,4,8,128]{3,2,1,0:T(8,128)S(1)} %get-tuple-element.45.mask_ref, f32[1,512]{1,0:T(1,128)S(1)} %get-tuple-element.46.gain_ref, bf16[512,512]{1,0:T(8,128)(2,1)S(1)} %get-tuple-element.47.wk_ref, ...), custom_call_target="tpu_custom_call" | custom-call | flops 65536 | bytes 1024 | tf_op jit(solution)/shard_map/slots_1/pallas_call | solution.py:477
  26.2 3.7 %collective-permute-done.8.refs_0_ = bf16[272,512]{1,0:T(8,128)(2,1)S(1)} collective-permute-done((bf16[272,512]{1,0:T(8,128)(2,1)S(1)}, bf16[272,512]{1,0:T(8,128)(2,1)S(1)}, u32[]{:S(2)}, u32[]{:S(2)}) %collective-permute-start.8) | collective-permute-done | bytes 278560 | tf_op jit(solution)/shard_map/ppermute | solution.py:39
  29.9 0.1 collective-permute-start.9
  29.9 1.7 %slots_2.1 = (f32[2,512,128]{2,1,0:T(8,128)S(1)}, f32[2,8,128]{2,1,0:T(8,128)S(1)}, f32[32,512]{1,0:T(8,128)S(1)}, f32[32,128]{1,0:T(8,128)S(1)}) custom-call(f32[2,4,8,128]{3,2,1,0:T(8,128)S(1)} %get-tuple-element.45.mask_ref, f32[1,512]{1,0:T(1,128)S(1)} %get-tuple-element.46.gain_ref, bf16[512,512]{1,0:T(8,128)(2,1)S(1)} %get-tuple-element.47.wk_ref, ...), custom_call_target="tpu_custom_call" | custom-call | flops 65536 | bytes 1024 | tf_op jit(solution)/shard_map/slots_2/pallas_call | solution.py:477
  31.6 2.1 %finish.1 = bf16[256,512]{1,0:T(8,128)(2,1)S(1)} custom-call(f32[2,4,8,128]{3,2,1,0:T(8,128)S(1)} %get-tuple-element.45.mask_ref, f32[1,512]{1,0:T(1,128)S(1)} %get-tuple-element.46.gain_ref, bf16[512,512]{1,0:T(8,128)(2,1)S(1)} %get-tuple-element.47.wk_ref, bf16[512,512]{1,0:T(8,128)(2,1)S(1)} %get-tuple-element.48.wvt_ref, ...), custom_call_target="tpu_custom_call" | custom-call | flops 65536 | bytes 1024 | tf_op jit(solution)/shard_map/finish/pallas_call | solution.py:519
  33.8 1.5 %collective-permute-start.10 = (bf16[1,256,512]{2,1,0:T(8,128)(2,1)S(1)}, bf16[1,256,512]{2,1,0:T(8,128)(2,1)S(1)}, u32[]{:S(2)}, u32[]{:S(2)}) collective-permute-start(bf16[1,256,512]{2,1,0:T(8,128)(2,1)S(1)} %bitcast.6), channel_id=1, source_target_pairs={{0,8},{8,16},{16,24},{24,0},{1,9},{9,17},{17,25},{25,1},{2,10},{10... | collective-permute-start | bytes 786440 | tf_op jit(solution)/shard_map/ppermute | solution.py:54
  35.3 8.1 %collective-permute-done.10 = bf16[1,256,512]{2,1,0:T(8,128)(2,1)S(1)} collective-permute-done((bf16[1,256,512]{2,1,0:T(8,128)(2,1)S(1)}, bf16[1,256,512]{2,1,0:T(8,128)(2,1)S(1)}, u32[]{:S(2)}, u32[]{:S(2)}) %collective-permute-start.10) | collective-permute-done | bytes 262176 | tf_op jit(solution)/shard_map/ppermute | solution.py:54
  43.4 0.7 %copy.12 = bf16[1,256,512]{2,1,0:T(8,128)(2,1)} copy(bf16[1,256,512]{2,1,0:T(8,128)(2,1)S(1)} %collective-permute-done.10) | data formatting | bytes 524288
  (10 shorter events, 0.1 us)
Async XLA Ops:
  1.0 8.3 %collective-permute-start = (bf16[272,512]{1,0:T(8,128)(2,1)S(1)}, bf16[272,512]{1,0:T(8,128)(2,1)S(1)}, u32[]{:S(2)}, u32[]{:S(2)}) collective-permute-start(bf16[272,512]{1,0:T(8,128)(2,1)S(1)} %pack_rows.1.load_ref), channel_id=1, source_target_pairs={{0,1},{1,0},{2,3},{3,2},{4,5},{5,4},{6,7},{7,6},{8,9},{9,8},{10,11... | collective-permute-start | bytes 835592 | tf_op jit(solution)/shard_map/ppermute | solution.py:43
  1.5 13.7 %collective-permute-start.2 = (bf16[272,512]{1,0:T(8,128)(2,1)S(1)}, bf16[272,512]{1,0:T(8,128)(2,1)S(1)}, u32[]{:S(2)}, u32[]{:S(2)}) collective-permute-start(bf16[272,512]{1,0:T(8,128)(2,1)S(1)} %pack_rows.1.load_ref), channel_id=1, source_target_pairs={{0,2},{1,3},{2,6},{3,7},{6,4},{7,5},{4,0},{5,1},{8,10},{9,11},{10,... | collective-permute-start | bytes 835592 | tf_op jit(solution)/shard_map/ppermute | solution.py:39
  8.1 7.1 %collective-permute-start.1 = (bf16[128,512]{1,0:T(8,128)(2,1)S(1)}, bf16[128,512]{1,0:T(8,128)(2,1)S(1)}, u32[]{:S(2)}, u32[]{:S(2)}) collective-permute-start(bf16[128,512]{1,0:T(8,128)(2,1)S(1)} %slice.16), channel_id=1, source_target_pairs={{0,4},{1,5},{2,0},{3,1},{6,2},{7,3},{4,6},{5,7},{8,12},{9,13},{10,... | collective-permute-start | bytes 393224 | tf_op jit(solution)/shard_map/ppermute | solution.py:39
  15.2 3.3 %collective-permute-start.3 = (bf16[144,512]{1,0:T(8,128)(2,1)S(1)}, bf16[144,512]{1,0:T(8,128)(2,1)S(1)}, u32[]{:S(2)}, u32[]{:S(2)}) collective-permute-start(bf16[144,512]{1,0:T(8,128)(2,1)S(1)} %slice.14), channel_id=1, source_target_pairs={{0,1},{1,0},{2,3},{3,2},{4,5},{5,4},{6,7},{7,6},{8,9},{9,8},{10,11... | collective-permute-start | bytes 442376 | tf_op jit(solution)/shard_map/ppermute | solution.py:43
  15.4 6.5 %collective-permute-start.5 = (bf16[144,512]{1,0:T(8,128)(2,1)S(1)}, bf16[144,512]{1,0:T(8,128)(2,1)S(1)}, u32[]{:S(2)}, u32[]{:S(2)}) collective-permute-start(bf16[144,512]{1,0:T(8,128)(2,1)S(1)} %slice.17), channel_id=1, source_target_pairs={{0,4},{1,5},{2,0},{3,1},{6,2},{7,3},{4,6},{5,7},{8,12},{9,13},{10,... | collective-permute-start | bytes 442376 | tf_op jit(solution)/shard_map/ppermute | solution.py:39
  17.1 1.4 %collective-permute-start.4 = (bf16[128,512]{1,0:T(8,128)(2,1)S(1)}, bf16[128,512]{1,0:T(8,128)(2,1)S(1)}, u32[]{:S(2)}, u32[]{:S(2)}) collective-permute-start(bf16[128,512]{1,0:T(8,128)(2,1)S(1)} %slice.15), channel_id=1, source_target_pairs={{0,1},{1,0},{2,3},{3,2},{4,5},{5,4},{6,7},{7,6},{8,9},{9,8},{10,11... | collective-permute-start | bytes 393224 | tf_op jit(solution)/shard_map/ppermute | solution.py:43
  17.3 12.5 %collective-permute-start.8 = (bf16[272,512]{1,0:T(8,128)(2,1)S(1)}, bf16[272,512]{1,0:T(8,128)(2,1)S(1)}, u32[]{:S(2)}, u32[]{:S(2)}) collective-permute-start(bf16[272,512]{1,0:T(8,128)(2,1)S(1)} %collective-permute-done.2.refs_0_), channel_id=1, source_target_pairs={{0,2},{1,3},{2,6},{3,7},{6,4},{7,5},{4,0},{5,1},{8,10},{9,11},{10,... | collective-permute-start | bytes 835592 | tf_op jit(solution)/shard_map/ppermute | solution.py:39
  21.9 1.6 %collective-permute-start.7 = (bf16[144,512]{1,0:T(8,128)(2,1)S(1)}, bf16[144,512]{1,0:T(8,128)(2,1)S(1)}, u32[]{:S(2)}, u32[]{:S(2)}) collective-permute-start(bf16[144,512]{1,0:T(8,128)(2,1)S(1)} %collective-permute-done.5.refs_1_), channel_id=1, source_target_pairs={{0,1},{1,0},{2,3},{3,2},{4,5},{5,4},{6,7},{7,6},{8,9},{9,8},{10,11... | collective-permute-start | bytes 442376 | tf_op jit(solution)/shard_map/ppermute | solution.py:43
  21.9 1.6 %collective-permute-start.6 = (bf16[128,512]{1,0:T(8,128)(2,1)S(1)}, bf16[128,512]{1,0:T(8,128)(2,1)S(1)}, u32[]{:S(2)}, u32[]{:S(2)}) collective-permute-start(bf16[128,512]{1,0:T(8,128)(2,1)S(1)} %collective-permute-done.1.refs_0_), channel_id=1, source_target_pairs={{0,1},{1,0},{2,3},{3,2},{4,5},{5,4},{6,7},{7,6},{8,9},{9,8},{10,11... | collective-permute-start | bytes 393224 | tf_op jit(solution)/shard_map/ppermute | solution.py:43
  29.9 1.7 %collective-permute-start.9 = (bf16[272,512]{1,0:T(8,128)(2,1)S(1)}, bf16[272,512]{1,0:T(8,128)(2,1)S(1)}, u32[]{:S(2)}, u32[]{:S(2)}) collective-permute-start(bf16[272,512]{1,0:T(8,128)(2,1)S(1)} %collective-permute-done.8.refs_0_), channel_id=1, source_target_pairs={{0,1},{1,0},{2,3},{3,2},{4,5},{5,4},{6,7},{7,6},{8,9},{9,8},{10,11... | collective-permute-start | bytes 835592 | tf_op jit(solution)/shard_map/ppermute | solution.py:43
  33.8 9.6 %collective-permute-start.10 = (bf16[1,256,512]{2,1,0:T(8,128)(2,1)S(1)}, bf16[1,256,512]{2,1,0:T(8,128)(2,1)S(1)}, u32[]{:S(2)}, u32[]{:S(2)}) collective-permute-start(bf16[1,256,512]{2,1,0:T(8,128)(2,1)S(1)} %bitcast.6), channel_id=1, source_target_pairs={{0,8},{8,16},{16,24},{24,0},{1,9},{9,17},{17,25},{25,1},{2,10},{10... | collective-permute-start | bytes 786440 | tf_op jit(solution)/shard_map/ppermute | solution.py:54

commit v8 on v6

--- a/solution.py
+++ b/solution.py
@@ -13,6 +13,7 @@
 CAP_LIMIT = 10.0
 LOG2E = 1.4426950408889634
 EXTRA = 16
+TILE = 8
 PARTS = 2
 F32 = jnp.float32
 BF16 = jnp.bfloat16
@@ -44,7 +45,7 @@
 
 
 def swapped_parts(value, devices, parts):
-    tiles = value.shape[0] // 16
+    tiles = -(-value.shape[0] // 16)
     cuts = [0] + [16 * (-(-tiles * (i + 1) // parts)) for i in range(parts)]
     return [swapped(value[a:b], devices, 1) for a, b in zip(cuts, cuts[1:])]
 
@@ -127,19 +128,19 @@
     rows = vid_ref.shape[1]
     copies = start_copies([(x_hbm, load_ref.at[:rows, :]), (vid_hbm, vid_ref)], sems)
     copies[1].wait()
-    tile = jnp.broadcast_to(vid_ref[...].astype(F32), (EXTRA, rows))
-    rest = jnp.zeros((EXTRA, load_ref.shape[1] - rows), F32)
+    tile = jnp.broadcast_to(vid_ref[...].astype(F32), (TILE, rows))
+    rest = jnp.zeros((TILE, load_ref.shape[1] - rows), F32)
     load_ref[rows:, :] = jnp.concatenate([tile, rest], axis=1).astype(BF16)
     copies[0].wait()
 
 
 def vid_row(load_ref, rows):
     last = load_ref.shape[0]
-    return load_ref[last - EXTRA :, :rows].astype(F32)[:1, :]
+    return load_ref[last - TILE :, :rows].astype(F32)[:1, :]
 
 
 def load_rows(refs):
-    last = refs[-1].shape[0] - EXTRA
+    last = refs[-1].shape[0] - TILE
     return jnp.concatenate([ref[...] for ref in refs[:-1]] + [refs[-1][:last, :]], axis=0)
 
 
@@ -181,7 +182,7 @@
     wq_ref, wv_ref, vk_ref, lrows_ref, srows_ref, sblock_ref, scount_ref, want_ref, sems,
 ):
     width = load_ref.shape[1]
-    rows = load_ref.shape[0] - EXTRA
+    rows = load_ref.shape[0] - TILE
     blocks, pairs, wide, _ = qbd_ref.shape
     chips = mask_ref.shape[1]
     slots = sblock_ref.shape[1]
@@ -388,7 +389,7 @@
 
     load = pl.pallas_call(
         pack_kernel,
-        out_shape=shape((rows + EXTRA, width), BF16),
+        out_shape=shape((rows + TILE, width), BF16),
         in_specs=[HBM] * 2,
         out_specs=VMEM,
         scratch_shapes=[pltpu.VMEM((1, rows), jnp.int32), pltpu.SemaphoreType.DMA((2,))],

time: 40.7 us -> 40.3 us (level)
  transfers between devices with their start and end apart: 10 -> 10, of which waited for: 2 -> 2; matrix products, arithmetic and copies ran while one was open for 0% -> 0% of each run, Pallas kernels for 31% -> 32%
where the time goes in v8:
time: 40.3 us; the launch traced here: 39.8 us
  Pallas kernels  15.7 us (39%)
  starting transfers between devices  13.7 us (34%)
  waiting for transfers between devices  9.51 us (24%)
  local copies, waits for them, and re-layouts  0.74 us (2%)
    ppermute x3, starting transfers between devices, to_next_chip(): return lax.ppermute(value, 'node', pairs)  10.3 us
    pallas_call x4, Pallas kernels, slots_call(): pl.pallas_call(functools.partial(slots_kernel, tuple(names), sizes), out_...  8.65 us
    ppermute x1, waiting for transfers between devices, to_next_segment(): lax.ppermute(value, 'segment', [(s, (s + 1) % count) for s in range(count)])  8.06 us
    pallas_call x1, Pallas kernels, body(): pl.pallas_call(prep_kernel, out_shape=(shape((blocks, pairs, wide, 2 * br...  3.97 us
    pallas_call x1, Pallas kernels, body(): pl.pallas_call(functools.partial(finish_kernel, names), out_shape=shape((...  2.14 us
    ppermute x6, starting transfers between devices, swapped(): lax.ppermute(value, 'node', [(d, d ^ distance) for d in range(devices)])  1.81 us
    ppermute x1, starting transfers between devices, to_next_segment(): lax.ppermute(value, 'segment', [(s, (s + 1) % count) for s in range(count)])  1.54 us
    ppermute x3, waiting for transfers between devices, to_next_chip(): return lax.ppermute(value, 'node', pairs)  1.43 us
  transfers between devices with their start and end apart: 10, of which 2 were waited for; matrix products, arithmetic and copies ran while one was open for 0% of the time, Pallas kernels for 32%

profile of v8, /device:TPU:0, one launch (start us, length us, event | category | flops | bytes accessed | tf_op | source)
XLA Modules:
  0.0 39.8 jit_solution(9712637577950490156)
XLA Ops:
  0.0 1.0 %pack_rows.1.load_ref = bf16[264,512]{1,0:T(8,128)(2,1)S(1)} custom-call(bf16[256,512]{1,0:T(8,128)(2,1)} %bitcast.9, s32[1,256]{1,0:T(1,128)} %bitcast.11), custom_call_target="tpu_custom_call" | custom-call | flops 65536 | bytes 1024 | tf_op jit(solution)/shard_map/pack_rows/pallas_call | solution.py:390
  1.0 0.5 %collective-permute-start = (bf16[264,512]{1,0:T(8,128)(2,1)S(1)}, bf16[264,512]{1,0:T(8,128)(2,1)S(1)}, u32[]{:S(2)}, u32[]{:S(2)}) collective-permute-start(bf16[264,512]{1,0:T(8,128)(2,1)S(1)} %pack_rows.1.load_ref), channel_id=1, source_target_pairs={{0,1},{1,0},{2,3},{3,2},{4,5},{5,4},{6,7},{7,6},{8,9},{9,8},{10,11... | collective-permute-start | bytes 811016 | tf_op jit(solution)/shard_map/ppermute | solution.py:44
  1.5 2.6 %collective-permute-start.2 = (bf16[264,512]{1,0:T(8,128)(2,1)S(1)}, bf16[264,512]{1,0:T(8,128)(2,1)S(1)}, u32[]{:S(2)}, u32[]{:S(2)}) collective-permute-start(bf16[264,512]{1,0:T(8,128)(2,1)S(1)} %pack_rows.1.load_ref), channel_id=1, source_target_pairs={{0,2},{1,3},{2,6},{3,7},{6,4},{7,5},{4,0},{5,1},{8,10},{9,11},{10,... | collective-permute-start | bytes 811016 | tf_op jit(solution)/shard_map/ppermute | solution.py:40
  4.1 4.0 %prepare.1 = (bf16[2,4,128,256]{3,2,1,0:T(8,128)(2,1)S(1)}, f32[2,512,128]{2,1,0:T(8,128)S(1)}, f32[2,8,128]{2,1,0:T(8,128)S(1)}, f32[2,4,2,128,128]{4,3,2,1,0:T...) custom-call(bf16[264,512]{1,0:T(8,128)(2,1)S(1)} %pack_rows.1.load_r, ...), custom_call_target="tpu_custom_call" | custom-call | flops 65536 | bytes 1024 | tf_op jit(solution)/shard_map/prepare/pallas_call | solution.py:413
  8.1 1.1 %collective-permute-start.1 = (bf16[264,512]{1,0:T(8,128)(2,1)S(1)}, bf16[264,512]{1,0:T(8,128)(2,1)S(1)}, u32[]{:S(2)}, u32[]{:S(2)}) collective-permute-start(bf16[264,512]{1,0:T(8,128)(2,1)S(1)} %pack_rows.1.load_ref), channel_id=1, source_target_pairs={{0,4},{1,5},{2,0},{3,1},{6,2},{7,3},{4,6},{5,7},{8,12},{9,13},{10,... | collective-permute-start | bytes 811016 | tf_op jit(solution)/shard_map/ppermute | solution.py:40
  9.2 0.0 collective-permute-done.refs_0_
  9.2 1.6 %slots_own.1 = (f32[2,512,128]{2,1,0:T(8,128)S(1)}, f32[2,8,128]{2,1,0:T(8,128)S(1)}, f32[32,512]{1,0:T(8,128)S(1)}, f32[32,128]{1,0:T(8,128)S(1)}) custom-call(f32[2,4,8,128]{3,2,1,0:T(8,128)S(1)} %get-tuple-element.42.mask_ref, f32[1,512]{1,0:T(1,128)S(1)} %get-tuple-element.43.gain_ref, bf16[512,512]{1,0:T(8,128)(2,1)S(1)} %get-tuple-element.44.wk_ref, ...), custom_call_target="tpu_custom_call" | custom-call | flops 65536 | bytes 1024 | tf_op jit(solution)/shard_map/slots_own/pallas_call | solution.py:477
  10.9 1.4 %collective-permute-done.2.refs_0_ = bf16[264,512]{1,0:T(8,128)(2,1)S(1)} collective-permute-done((bf16[264,512]{1,0:T(8,128)(2,1)S(1)}, bf16[264,512]{1,0:T(8,128)(2,1)S(1)}, u32[]{:S(2)}, u32[]{:S(2)}) %collective-permute-start.2) | collective-permute-done | bytes 270368 | tf_op jit(solution)/shard_map/ppermute | solution.py:40
  12.3 6.6 %collective-permute-start.7 = (bf16[264,512]{1,0:T(8,128)(2,1)S(1)}, bf16[264,512]{1,0:T(8,128)(2,1)S(1)}, u32[]{:S(2)}, u32[]{:S(2)}) collective-permute-start(bf16[264,512]{1,0:T(8,128)(2,1)S(1)} %collective-permute-done.2.refs_0_), channel_id=1, source_target_pairs={{0,2},{1,3},{2,6},{3,7},{6,4},{7,5},{4,0},{5,1},{8,10},{9,11},{10,... | collective-permute-start | bytes 811016 | tf_op jit(solution)/shard_map/ppermute | solution.py:40
  18.9 0.0 collective-permute-done.1.refs_1_
  18.9 0.1 collective-permute-start.5
  19.0 0.5 %collective-permute-start.3 = (bf16[144,512]{1,0:T(8,128)(2,1)S(1)}, bf16[144,512]{1,0:T(8,128)(2,1)S(1)}, u32[]{:S(2)}, u32[]{:S(2)}) collective-permute-start(bf16[144,512]{1,0:T(8,128)(2,1)S(1)} %slice.12), channel_id=1, source_target_pairs={{0,1},{1,0},{2,3},{3,2},{4,5},{5,4},{6,7},{7,6},{8,9},{9,8},{10,11... | collective-permute-start | bytes 442376 | tf_op jit(solution)/shard_map/ppermute | solution.py:44
  19.5 0.1 collective-permute-start.6
  19.7 0.4 %collective-permute-start.4 = (bf16[120,512]{1,0:T(8,128)(2,1)S(1)}, bf16[120,512]{1,0:T(8,128)(2,1)S(1)}, u32[]{:S(2)}, u32[]{:S(2)}) collective-permute-start(bf16[120,512]{1,0:T(8,128)(2,1)S(1)} %slice.13), channel_id=1, source_target_pairs={{0,1},{1,0},{2,3},{3,2},{4,5},{5,4},{6,7},{7,6},{8,9},{9,8},{10,11... | collective-permute-start | bytes 368648 | tf_op jit(solution)/shard_map/ppermute | solution.py:44
  20.1 2.7 %slots_near.1 = (f32[2,512,128]{2,1,0:T(8,128)S(1)}, f32[2,8,128]{2,1,0:T(8,128)S(1)}, f32[32,512]{1,0:T(8,128)S(1)}, f32[32,128]{1,0:T(8,128)S(1)}) custom-call(f32[2,4,8,128]{3,2,1,0:T(8,128)S(1)} %get-tuple-element.42.mask_ref, f32[1,512]{1,0:T(1,128)S(1)} %get-tuple-element.43.gain_ref, bf16[512,512]{1,0:T(8,128)(2,1)S(1)} %get-tuple-element.44.wk_ref, ...), custom_call_target="tpu_custom_call" | custom-call | flops 65536 | bytes 1024 | tf_op jit(solution)/shard_map/slots_near/pallas_call | solution.py:477
  22.8 0.0 collective-permute-done.4.refs_1_
  22.8 0.0 collective-permute-done.5.refs_2_
  22.8 2.7 %slots_far.1 = (f32[2,512,128]{2,1,0:T(8,128)S(1)}, f32[2,8,128]{2,1,0:T(8,128)S(1)}, f32[32,512]{1,0:T(8,128)S(1)}, f32[32,128]{1,0:T(8,128)S(1)}) custom-call(f32[2,4,8,128]{3,2,1,0:T(8,128)S(1)} %get-tuple-element.42.mask_ref, f32[1,512]{1,0:T(1,128)S(1)} %get-tuple-element.43.gain_ref, bf16[512,512]{1,0:T(8,128)(2,1)S(1)} %get-tuple-element.44.wk_ref, ...), custom_call_target="tpu_custom_call" | custom-call | flops 65536 | bytes 1024 | tf_op jit(solution)/shard_map/slots_far/pallas_call | solution.py:477
  25.5 0.1 collective-permute-start.8
  25.7 1.7 %slots_0.1 = (f32[2,512,128]{2,1,0:T(8,128)S(1)}, f32[2,8,128]{2,1,0:T(8,128)S(1)}, f32[32,512]{1,0:T(8,128)S(1)}, f32[32,128]{1,0:T(8,128)S(1)}) custom-call(f32[2,4,8,128]{3,2,1,0:T(8,128)S(1)} %get-tuple-element.42.mask_ref, f32[1,512]{1,0:T(1,128)S(1)} %get-tuple-element.43.gain_ref, bf16[512,512]{1,0:T(8,128)(2,1)S(1)} %get-tuple-element.44.wk_ref, ...), custom_call_target="tpu_custom_call" | custom-call | flops 65536 | bytes 1024 | tf_op jit(solution)/shard_map/slots_0/pallas_call | solution.py:477
  27.3 2.1 %finish.1 = bf16[256,512]{1,0:T(8,128)(2,1)S(1)} custom-call(f32[2,4,8,128]{3,2,1,0:T(8,128)S(1)} %get-tuple-element.42.mask_ref, f32[1,512]{1,0:T(1,128)S(1)} %get-tuple-element.43.gain_ref, bf16[512,512]{1,0:T(8,128)(2,1)S(1)} %get-tuple-element.44.wk_ref, bf16[512,512]{1,0:T(8,128)(2,1)S(1)} %get-tuple-element.45.wvt_ref, ...), custom_call_target="tpu_custom_call" | custom-call | flops 65536 | bytes 1024 | tf_op jit(solution)/shard_map/finish/pallas_call | solution.py:522
  29.5 1.5 %collective-permute-start.9 = (bf16[1,256,512]{2,1,0:T(8,128)(2,1)S(1)}, bf16[1,256,512]{2,1,0:T(8,128)(2,1)S(1)}, u32[]{:S(2)}, u32[]{:S(2)}) collective-permute-start(bf16[1,256,512]{2,1,0:T(8,128)(2,1)S(1)} %bitcast.6), channel_id=1, source_target_pairs={{0,8},{8,16},{16,24},{24,0},{1,9},{9,17},{17,25},{25,1},{2,10},{10... | collective-permute-start | bytes 786440 | tf_op jit(solution)/shard_map/ppermute | solution.py:55
  31.0 8.1 %collective-permute-done.9 = bf16[1,256,512]{2,1,0:T(8,128)(2,1)S(1)} collective-permute-done((bf16[1,256,512]{2,1,0:T(8,128)(2,1)S(1)}, bf16[1,256,512]{2,1,0:T(8,128)(2,1)S(1)}, u32[]{:S(2)}, u32[]{:S(2)}) %collective-permute-start.9) | collective-permute-done | bytes 262176 | tf_op jit(solution)/shard_map/ppermute | solution.py:55
  39.1 0.7 %copy.12 = bf16[1,256,512]{2,1,0:T(8,128)(2,1)} copy(bf16[1,256,512]{2,1,0:T(8,128)(2,1)S(1)} %collective-permute-done.9) | data formatting | bytes 524288
  (8 shorter events, 0.1 us)
Async XLA Ops:
  1.0 8.2 %collective-permute-start = (bf16[264,512]{1,0:T(8,128)(2,1)S(1)}, bf16[264,512]{1,0:T(8,128)(2,1)S(1)}, u32[]{:S(2)}, u32[]{:S(2)}) collective-permute-start(bf16[264,512]{1,0:T(8,128)(2,1)S(1)} %pack_rows.1.load_ref), channel_id=1, source_target_pairs={{0,1},{1,0},{2,3},{3,2},{4,5},{5,4},{6,7},{7,6},{8,9},{9,8},{10,11... | collective-permute-start | bytes 811016 | tf_op jit(solution)/shard_map/ppermute | solution.py:44
  1.5 10.8 %collective-permute-start.2 = (bf16[264,512]{1,0:T(8,128)(2,1)S(1)}, bf16[264,512]{1,0:T(8,128)(2,1)S(1)}, u32[]{:S(2)}, u32[]{:S(2)}) collective-permute-start(bf16[264,512]{1,0:T(8,128)(2,1)S(1)} %pack_rows.1.load_ref), channel_id=1, source_target_pairs={{0,2},{1,3},{2,6},{3,7},{6,4},{7,5},{4,0},{5,1},{8,10},{9,11},{10,... | collective-permute-start | bytes 811016 | tf_op jit(solution)/shard_map/ppermute | solution.py:40
  8.1 10.8 %collective-permute-start.1 = (bf16[264,512]{1,0:T(8,128)(2,1)S(1)}, bf16[264,512]{1,0:T(8,128)(2,1)S(1)}, u32[]{:S(2)}, u32[]{:S(2)}) collective-permute-start(bf16[264,512]{1,0:T(8,128)(2,1)S(1)} %pack_rows.1.load_ref), channel_id=1, source_target_pairs={{0,4},{1,5},{2,0},{3,1},{6,2},{7,3},{4,6},{5,7},{8,12},{9,13},{10,... | collective-permute-start | bytes 811016 | tf_op jit(solution)/shard_map/ppermute | solution.py:40
  12.3 13.2 %collective-permute-start.7 = (bf16[264,512]{1,0:T(8,128)(2,1)S(1)}, bf16[264,512]{1,0:T(8,128)(2,1)S(1)}, u32[]{:S(2)}, u32[]{:S(2)}) collective-permute-start(bf16[264,512]{1,0:T(8,128)(2,1)S(1)} %collective-permute-done.2.refs_0_), channel_id=1, source_target_pairs={{0,2},{1,3},{2,6},{3,7},{6,4},{7,5},{4,0},{5,1},{8,10},{9,11},{10,... | collective-permute-start | bytes 811016 | tf_op jit(solution)/shard_map/ppermute | solution.py:40
  18.9 3.9 %collective-permute-start.5 = (bf16[144,512]{1,0:T(8,128)(2,1)S(1)}, bf16[144,512]{1,0:T(8,128)(2,1)S(1)}, u32[]{:S(2)}, u32[]{:S(2)}) collective-permute-start(bf16[144,512]{1,0:T(8,128)(2,1)S(1)} %slice.14), channel_id=1, source_target_pairs={{0,1},{1,0},{2,3},{3,2},{4,5},{5,4},{6,7},{7,6},{8,9},{9,8},{10,11... | collective-permute-start | bytes 442376 | tf_op jit(solution)/shard_map/ppermute | solution.py:44
  19.0 3.8 %collective-permute-start.3 = (bf16[144,512]{1,0:T(8,128)(2,1)S(1)}, bf16[144,512]{1,0:T(8,128)(2,1)S(1)}, u32[]{:S(2)}, u32[]{:S(2)}) collective-permute-start(bf16[144,512]{1,0:T(8,128)(2,1)S(1)} %slice.12), channel_id=1, source_target_pairs={{0,1},{1,0},{2,3},{3,2},{4,5},{5,4},{6,7},{7,6},{8,9},{9,8},{10,11... | collective-permute-start | bytes 442376 | tf_op jit(solution)/shard_map/ppermute | solution.py:44
  19.5 3.3 %collective-permute-start.6 = (bf16[120,512]{1,0:T(8,128)(2,1)S(1)}, bf16[120,512]{1,0:T(8,128)(2,1)S(1)}, u32[]{:S(2)}, u32[]{:S(2)}) collective-permute-start(bf16[120,512]{1,0:T(8,128)(2,1)S(1)} %slice.15), channel_id=1, source_target_pairs={{0,1},{1,0},{2,3},{3,2},{4,5},{5,4},{6,7},{7,6},{8,9},{9,8},{10,11... | collective-permute-start | bytes 368648 | tf_op jit(solution)/shard_map/ppermute | solution.py:44
  19.7 3.1 %collective-permute-start.4 = (bf16[120,512]{1,0:T(8,128)(2,1)S(1)}, bf16[120,512]{1,0:T(8,128)(2,1)S(1)}, u32[]{:S(2)}, u32[]{:S(2)}) collective-permute-start(bf16[120,512]{1,0:T(8,128)(2,1)S(1)} %slice.13), channel_id=1, source_target_pairs={{0,1},{1,0},{2,3},{3,2},{4,5},{5,4},{6,7},{7,6},{8,9},{9,8},{10,11... | collective-permute-start | bytes 368648 | tf_op jit(solution)/shard_map/ppermute | solution.py:44
  25.5 1.8 %collective-permute-start.8 = (bf16[264,512]{1,0:T(8,128)(2,1)S(1)}, bf16[264,512]{1,0:T(8,128)(2,1)S(1)}, u32[]{:S(2)}, u32[]{:S(2)}) collective-permute-start(bf16[264,512]{1,0:T(8,128)(2,1)S(1)} %collective-permute-done.7.refs_0_), channel_id=1, source_target_pairs={{0,1},{1,0},{2,3},{3,2},{4,5},{5,4},{6,7},{7,6},{8,9},{9,8},{10,11... | collective-permute-start | bytes 811016 | tf_op jit(solution)/shard_map/ppermute | solution.py:44
  29.5 9.6 %collective-permute-start.9 = (bf16[1,256,512]{2,1,0:T(8,128)(2,1)S(1)}, bf16[1,256,512]{2,1,0:T(8,128)(2,1)S(1)}, u32[]{:S(2)}, u32[]{:S(2)}) collective-permute-start(bf16[1,256,512]{2,1,0:T(8,128)(2,1)S(1)} %bitcast.6), channel_id=1, source_target_pairs={{0,8},{8,16},{16,24},{24,0},{1,9},{9,17},{17,25},{25,1},{2,10},{10... | collective-permute-start | bytes 786440 | tf_op jit(solution)/shard_map/ppermute | solution.py:55

commit v9 on v6

--- a/solution.py
+++ b/solution.py
@@ -313,44 +313,66 @@
         add_sources(names, b, counts_ref, qbd_ref, k_ref, vt_ref, num_ref, den_ref)
 
 
-def finish_kernel(
-    names, mask_ref, gain_ref, wk_ref, wvt_ref, vkw_ref, counts_ref, qbd_ref,
-    num_in, den_in, pool_in, weight_in, last_ref, vcol_ref, load_ref, wo_ref,
-    out_ref, num_ref, den_ref, pool_ref, weight_ref, normed_ref, k_ref, vt_ref,
-):
-    slots_kernel(
-        names, (1,), mask_ref, gain_ref, wk_ref, wvt_ref, vkw_ref, counts_ref, qbd_ref,
-        num_in, den_in, pool_in, weight_in, last_ref,
-        num_ref, den_ref, pool_ref, weight_ref, normed_ref, k_ref, vt_ref,
-    )
-    blocks, width, br = num_ref.shape
+def finish_kernel(names, b, lead, *refs):
+    if lead:
+        (
+            mask_ref, gain_ref, wk_ref, wvt_ref, vkw_ref, pool_in, weight_in, last_ref,
+            counts_ref, qbd_ref, num_in, den_in, vcol_ref, load_ref, wo_ref,
+            out_ref, k_ref, vt_ref, pooled_ref,
+            num_ref, den_ref, pool_ref, weight_ref, normed_ref,
+        ) = refs
+    else:
+        (
+            k_ref, vt_ref, pooled_ref,
+            counts_ref, qbd_ref, num_in, den_in, vcol_ref, load_ref, wo_ref,
+            out_ref, num_ref, den_ref,
+        ) = refs
+    _, width, br = num_ref.shape
     head = width // HEADS
     lanes = vcol_ref.shape[1]
-    count = pool_ref.shape[0]
-    weight = jnp.concatenate([weight_ref[...]] * (width // lanes), axis=1)
-    both = mm_nt(halves(pool_ref[...] / weight), wvt_ref[...])
-    both = jnp.where(of_own_head((count, width)), both[:count] + both[count:], 0.0)
-    pooled = [
-        jnp.sum(both[j : j + HEADS], axis=0, keepdims=True) for j in range(0, count, HEADS)
-    ]
-    for b in range(blocks):
-        part = slice(b * br, (b + 1) * br)
-        vid = vcol_ref[part, :]
-        att = jnp.concatenate(
-            [
-                num_ref[b, h * head : (h + 1) * head, :] / den_ref[b, h : h + 1, :]
-                for h in range(HEADS)
-            ],
-            axis=0,
-        ).T
-        pieces = []
-        for c in range(0, width, lanes):
-            own = jnp.broadcast_to(pooled[0][:, c : c + lanes], (br, lanes))
-            for j in range(1, len(pooled)):
-                own = jnp.where(vid == float(j), pooled[j][:, c : c + lanes], own)
-            pieces.append((att[:, c : c + lanes] + own).astype(BF16))
-        mixed = jnp.concatenate(pieces, axis=1)
-        out_ref[part, :] = (load_ref[part, :].astype(F32) + mm(mixed, wo_ref[...])).astype(BF16)
+    num_ref[b] = num_in[b]
+    den_ref[b] = den_in[b]
+    if lead:
+        pool_ref[...] = pool_in[...]
+        weight_ref[...] = weight_in[...]
+        take_sources(
+            names, [[last_ref]], mask_ref, gain_ref, wk_ref, wvt_ref, vkw_ref,
+            normed_ref, k_ref, vt_ref, pool_ref, weight_ref,
+        )
+        count = pool_ref.shape[0]
+        weight = jnp.concatenate([weight_ref[...]] * (width // lanes), axis=1)
+        both = mm_nt(halves(pool_ref[...] / weight), wvt_ref[...])
+        both = jnp.where(of_own_head((count, width)), both[:count] + both[count:], 0.0)
+        for j in range(0, count, HEADS):
+            pooled_ref[j // HEADS : j // HEADS + 1, :] = jnp.sum(
+                both[j : j + HEADS], axis=0, keepdims=True
+            )
+    add_sources(names, b, counts_ref, qbd_ref, k_ref, vt_ref, num_ref, den_ref)
+    part = slice(b * br, (b + 1) * br)
+    vid = vcol_ref[part, :]
+    att = jnp.concatenate(
+        [
+            num_ref[b, h * head : (h + 1) * head, :] / den_ref[b, h : h + 1, :]
+            for h in range(HEADS)
+        ],
+        axis=0,
+    ).T
+    pieces = []
+    for c in range(0, width, lanes):
+        own = jnp.broadcast_to(pooled_ref[0:1, c : c + lanes], (br, lanes))
+        for j in range(1, pooled_ref.shape[0]):
+            own = jnp.where(vid == float(j), pooled_ref[j : j + 1, c : c + lanes], own)
+        pieces.append((att[:, c : c + lanes] + own).astype(BF16))
+    mixed = jnp.concatenate(pieces, axis=1)
+    out_ref[...] = (load_ref[part, :].astype(F32) + mm(mixed, wo_ref[...])).astype(BF16)
+
+
+def place_kernel(b, rows_ref, *refs):
+    out_ref, sems = refs[-2:]
+    br = rows_ref.shape[0]
+    copy = pltpu.make_async_copy(rows_ref, out_ref.at[0, b * br : (b + 1) * br, :], sems.at[0])
+    copy.start()
+    copy.wait()
 
 
 def params(mib):
@@ -518,19 +540,49 @@
             names = names[:1]
         sums = slots_call(names, sums, "slots_%d" % i)
     names = ((1, order[-1][0]),)
-    updated = pl.pallas_call(
-        functools.partial(finish_kernel, names),
-        out_shape=shape((rows, width), BF16),
-        in_specs=[VMEM] * 15,
-        out_specs=VMEM,
-        scratch_shapes=[pltpu.VMEM(leaf.shape, leaf.dtype) for leaf in accumulators] + work(1),
-        compiler_params=params(40),
-        cost_estimate=cost(unit),
-        name="finish",
-    )(
-        mask, gain, wk, wvt, vkw, counts, qbd, *sums, far[names[0][1]], vcol, load, wo
-    )
-    return to_next_segment(updated[None])
+    shared = (counts, qbd, sums[0], sums[1], vcol, load, wo)
+    scratch = [pltpu.VMEM(leaf.shape, leaf.dtype) for leaf in accumulators]
+    carried = (
+        shape((br, width), BF16), shape((width, br), BF16), shape((virtual, width), F32)
+    )
+    results = []
+    for b in range(blocks):
+        lead = b == 0
+        outs = pl.pallas_call(
+            functools.partial(finish_kernel, names, b, lead),
+            out_shape=(shape((br, width), BF16),) + (carried if lead else ()),
+            in_specs=[VMEM] * (15 if lead else 10),
+            out_specs=(VMEM,) * (4 if lead else 1),
+            scratch_shapes=scratch + work(1)[:1] if lead else scratch[:2],
+            compiler_params=params(40),
+            cost_estimate=cost(unit),
+            name="finish_%d" % b,
+        )(
+            *(
+                (mask, gain, wk, wvt, vkw, sums[2], sums[3], far[names[0][1]])
+                if lead
+                else kept
+            ),
+            *shared,
+        )
+        if lead:
+            kept = tuple(outs[1:])
+        results.append(to_next_segment(outs[0]))
+    joined = None
+    for b in range(blocks):
+        earlier = [] if joined is None else [joined]
+        joined = pl.pallas_call(
+            functools.partial(place_kernel, b),
+            out_shape=shape((1, rows, width), BF16),
+            in_specs=[VMEM] + [HBM] * len(earlier),
+            out_specs=HBM,
+            scratch_shapes=[pltpu.SemaphoreType.DMA((1,))],
+            input_output_aliases={1: 0} if earlier else {},
+            compiler_params=params(24),
+            cost_estimate=cost(unit),
+            name="place_%d" % b,
+        )(results[b], *earlier)
+    return joined
 
 
 def solution(mesh):

time: 40.7 us -> 40.1 us (0.985)
  waiting for transfers between devices: 9.7 us -> 6.74 us
  starting transfers between devices: 13.8 us -> 15.4 us
  Pallas kernels: 15.7 us -> 17.2 us
  local copies, waits for them, and re-layouts: 0.74 us -> 0.04 us
    ppermute x1 -> x2, waiting for transfers between devices: 8.06 us -> 5.1 us  [to_next_segment(): lax.ppermute(value, 'segment', [(s, (s + 1) % count) for s in range(count)])]
    ppermute x1 -> x2, starting transfers between devices: 1.53 us -> 3.09 us  [to_next_segment(): lax.ppermute(value, 'segment', [(s, (s + 1) % count) for s in range(count)])]
    pallas_call x1 -> x4, Pallas kernels: 2.14 us -> 3.67 us  [the longest x2 2.34 us: body(): pl.pallas_call(functools.partial(finish_kernel, names, b, lead), out_shap...]
    unnamed x1 -> x0, local copies, waits for them, and re-layouts: 0.7 us -> none
  transfers between devices with their start and end apart: 10 -> 11, of which waited for: 2 -> 3; matrix products, arithmetic and copies ran while one was open for 0% -> 0% of each run, Pallas kernels for 31% -> 35%
where the time goes in v9:
time: 40.1 us; the launch traced here: 39.6 us
  Pallas kernels  17.2 us (43%)
  starting transfers between devices  15.4 us (38%)
  waiting for transfers between devices  6.74 us (17%)
    ppermute x3, starting transfers between devices, to_next_chip(): return lax.ppermute(value, 'node', pairs)  10.5 us
    pallas_call x4, Pallas kernels, slots_call(): pl.pallas_call(functools.partial(slots_kernel, tuple(names), sizes), out_...  8.65 us
    ppermute x2, waiting for transfers between devices, to_next_segment(): lax.ppermute(value, 'segment', [(s, (s + 1) % count) for s in range(count)])  5.1 us
    pallas_call x1, Pallas kernels, body(): pl.pallas_call(prep_kernel, out_shape=(shape((blocks, pairs, wide, 2 * br...  3.97 us
    ppermute x2, starting transfers between devices, to_next_segment(): lax.ppermute(value, 'segment', [(s, (s + 1) % count) for s in range(count)])  3.09 us
    pallas_call x2, Pallas kernels, body(): pl.pallas_call(functools.partial(finish_kernel, names, b, lead), out_shap...  2.34 us
    ppermute x6, starting transfers between devices, swapped(): lax.ppermute(value, 'node', [(d, d ^ distance) for d in range(devices)])  1.82 us
    ppermute x3, waiting for transfers between devices, to_next_chip(): return lax.ppermute(value, 'node', pairs)  1.62 us
  transfers between devices with their start and end apart: 11, of which 3 were waited for; matrix products, arithmetic and copies ran while one was open for 0% of the time, Pallas kernels for 35%

profile of v9, /device:TPU:0, one launch (start us, length us, event | category | flops | bytes accessed | tf_op | source)
XLA Modules:
  0.0 39.6 jit_solution(9132300791686238037)
XLA Ops:
  0.0 1.0 %pack_rows.1.load_ref.refs_13_.refs_8_ = bf16[272,512]{1,0:T(8,128)(2,1)S(1)} custom-call(bf16[256,512]{1,0:T(8,128)(2,1)} %bitcast.7, s32[1,256]{1,0:T(1,128)} %bitcast.9), custom_call_target="tpu_custom_call" | custom-call | flops 65536 | bytes 1024 | tf_op jit(solution)/shard_map/pack_rows/pallas_call | solution.py:411
  1.0 0.5 %collective-permute-start = (bf16[272,512]{1,0:T(8,128)(2,1)S(1)}, bf16[272,512]{1,0:T(8,128)(2,1)S(1)}, u32[]{:S(2)}, u32[]{:S(2)}) collective-permute-start(bf16[272,512]{1,0:T(8,128)(2,1)S(1)} %pack_rows.1.load_ref.refs_13_.refs_8_), channel_id=1, source_target_pairs={{0,1},{1,0},{2,3},{3,2},{4,5},{5,4},{6,7},{7,6},{8,9},{9,8},{10,11... | collective-permute-start | bytes 835592 | tf_op jit(solution)/shard_map/ppermute | solution.py:43
  1.5 2.6 %collective-permute-start.2 = (bf16[272,512]{1,0:T(8,128)(2,1)S(1)}, bf16[272,512]{1,0:T(8,128)(2,1)S(1)}, u32[]{:S(2)}, u32[]{:S(2)}) collective-permute-start(bf16[272,512]{1,0:T(8,128)(2,1)S(1)} %pack_rows.1.load_ref.refs_13_.refs_8_), channel_id=1, source_target_pairs={{0,2},{1,3},{2,6},{3,7},{6,4},{7,5},{4,0},{5,1},{8,10},{9,11},{10,... | collective-permute-start | bytes 835592 | tf_op jit(solution)/shard_map/ppermute | solution.py:39
  4.1 4.0 %prepare.1 = (bf16[2,4,128,256]{3,2,1,0:T(8,128)(2,1)S(1)}, f32[2,512,128]{2,1,0:T(8,128)S(1)}, f32[2,8,128]{2,1,0:T(8,128)S(1)}, f32[2,4,2,128,128]{4,3,2,1,0:T...) custom-call(bf16[272,512]{1,0:T(8,128)(2,1)S(1)} %pack_rows.1.load_r, ...), custom_call_target="tpu_custom_call" | custom-call | flops 65536 | bytes 1024 | tf_op jit(solution)/shard_map/prepare/pallas_call | solution.py:434
  8.1 1.1 %collective-permute-start.1 = (bf16[272,512]{1,0:T(8,128)(2,1)S(1)}, bf16[272,512]{1,0:T(8,128)(2,1)S(1)}, u32[]{:S(2)}, u32[]{:S(2)}) collective-permute-start(bf16[272,512]{1,0:T(8,128)(2,1)S(1)} %pack_rows.1.load_ref.refs_13_.refs_8_), channel_id=1, source_target_pairs={{0,4},{1,5},{2,0},{3,1},{6,2},{7,3},{4,6},{5,7},{8,12},{9,13},{10,... | collective-permute-start | bytes 835592 | tf_op jit(solution)/shard_map/ppermute | solution.py:39
  9.2 1.6 %slots_own.1 = (f32[2,512,128]{2,1,0:T(8,128)S(1)}, f32[2,8,128]{2,1,0:T(8,128)S(1)}, f32[32,512]{1,0:T(8,128)S(1)}, f32[32,128]{1,0:T(8,128)S(1)}) custom-call(f32[2,4,8,128]{3,2,1,0:T(8,128)S(1)} %get-tuple-element.46.mask_ref.refs_0_, f32[1,512]{1,0:T(1,128)S(1)} %get-tuple-element.47.gain_ref.refs_1_, ...), custom_call_target="tpu_custom_call" | custom-call | flops 65536 | bytes 1024 | tf_op jit(solution)/shard_map/slots_own/pallas_call | solution.py:498
  10.9 1.6 %collective-permute-done.2.refs_0_ = bf16[272,512]{1,0:T(8,128)(2,1)S(1)} collective-permute-done((bf16[272,512]{1,0:T(8,128)(2,1)S(1)}, bf16[272,512]{1,0:T(8,128)(2,1)S(1)}, u32[]{:S(2)}, u32[]{:S(2)}) %collective-permute-start.2) | collective-permute-done | bytes 278560 | tf_op jit(solution)/shard_map/ppermute | solution.py:39
  12.5 6.7 %collective-permute-start.7 = (bf16[272,512]{1,0:T(8,128)(2,1)S(1)}, bf16[272,512]{1,0:T(8,128)(2,1)S(1)}, u32[]{:S(2)}, u32[]{:S(2)}) collective-permute-start(bf16[272,512]{1,0:T(8,128)(2,1)S(1)} %collective-permute-done.2.refs_0_), channel_id=1, source_target_pairs={{0,2},{1,3},{2,6},{3,7},{6,4},{7,5},{4,0},{5,1},{8,10},{9,11},{10,... | collective-permute-start | bytes 835592 | tf_op jit(solution)/shard_map/ppermute | solution.py:39
  19.3 0.1 collective-permute-start.5
  19.3 0.5 %collective-permute-start.3 = (bf16[144,512]{1,0:T(8,128)(2,1)S(1)}, bf16[144,512]{1,0:T(8,128)(2,1)S(1)}, u32[]{:S(2)}, u32[]{:S(2)}) collective-permute-start(bf16[144,512]{1,0:T(8,128)(2,1)S(1)} %slice.12), channel_id=1, source_target_pairs={{0,1},{1,0},{2,3},{3,2},{4,5},{5,4},{6,7},{7,6},{8,9},{9,8},{10,11... | collective-permute-start | bytes 442376 | tf_op jit(solution)/shard_map/ppermute | solution.py:43
  19.9 0.1 collective-permute-start.6
  20.0 0.4 %collective-permute-start.4 = (bf16[128,512]{1,0:T(8,128)(2,1)S(1)}, bf16[128,512]{1,0:T(8,128)(2,1)S(1)}, u32[]{:S(2)}, u32[]{:S(2)}) collective-permute-start(bf16[128,512]{1,0:T(8,128)(2,1)S(1)} %slice.13), channel_id=1, source_target_pairs={{0,1},{1,0},{2,3},{3,2},{4,5},{5,4},{6,7},{7,6},{8,9},{9,8},{10,11... | collective-permute-start | bytes 393224 | tf_op jit(solution)/shard_map/ppermute | solution.py:43
  20.4 2.7 %slots_near.1 = (f32[2,512,128]{2,1,0:T(8,128)S(1)}, f32[2,8,128]{2,1,0:T(8,128)S(1)}, f32[32,512]{1,0:T(8,128)S(1)}, f32[32,128]{1,0:T(8,128)S(1)}) custom-call(f32[2,4,8,128]{3,2,1,0:T(8,128)S(1)} %get-tuple-element.46.mask_ref.refs_0_, f32[1,512]{1,0:T(1,128)S(1)} %get-tuple-element.47.gain_ref.refs_1_, ...), custom_call_target="tpu_custom_call" | custom-call | flops 65536 | bytes 1024 | tf_op jit(solution)/shard_map/slots_near/pallas_call | solution.py:498
  23.2 2.7 %slots_far.1 = (f32[2,512,128]{2,1,0:T(8,128)S(1)}, f32[2,8,128]{2,1,0:T(8,128)S(1)}, f32[32,512]{1,0:T(8,128)S(1)}, f32[32,128]{1,0:T(8,128)S(1)}) custom-call(f32[2,4,8,128]{3,2,1,0:T(8,128)S(1)} %get-tuple-element.46.mask_ref.refs_0_, f32[1,512]{1,0:T(1,128)S(1)} %get-tuple-element.47.gain_ref.refs_1_, ...), custom_call_target="tpu_custom_call" | custom-call | flops 65536 | bytes 1024 | tf_op jit(solution)/shard_map/slots_far/pallas_call | solution.py:498
  25.9 0.2 collective-permute-start.8
  26.0 1.6 %slots_0.1 = (f32[2,512,128]{2,1,0:T(8,128)S(1)}, f32[2,8,128]{2,1,0:T(8,128)S(1)}, f32[32,512]{1,0:T(8,128)S(1)}, f32[32,128]{1,0:T(8,128)S(1)}) custom-call(f32[2,4,8,128]{3,2,1,0:T(8,128)S(1)} %get-tuple-element.46.mask_ref.refs_0_, f32[1,512]{1,0:T(1,128)S(1)} %get-tuple-element.47.gain_ref.refs_1_, ...), custom_call_target="tpu_custom_call" | custom-call | flops 65536 | bytes 1024 | tf_op jit(solution)/shard_map/slots_0/pallas_call | solution.py:498
  27.7 1.6 %finish_0.1 = (bf16[128,512]{1,0:T(8,128)(2,1)S(1)}, bf16[128,512]{1,0:T(8,128)(2,1)S(1)}, bf16[512,128]{1,0:T(8,128)(2,1)S(1)}, f32[4,512]{1,0:T(4,128)S(1)}) custom-call(f32[2,4,8,128]{3,2,1,0:T(8,128)S(1)} %get-tuple-element.46.mask_ref.refs_0_, f32[1,512]{1,0:T(1,128)S(1)} %get-tuple-element.47.gain_ref.refs_1_, ...), custom_call_target="tpu_custom_call" | custom-call | flops 65536 | bytes 1024 | tf_op jit(solution)/shard_map/finish_0/pallas_call | solution.py:551
  29.3 1.5 %collective-permute-start.10 = (bf16[128,512]{1,0:T(8,128)(2,1)S(1)}, bf16[128,512]{1,0:T(8,128)(2,1)S(1)}, u32[]{:S(2)}, u32[]{:S(2)}) collective-permute-start(bf16[128,512]{1,0:T(8,128)(2,1)S(1)} %get-tuple-element.86), channel_id=1, source_target_pairs={{0,8},{8,16},{16,24},{24,0},{1,9},{9,17},{17,25},{25,1},{2,10},{10... | collective-permute-start | bytes 393224 | tf_op jit(solution)/shard_map/ppermute | solution.py:54
  30.8 0.7 %finish_1.1 = bf16[128,512]{1,0:T(8,128)(2,1)S(1)} custom-call(bf16[128,512]{1,0:T(8,128)(2,1)S(1)} %get-tuple-element.83.refs_0_, bf16[512,128]{1,0:T(8,128)(2,1)S(1)} %get-tuple-element.84.refs_1_, f32[4,512]{1,0:T(4,128)S(1)} %get-tuple-element.85.refs_2_, f32[2,4,2,128,128]{4,3,2,1,0:T(8,128)S(1)} %get-tuple-element.51.counts_ref.refs_8_.refs_3_, ...), custom_call_target="tpu_custom_call" | custom-call | flops 65536 | bytes 1024 | tf_op jit(solution)/shard_map/finish_1/pallas_call | solution.py:551
  31.6 1.6 %collective-permute-start.9 = (bf16[128,512]{1,0:T(8,128)(2,1)S(1)}, bf16[128,512]{1,0:T(8,128)(2,1)S(1)}, u32[]{:S(2)}, u32[]{:S(2)}) collective-permute-start(bf16[128,512]{1,0:T(8,128)(2,1)S(1)} %finish_1.1), channel_id=1, source_target_pairs={{0,8},{8,16},{16,24},{24,0},{1,9},{9,17},{17,25},{25,1},{2,10},{10... | collective-permute-start | bytes 393224 | tf_op jit(solution)/shard_map/ppermute | solution.py:54
  33.1 3.4 %collective-permute-done.10.rows_ref = bf16[128,512]{1,0:T(8,128)(2,1)S(1)} collective-permute-done((bf16[128,512]{1,0:T(8,128)(2,1)S(1)}, bf16[128,512]{1,0:T(8,128)(2,1)S(1)}, u32[]{:S(2)}, u32[]{:S(2)}) %collective-permute-start.10) | collective-permute-done | bytes 131104 | tf_op jit(solution)/shard_map/ppermute | solution.py:54
  36.6 0.7 %place_0.1.refs_0_ = bf16[1,256,512]{2,1,0:T(8,128)(2,1)} custom-call(bf16[128,512]{1,0:T(8,128)(2,1)S(1)} %collective-permute-done.10.rows_ref), custom_call_target="tpu_custom_call" | custom-call | flops 65536 | bytes 1024 | tf_op jit(solution)/shard_map/place_0/pallas_call | solution.py:574
  37.2 1.7 %collective-permute-done.9.rows_ref = bf16[128,512]{1,0:T(8,128)(2,1)S(1)} collective-permute-done((bf16[128,512]{1,0:T(8,128)(2,1)S(1)}, bf16[128,512]{1,0:T(8,128)(2,1)S(1)}, u32[]{:S(2)}, u32[]{:S(2)}) %collective-permute-start.9) | collective-permute-done | bytes 131104 | tf_op jit(solution)/shard_map/ppermute | solution.py:54
  38.9 0.7 %place_1.1 = bf16[1,256,512]{2,1,0:T(8,128)(2,1)} custom-call(bf16[128,512]{1,0:T(8,128)(2,1)S(1)} %collective-permute-done.9.rows_ref, bf16[1,256,512]{2,1,0:T(8,128)(2,1)} %place_0.1.refs_0_), custom_call_target="tpu_custom_call", output_to_operand_aliasing={{}: (1, {})} | custom-call | flops 65536 | bytes 1024 | tf_op jit(solution)/shard_map/place_1/pallas_call | solution.py:574
  (12 shorter events, 0.1 us)
Async XLA Ops:
  1.0 8.2 %collective-permute-start = (bf16[272,512]{1,0:T(8,128)(2,1)S(1)}, bf16[272,512]{1,0:T(8,128)(2,1)S(1)}, u32[]{:S(2)}, u32[]{:S(2)}) collective-permute-start(bf16[272,512]{1,0:T(8,128)(2,1)S(1)} %pack_rows.1.load_ref.refs_13_.refs_8_), channel_id=1, source_target_pairs={{0,1},{1,0},{2,3},{3,2},{4,5},{5,4},{6,7},{7,6},{8,9},{9,8},{10,11... | collective-permute-start | bytes 835592 | tf_op jit(solution)/shard_map/ppermute | solution.py:43
  1.5 11.0 %collective-permute-start.2 = (bf16[272,512]{1,0:T(8,128)(2,1)S(1)}, bf16[272,512]{1,0:T(8,128)(2,1)S(1)}, u32[]{:S(2)}, u32[]{:S(2)}) collective-permute-start(bf16[272,512]{1,0:T(8,128)(2,1)S(1)} %pack_rows.1.load_ref.refs_13_.refs_8_), channel_id=1, source_target_pairs={{0,2},{1,3},{2,6},{3,7},{6,4},{7,5},{4,0},{5,1},{8,10},{9,11},{10,... | collective-permute-start | bytes 835592 | tf_op jit(solution)/shard_map/ppermute | solution.py:39
  8.1 11.1 %collective-permute-start.1 = (bf16[272,512]{1,0:T(8,128)(2,1)S(1)}, bf16[272,512]{1,0:T(8,128)(2,1)S(1)}, u32[]{:S(2)}, u32[]{:S(2)}) collective-permute-start(bf16[272,512]{1,0:T(8,128)(2,1)S(1)} %pack_rows.1.load_ref.refs_13_.refs_8_), channel_id=1, source_target_pairs={{0,4},{1,5},{2,0},{3,1},{6,2},{7,3},{4,6},{5,7},{8,12},{9,13},{10,... | collective-permute-start | bytes 835592 | tf_op jit(solution)/shard_map/ppermute | solution.py:39
  12.5 13.4 %collective-permute-start.7 = (bf16[272,512]{1,0:T(8,128)(2,1)S(1)}, bf16[272,512]{1,0:T(8,128)(2,1)S(1)}, u32[]{:S(2)}, u32[]{:S(2)}) collective-permute-start(bf16[272,512]{1,0:T(8,128)(2,1)S(1)} %collective-permute-done.2.refs_0_), channel_id=1, source_target_pairs={{0,2},{1,3},{2,6},{3,7},{6,4},{7,5},{4,0},{5,1},{8,10},{9,11},{10,... | collective-permute-start | bytes 835592 | tf_op jit(solution)/shard_map/ppermute | solution.py:39
  19.3 3.9 %collective-permute-start.5 = (bf16[144,512]{1,0:T(8,128)(2,1)S(1)}, bf16[144,512]{1,0:T(8,128)(2,1)S(1)}, u32[]{:S(2)}, u32[]{:S(2)}) collective-permute-start(bf16[144,512]{1,0:T(8,128)(2,1)S(1)} %slice.14), channel_id=1, source_target_pairs={{0,1},{1,0},{2,3},{3,2},{4,5},{5,4},{6,7},{7,6},{8,9},{9,8},{10,11... | collective-permute-start | bytes 442376 | tf_op jit(solution)/shard_map/ppermute | solution.py:43
  19.3 3.8 %collective-permute-start.3 = (bf16[144,512]{1,0:T(8,128)(2,1)S(1)}, bf16[144,512]{1,0:T(8,128)(2,1)S(1)}, u32[]{:S(2)}, u32[]{:S(2)}) collective-permute-start(bf16[144,512]{1,0:T(8,128)(2,1)S(1)} %slice.12), channel_id=1, source_target_pairs={{0,1},{1,0},{2,3},{3,2},{4,5},{5,4},{6,7},{7,6},{8,9},{9,8},{10,11... | collective-permute-start | bytes 442376 | tf_op jit(solution)/shard_map/ppermute | solution.py:43
  19.9 3.3 %collective-permute-start.6 = (bf16[128,512]{1,0:T(8,128)(2,1)S(1)}, bf16[128,512]{1,0:T(8,128)(2,1)S(1)}, u32[]{:S(2)}, u32[]{:S(2)}) collective-permute-start(bf16[128,512]{1,0:T(8,128)(2,1)S(1)} %slice.15), channel_id=1, source_target_pairs={{0,1},{1,0},{2,3},{3,2},{4,5},{5,4},{6,7},{7,6},{8,9},{9,8},{10,11... | collective-permute-start | bytes 393224 | tf_op jit(solution)/shard_map/ppermute | solution.py:43
  20.0 3.1 %collective-permute-start.4 = (bf16[128,512]{1,0:T(8,128)(2,1)S(1)}, bf16[128,512]{1,0:T(8,128)(2,1)S(1)}, u32[]{:S(2)}, u32[]{:S(2)}) collective-permute-start(bf16[128,512]{1,0:T(8,128)(2,1)S(1)} %slice.13), channel_id=1, source_target_pairs={{0,1},{1,0},{2,3},{3,2},{4,5},{5,4},{6,7},{7,6},{8,9},{9,8},{10,11... | collective-permute-start | bytes 393224 | tf_op jit(solution)/shard_map/ppermute | solution.py:43
  25.9 1.8 %collective-permute-start.8 = (bf16[272,512]{1,0:T(8,128)(2,1)S(1)}, bf16[272,512]{1,0:T(8,128)(2,1)S(1)}, u32[]{:S(2)}, u32[]{:S(2)}) collective-permute-start(bf16[272,512]{1,0:T(8,128)(2,1)S(1)} %collective-permute-done.7.refs_0_), channel_id=1, source_target_pairs={{0,1},{1,0},{2,3},{3,2},{4,5},{5,4},{6,7},{7,6},{8,9},{9,8},{10,11... | collective-permute-start | bytes 835592 | tf_op jit(solution)/shard_map/ppermute | solution.py:43
  29.3 7.3 %collective-permute-start.10 = (bf16[128,512]{1,0:T(8,128)(2,1)S(1)}, bf16[128,512]{1,0:T(8,128)(2,1)S(1)}, u32[]{:S(2)}, u32[]{:S(2)}) collective-permute-start(bf16[128,512]{1,0:T(8,128)(2,1)S(1)} %get-tuple-element.86), channel_id=1, source_target_pairs={{0,8},{8,16},{16,24},{24,0},{1,9},{9,17},{17,25},{25,1},{2,10},{10... | collective-permute-start | bytes 393224 | tf_op jit(solution)/shard_map/ppermute | solution.py:54
  31.6 7.3 %collective-permute-start.9 = (bf16[128,512]{1,0:T(8,128)(2,1)S(1)}, bf16[128,512]{1,0:T(8,128)(2,1)S(1)}, u32[]{:S(2)}, u32[]{:S(2)}) collective-permute-start(bf16[128,512]{1,0:T(8,128)(2,1)S(1)} %finish_1.1), channel_id=1, source_target_pairs={{0,8},{8,16},{16,24},{24,0},{1,9},{9,17},{17,25},{25,1},{2,10},{10... | collective-permute-start | bytes 393224 | tf_op jit(solution)/shard_map/ppermute | solution.py:54

commit v10 on v9

--- a/solution.py
+++ b/solution.py
@@ -529,8 +529,8 @@
     for step, _ in firsts:
         far[step] = swapped_parts(near[step], devices, PARTS)
     if firsts:
-        sums = slots_call([(0, step) for step, _ in firsts], sums, "slots_near")
-        sums = slots_call([(1, step) for step, _ in firsts], sums, "slots_far")
+        names = [(other, step) for other in range(CORES) for step, _ in firsts]
+        sums = slots_call(names, sums, "slots_both")
     for i, (step, way) in enumerate(order[len(firsts) :]):
         sums = arrive(step, sums)
         hop_on(step, way)

time: 40.1 us -> 39.9 us (level)
  Pallas kernels: 17.2 us -> 16.1 us
  waiting for transfers between devices: 6.74 us -> 7.69 us
    pallas_call x4 -> x3, Pallas kernels: 8.65 us -> 7.47 us  [slots_call(): pl.pallas_call(functools.partial(slots_kernel, tuple(names), sizes), out_...]
    ppermute x6, waiting for transfers between devices: 0.02 us -> 1.03 us  [swapped(): lax.ppermute(value, 'node', [(d, d ^ distance) for d in range(devices)])]
  transfers between devices with their start and end apart: 11 -> 11, of which waited for: 3 -> 6; matrix products, arithmetic and copies ran while one was open for 0% -> 0% of each run, Pallas kernels for 35% -> 33%
where the time goes in v10:
time: 39.9 us; the launch traced here: 39.4 us
  Pallas kernels  16.1 us (40%)
  starting transfers between devices  15.5 us (39%)
  waiting for transfers between devices  7.69 us (19%)
    ppermute x3, starting transfers between devices, to_next_chip(): return lax.ppermute(value, 'node', pairs)  10.5 us
    pallas_call x3, Pallas kernels, slots_call(): pl.pallas_call(functools.partial(slots_kernel, tuple(names), sizes), out_...  7.47 us
    ppermute x2, waiting for transfers between devices, to_next_segment(): lax.ppermute(value, 'segment', [(s, (s + 1) % count) for s in range(count)])  4.91 us
    pallas_call x1, Pallas kernels, body(): pl.pallas_call(prep_kernel, out_shape=(shape((blocks, pairs, wide, 2 * br...  3.97 us
    ppermute x2, starting transfers between devices, to_next_segment(): lax.ppermute(value, 'segment', [(s, (s + 1) % count) for s in range(count)])  3.08 us
    pallas_call x2, Pallas kernels, body(): pl.pallas_call(functools.partial(finish_kernel, names, b, lead), out_shap...  2.35 us
    ppermute x6, starting transfers between devices, swapped(): lax.ppermute(value, 'node', [(d, d ^ distance) for d in range(devices)])  1.94 us
    ppermute x3, waiting for transfers between devices, to_next_chip(): return lax.ppermute(value, 'node', pairs)  1.75 us
  transfers between devices with their start and end apart: 11, of which 6 were waited for; matrix products, arithmetic and copies ran while one was open for 0% of the time, Pallas kernels for 33%

profile of v10, /device:TPU:0, one launch (start us, length us, event | category | flops | bytes accessed | tf_op | source)
XLA Modules:
  0.0 39.4 jit_solution(14472886730109379923)
XLA Ops:
  0.0 1.0 %pack_rows.1.load_ref.refs_13_.refs_8_ = bf16[272,512]{1,0:T(8,128)(2,1)S(1)} custom-call(bf16[256,512]{1,0:T(8,128)(2,1)} %bitcast.7, s32[1,256]{1,0:T(1,128)} %bitcast.9), custom_call_target="tpu_custom_call" | custom-call | flops 65536 | bytes 1024 | tf_op jit(solution)/shard_map/pack_rows/pallas_call | solution.py:411
  1.0 0.5 %collective-permute-start = (bf16[272,512]{1,0:T(8,128)(2,1)S(1)}, bf16[272,512]{1,0:T(8,128)(2,1)S(1)}, u32[]{:S(2)}, u32[]{:S(2)}) collective-permute-start(bf16[272,512]{1,0:T(8,128)(2,1)S(1)} %pack_rows.1.load_ref.refs_13_.refs_8_), channel_id=1, source_target_pairs={{0,1},{1,0},{2,3},{3,2},{4,5},{5,4},{6,7},{7,6},{8,9},{9,8},{10,11... | collective-permute-start | bytes 835592 | tf_op jit(solution)/shard_map/ppermute | solution.py:43
  1.5 2.6 %collective-permute-start.2 = (bf16[272,512]{1,0:T(8,128)(2,1)S(1)}, bf16[272,512]{1,0:T(8,128)(2,1)S(1)}, u32[]{:S(2)}, u32[]{:S(2)}) collective-permute-start(bf16[272,512]{1,0:T(8,128)(2,1)S(1)} %pack_rows.1.load_ref.refs_13_.refs_8_), channel_id=1, source_target_pairs={{0,2},{1,3},{2,6},{3,7},{6,4},{7,5},{4,0},{5,1},{8,10},{9,11},{10,... | collective-permute-start | bytes 835592 | tf_op jit(solution)/shard_map/ppermute | solution.py:39
  4.1 4.0 %prepare.1 = (bf16[2,4,128,256]{3,2,1,0:T(8,128)(2,1)S(1)}, f32[2,512,128]{2,1,0:T(8,128)S(1)}, f32[2,8,128]{2,1,0:T(8,128)S(1)}, f32[2,4,2,128,128]{4,3,2,1,0:T...) custom-call(bf16[272,512]{1,0:T(8,128)(2,1)S(1)} %pack_rows.1.load_r, ...), custom_call_target="tpu_custom_call" | custom-call | flops 65536 | bytes 1024 | tf_op jit(solution)/shard_map/prepare/pallas_call | solution.py:434
  8.1 1.1 %collective-permute-start.1 = (bf16[272,512]{1,0:T(8,128)(2,1)S(1)}, bf16[272,512]{1,0:T(8,128)(2,1)S(1)}, u32[]{:S(2)}, u32[]{:S(2)}) collective-permute-start(bf16[272,512]{1,0:T(8,128)(2,1)S(1)} %pack_rows.1.load_ref.refs_13_.refs_8_), channel_id=1, source_target_pairs={{0,4},{1,5},{2,0},{3,1},{6,2},{7,3},{4,6},{5,7},{8,12},{9,13},{10,... | collective-permute-start | bytes 835592 | tf_op jit(solution)/shard_map/ppermute | solution.py:39
  9.2 1.6 %slots_own.1 = (f32[2,512,128]{2,1,0:T(8,128)S(1)}, f32[2,8,128]{2,1,0:T(8,128)S(1)}, f32[32,512]{1,0:T(8,128)S(1)}, f32[32,128]{1,0:T(8,128)S(1)}) custom-call(f32[2,4,8,128]{3,2,1,0:T(8,128)S(1)} %get-tuple-element.42.mask_ref.refs_0_, f32[1,512]{1,0:T(1,128)S(1)} %get-tuple-element.43.gain_ref.refs_1_, ...), custom_call_target="tpu_custom_call" | custom-call | flops 65536 | bytes 1024 | tf_op jit(solution)/shard_map/slots_own/pallas_call | solution.py:498
  10.9 1.6 %collective-permute-done.2.refs_0_ = bf16[272,512]{1,0:T(8,128)(2,1)S(1)} collective-permute-done((bf16[272,512]{1,0:T(8,128)(2,1)S(1)}, bf16[272,512]{1,0:T(8,128)(2,1)S(1)}, u32[]{:S(2)}, u32[]{:S(2)}) %collective-permute-start.2) | collective-permute-done | bytes 278560 | tf_op jit(solution)/shard_map/ppermute | solution.py:39
  12.5 6.7 %collective-permute-start.7 = (bf16[272,512]{1,0:T(8,128)(2,1)S(1)}, bf16[272,512]{1,0:T(8,128)(2,1)S(1)}, u32[]{:S(2)}, u32[]{:S(2)}) collective-permute-start(bf16[272,512]{1,0:T(8,128)(2,1)S(1)} %collective-permute-done.2.refs_0_), channel_id=1, source_target_pairs={{0,2},{1,3},{2,6},{3,7},{6,4},{7,5},{4,0},{5,1},{8,10},{9,11},{10,... | collective-permute-start | bytes 835592 | tf_op jit(solution)/shard_map/ppermute | solution.py:39
  19.3 0.5 %collective-permute-start.3 = (bf16[144,512]{1,0:T(8,128)(2,1)S(1)}, bf16[144,512]{1,0:T(8,128)(2,1)S(1)}, u32[]{:S(2)}, u32[]{:S(2)}) collective-permute-start(bf16[144,512]{1,0:T(8,128)(2,1)S(1)} %slice.12), channel_id=1, source_target_pairs={{0,1},{1,0},{2,3},{3,2},{4,5},{5,4},{6,7},{7,6},{8,9},{9,8},{10,11... | collective-permute-start | bytes 442376 | tf_op jit(solution)/shard_map/ppermute | solution.py:43
  19.9 0.1 collective-permute-start.6
  20.0 0.4 %collective-permute-start.4 = (bf16[128,512]{1,0:T(8,128)(2,1)S(1)}, bf16[128,512]{1,0:T(8,128)(2,1)S(1)}, u32[]{:S(2)}, u32[]{:S(2)}) collective-permute-start(bf16[128,512]{1,0:T(8,128)(2,1)S(1)} %slice.13), channel_id=1, source_target_pairs={{0,1},{1,0},{2,3},{3,2},{4,5},{5,4},{6,7},{7,6},{8,9},{9,8},{10,11... | collective-permute-start | bytes 393224 | tf_op jit(solution)/shard_map/ppermute | solution.py:43
  20.4 0.8 %collective-permute-done.6.refs_5_ = bf16[128,512]{1,0:T(8,128)(2,1)S(1)} collective-permute-done((bf16[128,512]{1,0:T(8,128)(2,1)S(1)}, bf16[128,512]{1,0:T(8,128)(2,1)S(1)}, u32[]{:S(2)}, u32[]{:S(2)}) %collective-permute-start.6) | collective-permute-done | bytes 131104 | tf_op jit(solution)/shard_map/ppermute | solution.py:43
  21.3 0.2 collective-permute-done.4.refs_3_
  21.5 4.2 %slots_both.1 = (f32[2,512,128]{2,1,0:T(8,128)S(1)}, f32[2,8,128]{2,1,0:T(8,128)S(1)}, f32[32,512]{1,0:T(8,128)S(1)}, f32[32,128]{1,0:T(8,128)S(1)}) custom-call(f32[2,4,8,128]{3,2,1,0:T(8,128)S(1)} %get-tuple-element.42.mask_ref.refs_0_, f32[1,512]{1,0:T(1,128)S(1)} %get-tuple-element.43.gain_ref.refs_1_, ...), custom_call_target="tpu_custom_call" | custom-call | flops 65536 | bytes 1024 | tf_op jit(solution)/shard_map/slots_both/pallas_call | solution.py:498
  25.8 0.3 collective-permute-start.8
  26.1 1.7 %slots_0.1 = (f32[2,512,128]{2,1,0:T(8,128)S(1)}, f32[2,8,128]{2,1,0:T(8,128)S(1)}, f32[32,512]{1,0:T(8,128)S(1)}, f32[32,128]{1,0:T(8,128)S(1)}) custom-call(f32[2,4,8,128]{3,2,1,0:T(8,128)S(1)} %get-tuple-element.42.mask_ref.refs_0_, f32[1,512]{1,0:T(1,128)S(1)} %get-tuple-element.43.gain_ref.refs_1_, ...), custom_call_target="tpu_custom_call" | custom-call | flops 65536 | bytes 1024 | tf_op jit(solution)/shard_map/slots_0/pallas_call | solution.py:498
  27.7 1.6 %finish_0.1 = (bf16[128,512]{1,0:T(8,128)(2,1)S(1)}, bf16[128,512]{1,0:T(8,128)(2,1)S(1)}, bf16[512,128]{1,0:T(8,128)(2,1)S(1)}, f32[4,512]{1,0:T(4,128)S(1)}) custom-call(f32[2,4,8,128]{3,2,1,0:T(8,128)S(1)} %get-tuple-element.42.mask_ref.refs_0_, f32[1,512]{1,0:T(1,128)S(1)} %get-tuple-element.43.gain_ref.refs_1_, ...), custom_call_target="tpu_custom_call" | custom-call | flops 65536 | bytes 1024 | tf_op jit(solution)/shard_map/finish_0/pallas_call | solution.py:551
  29.4 1.5 %collective-permute-start.10 = (bf16[128,512]{1,0:T(8,128)(2,1)S(1)}, bf16[128,512]{1,0:T(8,128)(2,1)S(1)}, u32[]{:S(2)}, u32[]{:S(2)}) collective-permute-start(bf16[128,512]{1,0:T(8,128)(2,1)S(1)} %get-tuple-element.78), channel_id=1, source_target_pairs={{0,8},{8,16},{16,24},{24,0},{1,9},{9,17},{17,25},{25,1},{2,10},{10... | collective-permute-start | bytes 393224 | tf_op jit(solution)/shard_map/ppermute | solution.py:54
  30.9 0.7 %finish_1.1 = bf16[128,512]{1,0:T(8,128)(2,1)S(1)} custom-call(bf16[128,512]{1,0:T(8,128)(2,1)S(1)} %get-tuple-element.75.refs_0_, bf16[512,128]{1,0:T(8,128)(2,1)S(1)} %get-tuple-element.76.refs_1_, f32[4,512]{1,0:T(4,128)S(1)} %get-tuple-element.77.refs_2_, f32[2,4,2,128,128]{4,3,2,1,0:T(8,128)S(1)} %get-tuple-element.47.counts_ref.refs_8_.refs_3_, ...), custom_call_target="tpu_custom_call" | custom-call | flops 65536 | bytes 1024 | tf_op jit(solution)/shard_map/finish_1/pallas_call | solution.py:551
  31.6 1.5 %collective-permute-start.9 = (bf16[128,512]{1,0:T(8,128)(2,1)S(1)}, bf16[128,512]{1,0:T(8,128)(2,1)S(1)}, u32[]{:S(2)}, u32[]{:S(2)}) collective-permute-start(bf16[128,512]{1,0:T(8,128)(2,1)S(1)} %finish_1.1), channel_id=1, source_target_pairs={{0,8},{8,16},{16,24},{24,0},{1,9},{9,17},{17,25},{25,1},{2,10},{10... | collective-permute-start | bytes 393224 | tf_op jit(solution)/shard_map/ppermute | solution.py:54
  33.2 3.5 %collective-permute-done.10.rows_ref = bf16[128,512]{1,0:T(8,128)(2,1)S(1)} collective-permute-done((bf16[128,512]{1,0:T(8,128)(2,1)S(1)}, bf16[128,512]{1,0:T(8,128)(2,1)S(1)}, u32[]{:S(2)}, u32[]{:S(2)}) %collective-permute-start.10) | collective-permute-done | bytes 131104 | tf_op jit(solution)/shard_map/ppermute | solution.py:54
  36.6 0.7 %place_0.1.refs_0_ = bf16[1,256,512]{2,1,0:T(8,128)(2,1)} custom-call(bf16[128,512]{1,0:T(8,128)(2,1)S(1)} %collective-permute-done.10.rows_ref), custom_call_target="tpu_custom_call" | custom-call | flops 65536 | bytes 1024 | tf_op jit(solution)/shard_map/place_0/pallas_call | solution.py:574
  37.3 1.4 %collective-permute-done.9.rows_ref = bf16[128,512]{1,0:T(8,128)(2,1)S(1)} collective-permute-done((bf16[128,512]{1,0:T(8,128)(2,1)S(1)}, bf16[128,512]{1,0:T(8,128)(2,1)S(1)}, u32[]{:S(2)}, u32[]{:S(2)}) %collective-permute-start.9) | collective-permute-done | bytes 131104 | tf_op jit(solution)/shard_map/ppermute | solution.py:54
  38.7 0.7 %place_1.1 = bf16[1,256,512]{2,1,0:T(8,128)(2,1)} custom-call(bf16[128,512]{1,0:T(8,128)(2,1)S(1)} %collective-permute-done.9.rows_ref, bf16[1,256,512]{2,1,0:T(8,128)(2,1)} %place_0.1.refs_0_), custom_call_target="tpu_custom_call", output_to_operand_aliasing={{}: (1, {})} | custom-call | flops 65536 | bytes 1024 | tf_op jit(solution)/shard_map/place_1/pallas_call | solution.py:574
  (11 shorter events, 0.2 us)
Async XLA Ops:
  1.0 8.2 %collective-permute-start = (bf16[272,512]{1,0:T(8,128)(2,1)S(1)}, bf16[272,512]{1,0:T(8,128)(2,1)S(1)}, u32[]{:S(2)}, u32[]{:S(2)}) collective-permute-start(bf16[272,512]{1,0:T(8,128)(2,1)S(1)} %pack_rows.1.load_ref.refs_13_.refs_8_), channel_id=1, source_target_pairs={{0,1},{1,0},{2,3},{3,2},{4,5},{5,4},{6,7},{7,6},{8,9},{9,8},{10,11... | collective-permute-start | bytes 835592 | tf_op jit(solution)/shard_map/ppermute | solution.py:43
  1.5 11.0 %collective-permute-start.2 = (bf16[272,512]{1,0:T(8,128)(2,1)S(1)}, bf16[272,512]{1,0:T(8,128)(2,1)S(1)}, u32[]{:S(2)}, u32[]{:S(2)}) collective-permute-start(bf16[272,512]{1,0:T(8,128)(2,1)S(1)} %pack_rows.1.load_ref.refs_13_.refs_8_), channel_id=1, source_target_pairs={{0,2},{1,3},{2,6},{3,7},{6,4},{7,5},{4,0},{5,1},{8,10},{9,11},{10,... | collective-permute-start | bytes 835592 | tf_op jit(solution)/shard_map/ppermute | solution.py:39
  8.1 11.1 %collective-permute-start.1 = (bf16[272,512]{1,0:T(8,128)(2,1)S(1)}, bf16[272,512]{1,0:T(8,128)(2,1)S(1)}, u32[]{:S(2)}, u32[]{:S(2)}) collective-permute-start(bf16[272,512]{1,0:T(8,128)(2,1)S(1)} %pack_rows.1.load_ref.refs_13_.refs_8_), channel_id=1, source_target_pairs={{0,4},{1,5},{2,0},{3,1},{6,2},{7,3},{4,6},{5,7},{8,12},{9,13},{10,... | collective-permute-start | bytes 835592 | tf_op jit(solution)/shard_map/ppermute | solution.py:39
  12.5 13.3 %collective-permute-start.7 = (bf16[272,512]{1,0:T(8,128)(2,1)S(1)}, bf16[272,512]{1,0:T(8,128)(2,1)S(1)}, u32[]{:S(2)}, u32[]{:S(2)}) collective-permute-start(bf16[272,512]{1,0:T(8,128)(2,1)S(1)} %collective-permute-done.2.refs_0_), channel_id=1, source_target_pairs={{0,2},{1,3},{2,6},{3,7},{6,4},{7,5},{4,0},{5,1},{8,10},{9,11},{10,... | collective-permute-start | bytes 835592 | tf_op jit(solution)/shard_map/ppermute | solution.py:39
  19.3 2.2 %collective-permute-start.5 = (bf16[144,512]{1,0:T(8,128)(2,1)S(1)}, bf16[144,512]{1,0:T(8,128)(2,1)S(1)}, u32[]{:S(2)}, u32[]{:S(2)}) collective-permute-start(bf16[144,512]{1,0:T(8,128)(2,1)S(1)} %slice.14), channel_id=1, source_target_pairs={{0,1},{1,0},{2,3},{3,2},{4,5},{5,4},{6,7},{7,6},{8,9},{9,8},{10,11... | collective-permute-start | bytes 442376 | tf_op jit(solution)/shard_map/ppermute | solution.py:43
  19.3 2.1 %collective-permute-start.3 = (bf16[144,512]{1,0:T(8,128)(2,1)S(1)}, bf16[144,512]{1,0:T(8,128)(2,1)S(1)}, u32[]{:S(2)}, u32[]{:S(2)}) collective-permute-start(bf16[144,512]{1,0:T(8,128)(2,1)S(1)} %slice.12), channel_id=1, source_target_pairs={{0,1},{1,0},{2,3},{3,2},{4,5},{5,4},{6,7},{7,6},{8,9},{9,8},{10,11... | collective-permute-start | bytes 442376 | tf_op jit(solution)/shard_map/ppermute | solution.py:43
  19.9 1.4 %collective-permute-start.6 = (bf16[128,512]{1,0:T(8,128)(2,1)S(1)}, bf16[128,512]{1,0:T(8,128)(2,1)S(1)}, u32[]{:S(2)}, u32[]{:S(2)}) collective-permute-start(bf16[128,512]{1,0:T(8,128)(2,1)S(1)} %slice.15), channel_id=1, source_target_pairs={{0,1},{1,0},{2,3},{3,2},{4,5},{5,4},{6,7},{7,6},{8,9},{9,8},{10,11... | collective-permute-start | bytes 393224 | tf_op jit(solution)/shard_map/ppermute | solution.py:43
  20.0 1.5 %collective-permute-start.4 = (bf16[128,512]{1,0:T(8,128)(2,1)S(1)}, bf16[128,512]{1,0:T(8,128)(2,1)S(1)}, u32[]{:S(2)}, u32[]{:S(2)}) collective-permute-start(bf16[128,512]{1,0:T(8,128)(2,1)S(1)} %slice.13), channel_id=1, source_target_pairs={{0,1},{1,0},{2,3},{3,2},{4,5},{5,4},{6,7},{7,6},{8,9},{9,8},{10,11... | collective-permute-start | bytes 393224 | tf_op jit(solution)/shard_map/ppermute | solution.py:43
  25.8 1.9 %collective-permute-start.8 = (bf16[272,512]{1,0:T(8,128)(2,1)S(1)}, bf16[272,512]{1,0:T(8,128)(2,1)S(1)}, u32[]{:S(2)}, u32[]{:S(2)}) collective-permute-start(bf16[272,512]{1,0:T(8,128)(2,1)S(1)} %collective-permute-done.7.refs_0_), channel_id=1, source_target_pairs={{0,1},{1,0},{2,3},{3,2},{4,5},{5,4},{6,7},{7,6},{8,9},{9,8},{10,11... | collective-permute-start | bytes 835592 | tf_op jit(solution)/shard_map/ppermute | solution.py:43
  29.4 7.3 %collective-permute-start.10 = (bf16[128,512]{1,0:T(8,128)(2,1)S(1)}, bf16[128,512]{1,0:T(8,128)(2,1)S(1)}, u32[]{:S(2)}, u32[]{:S(2)}) collective-permute-start(bf16[128,512]{1,0:T(8,128)(2,1)S(1)} %get-tuple-element.78), channel_id=1, source_target_pairs={{0,8},{8,16},{16,24},{24,0},{1,9},{9,17},{17,25},{25,1},{2,10},{10... | collective-permute-start | bytes 393224 | tf_op jit(solution)/shard_map/ppermute | solution.py:54
  31.6 7.1 %collective-permute-start.9 = (bf16[128,512]{1,0:T(8,128)(2,1)S(1)}, bf16[128,512]{1,0:T(8,128)(2,1)S(1)}, u32[]{:S(2)}, u32[]{:S(2)}) collective-permute-start(bf16[128,512]{1,0:T(8,128)(2,1)S(1)} %finish_1.1), channel_id=1, source_target_pairs={{0,8},{8,16},{16,24},{24,0},{1,9},{9,17},{17,25},{25,1},{2,10},{10... | collective-permute-start | bytes 393224 | tf_op jit(solution)/shard_map/ppermute | solution.py:54
